TPU v7x, 32 devices: a whole 2x2x4 slice. The times are simulated.
32 devices in a mesh: dp: 4 (over y, x), fsdp: 8 (over z, core).
Axes of the slice: x: 2, y: 2, z: 4, core: 2. Of those that a mesh axis runs over, the one named last changes fastest.
Arguments:
- tokens: bfloat16 [8, 2048, 768], P('dp', 'fsdp'), may hold values from -6 to 6
- doc_ids: int32 [8, 16], P('dp'), may hold values from 0 to 2, never falling along the last dimension, each value on 1 to 12 neighbouring positions
- pos_embed: bfloat16 [16, 768], P(None, ('dp', 'fsdp')), may hold values from -3 to 3
- w_qkv: bfloat16 [2, 768, 2304], P(None, ('dp', 'fsdp')), may hold values from -0.21875 to 0.21875
- w_out: bfloat16 [2, 768, 768], P(None, ('dp', 'fsdp')), may hold values from -1.25 to 1.25
- w_in: bfloat16 [2, 768, 3072], P(None, ('dp', 'fsdp')), may hold values from -0.21875 to 0.21875
- w_back: bfloat16 [2, 3072, 768], P(None, None, ('dp', 'fsdp')), may hold values from -0.109375 to 0.109375
- norm_gain: bfloat16 [2, 2, 768], P(None, None, ('dp', 'fsdp')), may hold values from 0.099609375 to 1.8984375
- norm_bias: bfloat16 [2, 2, 768], P(None, None, ('dp', 'fsdp')), may hold values from -1.796875 to 1.796875
- cotangent: bfloat16 [8, 2048, 768], P('dp', 'fsdp'), may hold values from -40 to 40
Outputs:
- output: bfloat16 [8, 2048, 768], P('dp', 'fsdp')
- grad_tokens: bfloat16 [8, 2048, 768], P('dp', 'fsdp')
- grad_pos: float32 [16, 768], P(None, ('dp', 'fsdp'))
- grad_qkv: float32 [2, 768, 2304], P(None, ('dp', 'fsdp'))
- grad_out: float32 [2, 768, 768], P(None, ('dp', 'fsdp'))
- grad_in: float32 [2, 768, 3072], P(None, ('dp', 'fsdp'))
- grad_back: float32 [2, 3072, 768], P(None, None, ('dp', 'fsdp'))
- grad_gain: float32 [2, 2, 768], P(None, None, ('dp', 'fsdp'))
- grad_bias: float32 [2, 2, 768], P(None, None, ('dp', 'fsdp'))
Inputs may be any that keep to these rules, and one draw needn't show every extreme that they name: `doc_ids`: within a row, document numbers never fall from one segment to the next.
All inputs are finite; a program needn't handle non-finite values.
Results may differ from a plain program's by a relative error of at most 0.024.
Values may be sent and summed in bfloat16 or wider, within the bound.
A program may use at most 256 MiB of HBM per device.

v0:
```python
from functools import partial

import jax
import jax.numpy as jnp
from jax import lax
from jax.sharding import PartitionSpec as P

HEADS = 12
SEG_LEN = 128


epsilon = 1e-05
root_half = 0.7071067811865476
inv_root_tau = 0.3989422804014327


def matmul(left, right, form):
    return jnp.einsum(form, left, right, preferred_element_type=jnp.float32)


def norm_forward(summed, gains, biases):
    average = jnp.mean(summed, axis=-1, keepdims=True)
    centred = summed - average
    variance = jnp.mean(centred * centred, axis=-1, keepdims=True)
    inverse = lax.rsqrt(variance + epsilon)
    scaled = centred * inverse
    return (scaled * gains + biases, scaled, inverse)


def norm_backward(grad_result, scaled, inverse, gains):
    grad_scaled = grad_result * gains
    first_mean = jnp.mean(grad_scaled, axis=-1, keepdims=True)
    second_mean = jnp.mean(grad_scaled * scaled, axis=-1, keepdims=True)
    grad_sum = inverse * (grad_scaled - first_mean - scaled * second_mean)
    return (grad_sum, jnp.sum(grad_result * scaled, axis=(0, 1)), jnp.sum(grad_result, axis=(0, 1)))


def split_heads(packed):
    groups, length, model_width = packed.shape
    return packed.reshape(groups, length, HEADS, model_width // HEADS)


def join_heads(split_part):
    groups, length, heads_count, head_size = split_part.shape
    return split_part.reshape(groups, length, heads_count * head_size)


def attend_forward(query_part, key_part, value_part, allowed):
    head_size = query_part.shape[-1]
    scores = matmul(query_part, key_part, "glhe,gmhe->ghlm") * head_size ** (-0.5)
    scores = jnp.where(allowed[:, None], scores, -1e30)
    row_max = jnp.max(scores, axis=-1, keepdims=True)
    exp_terms = jnp.exp(scores - row_max)
    row_total = jnp.sum(exp_terms, axis=-1, keepdims=True)
    attention = exp_terms / row_total
    context = matmul(attention.astype(jnp.bfloat16), value_part, "ghlm,gmhe->glhe")
    return (join_heads(context).astype(jnp.bfloat16), row_max + jnp.log(row_total))


def attend_backward(query_part, key_part, value_part, allowed, log_total, grad_context):
    head_size = query_part.shape[-1]
    factor = head_size ** (-0.5)
    scores = matmul(query_part, key_part, "glhe,gmhe->ghlm") * factor
    scores = jnp.where(allowed[:, None], scores, -1e30)
    attention = jnp.exp(scores - log_total)
    grad_attention = matmul(grad_context, value_part, "glhe,gmhe->ghlm")
    grad_value = matmul(attention.astype(jnp.bfloat16), grad_context, "ghlm,glhe->gmhe")
    inner = jnp.sum(attention * grad_attention, axis=-1, keepdims=True)
    grad_scores = (attention * (grad_attention - inner)).astype(jnp.bfloat16)
    grad_query = matmul(grad_scores, key_part, "ghlm,gmhe->glhe") * factor
    grad_key = matmul(grad_scores, query_part, "ghlm,glhe->gmhe") * factor
    return (join_heads(grad_query), join_heads(grad_key), join_heads(grad_value))


def segment_attend(packed):
    groups, length, total_width = packed.shape
    model_width = total_width // 3
    allowed = jnp.ones((groups, length, length), dtype=jnp.bool_)
    context, log_total = attend_forward(
        split_heads(packed[..., :model_width]),
        split_heads(packed[..., model_width : 2 * model_width]),
        split_heads(packed[..., 2 * model_width :]),
        allowed,
    )
    return (context, log_total)


def segment_attend_back(packed, log_total, grad_context):
    groups, length, total_width = packed.shape
    model_width = total_width // 3
    allowed = jnp.ones((groups, length, length), dtype=jnp.bool_)
    grad_query, grad_key, grad_value = attend_backward(
        split_heads(packed[..., :model_width]),
        split_heads(packed[..., model_width : 2 * model_width]),
        split_heads(packed[..., 2 * model_width :]),
        allowed,
        log_total,
        split_heads(grad_context),
    )
    return jnp.concatenate([grad_query, grad_key, grad_value], axis=-1)


def cross_attend(packed, allowed):
    model_width = packed.shape[-1] // 3
    remote = lax.all_gather(packed[..., model_width:], "fsdp", axis=1, tiled=True)
    context, log_total = attend_forward(
        split_heads(packed[..., :model_width]),
        split_heads(remote[..., :model_width]),
        split_heads(remote[..., model_width:]),
        allowed,
    )
    return (context, (remote, log_total))


def cross_attend_back(packed, saved, grad_context, allowed):
    remote, log_total = saved
    model_width = packed.shape[-1] // 3
    grad_query, grad_key, grad_value = attend_backward(
        split_heads(packed[..., :model_width]),
        split_heads(remote[..., :model_width]),
        split_heads(remote[..., model_width:]),
        allowed,
        log_total,
        split_heads(grad_context),
    )
    shared = jnp.concatenate([grad_key, grad_value], axis=-1)
    own_part = lax.psum_scatter(
        shared.astype(jnp.bfloat16), "fsdp", scatter_dimension=1, tiled=True
    ).astype(jnp.float32)
    return jnp.concatenate([grad_query, own_part], axis=-1)


def block_forward(states, weights, attend):
    w_qkv, w_out, w_in, w_back, gains, biases = weights
    gains = gains.astype(jnp.float32)
    biases = biases.astype(jnp.float32)
    states_low = states.astype(jnp.bfloat16)
    packed = matmul(states_low, w_qkv, "gld,de->gle").astype(jnp.bfloat16)
    context, saved = attend(packed)
    branch = matmul(context, w_out, "gld,de->gle")
    normed, scaled_one, inverse_one = norm_forward(states + branch, gains[0], biases[0])
    normed_low = normed.astype(jnp.bfloat16)
    hidden = matmul(normed_low, w_in, "gld,df->glf")
    active_low = jax.nn.gelu(hidden, approximate=False).astype(jnp.bfloat16)
    feed_out = matmul(active_low, w_back, "glf,fd->gld")
    result, scaled_two, inverse_two = norm_forward(normed + feed_out, gains[1], biases[1])
    kept = (
        states_low,
        packed,
        context,
        saved,
        scaled_one,
        inverse_one,
        normed_low,
        hidden,
        active_low,
        scaled_two,
        inverse_two,
    )
    return (result, kept)


def block_backward(grad_result, kept, weights, attend_back):
    w_qkv, w_out, w_in, w_back, gains, biases = weights
    gains = gains.astype(jnp.float32)
    (
        states_low,
        packed,
        context,
        saved,
        scaled_one,
        inverse_one,
        normed_low,
        hidden,
        active_low,
        scaled_two,
        inverse_two,
    ) = kept
    grad_sum_two, gain_two, bias_two = norm_backward(grad_result, scaled_two, inverse_two, gains[1])
    grad_feed = grad_sum_two.astype(jnp.bfloat16)
    grad_active = matmul(grad_feed, w_back, "gld,fd->glf")
    cumulative = 0.5 * (1.0 + lax.erf(hidden * root_half))
    slope = cumulative + hidden * inv_root_tau * jnp.exp(-0.5 * hidden * hidden)
    grad_hidden = (grad_active * slope).astype(jnp.bfloat16)
    grad_normed = grad_sum_two + matmul(grad_hidden, w_in, "glf,df->gld")
    grad_sum_one, gain_one, bias_one = norm_backward(grad_normed, scaled_one, inverse_one, gains[0])
    grad_branch = grad_sum_one.astype(jnp.bfloat16)
    grad_context = matmul(grad_branch, w_out, "gle,de->gld").astype(jnp.bfloat16)
    grad_packed = attend_back(packed, saved, grad_context).astype(jnp.bfloat16)
    grad_states = grad_sum_one + matmul(grad_packed, w_qkv, "gle,de->gld")
    factors = (
        states_low,
        grad_packed,
        context,
        grad_branch,
        normed_low,
        grad_hidden,
        grad_feed,
        active_low,
    )
    smalls = (jnp.stack([gain_one, gain_two]), jnp.stack([bias_one, bias_two]))
    return (grad_states, factors, smalls)


def weight_terms(factors):
    (
        states_low,
        grad_packed,
        context,
        grad_branch,
        normed_low,
        grad_hidden,
        grad_feed,
        active_low,
    ) = factors
    term_qkv = matmul(states_low, grad_packed, "gld,gle->de")
    term_out = matmul(context, grad_branch, "gld,gle->de")
    term_in = matmul(normed_low, grad_hidden, "gld,glf->df")
    term_back = matmul(grad_feed, active_low, "gld,glf->df")
    return jnp.concatenate([term_qkv, term_out, term_in, term_back], axis=1)


def gather_segment(w_qkv, w_out, w_in, w_back, norm_gain, norm_bias):
    return (
        lax.all_gather(w_qkv[0], ("dp", "fsdp"), axis=0, tiled=True),
        lax.all_gather(w_out[0], ("dp", "fsdp"), axis=0, tiled=True),
        lax.all_gather(w_in[0], ("dp", "fsdp"), axis=0, tiled=True),
        lax.all_gather(w_back[0], ("dp", "fsdp"), axis=1, tiled=True),
        lax.all_gather(norm_gain[0], ("dp", "fsdp"), axis=1, tiled=True),
        lax.all_gather(norm_bias[0], ("dp", "fsdp"), axis=1, tiled=True),
    )


def gather_cross(pos_embed, w_qkv, w_out, w_in, w_back, norm_gain, norm_bias):
    gathered = (
        lax.all_gather(w_qkv[1], ("dp", "fsdp"), axis=0, tiled=True),
        lax.all_gather(w_out[1], ("dp", "fsdp"), axis=0, tiled=True),
        lax.all_gather(w_in[1], ("dp", "fsdp"), axis=0, tiled=True),
        lax.all_gather(w_back[1], ("dp", "fsdp"), axis=1, tiled=True),
        lax.all_gather(norm_gain[1], ("dp", "fsdp"), axis=1, tiled=True),
        lax.all_gather(norm_bias[1], ("dp", "fsdp"), axis=1, tiled=True),
        lax.all_gather(pos_embed, ("dp", "fsdp"), axis=1, tiled=True),
    )
    return (gathered[:6], gathered[6])


def layer_forward(tokens, doc_ids, seg_weights, cross_weights, pos_full):
    rows, local_len, model_width = tokens.shape
    seg_count = local_len // SEG_LEN
    segments = tokens.reshape(rows * seg_count, SEG_LEN, model_width).astype(jnp.float32)
    seg_out, seg_kept = block_forward(segments, seg_weights, segment_attend)
    start = lax.axis_index("fsdp") * seg_count
    pos_local = lax.dynamic_slice_in_dim(pos_full, start, seg_count, 0).astype(jnp.float32)
    leaders = seg_out[:, 0, :].reshape(rows, seg_count, model_width) + pos_local
    own_docs = lax.dynamic_slice_in_dim(doc_ids, start, seg_count, 1)
    allowed = own_docs[:, :, None] == doc_ids[:, None, :]
    cross_out, cross_kept = block_forward(
        leaders, cross_weights, partial(cross_attend, allowed=allowed)
    )
    joined = jnp.concatenate(
        [cross_out.reshape(rows * seg_count, 1, model_width), seg_out[:, 1:, :]], axis=1
    )
    output = joined.reshape(rows, local_len, model_width).astype(jnp.bfloat16)
    return (output, (seg_kept, cross_kept, allowed))


def layer_backward(cotangent, doc_ids, kept, seg_weights, cross_weights):
    seg_kept, cross_kept, allowed = kept
    rows, local_len, model_width = cotangent.shape
    seg_count = local_len // SEG_LEN
    grad_all = cotangent.reshape(rows * seg_count, SEG_LEN, model_width).astype(jnp.float32)
    grad_cross = grad_all[:, 0, :].reshape(rows, seg_count, model_width)
    grad_leaders, cross_factors, cross_smalls = block_backward(
        grad_cross, cross_kept, cross_weights, partial(cross_attend_back, allowed=allowed)
    )
    start = lax.axis_index("fsdp") * seg_count
    empty_pos = jnp.zeros((doc_ids.shape[1], model_width), jnp.float32)
    grad_pos = lax.dynamic_update_slice_in_dim(empty_pos, jnp.sum(grad_leaders, axis=0), start, 0)
    grad_seg = jnp.concatenate(
        [grad_leaders.reshape(rows * seg_count, 1, model_width), grad_all[:, 1:, :]], axis=1
    )
    grad_states, seg_factors, seg_smalls = block_backward(
        grad_seg, seg_kept, seg_weights, segment_attend_back
    )
    grad_tokens = grad_states.reshape(rows, local_len, model_width).astype(jnp.bfloat16)
    return (grad_tokens, seg_factors, cross_factors, seg_smalls, cross_smalls, grad_pos)


def body(tokens, doc_ids, pos_embed, w_qkv, w_out, w_in, w_back, norm_gain, norm_bias, cotangent):
    seg_weights = gather_segment(w_qkv, w_out, w_in, w_back, norm_gain, norm_bias)
    cross_weights, pos_full = gather_cross(
        pos_embed, w_qkv, w_out, w_in, w_back, norm_gain, norm_bias
    )
    output, kept = layer_forward(tokens, doc_ids, seg_weights, cross_weights, pos_full)
    shards = lax.optimization_barrier(
        (output, tokens, pos_embed, w_qkv, w_out, w_in, w_back, norm_gain, norm_bias)
    )
    seg_weights = gather_segment(shards[3], shards[4], shards[5], shards[6], shards[7], shards[8])
    cross_weights, pos_full = gather_cross(
        shards[2], shards[3], shards[4], shards[5], shards[6], shards[7], shards[8]
    )
    recomputed, kept = layer_forward(shards[1], doc_ids, seg_weights, cross_weights, pos_full)
    grad_tokens, seg_factors, cross_factors, seg_smalls, cross_smalls, grad_pos = layer_backward(
        cotangent, doc_ids, kept, seg_weights, cross_weights
    )
    model_width = tokens.shape[2]
    hidden_width = w_in.shape[2]
    seg_term = lax.psum_scatter(
        weight_terms(seg_factors), ("dp", "fsdp"), scatter_dimension=0, tiled=True
    )
    cross_term = lax.psum_scatter(
        weight_terms(cross_factors), ("dp", "fsdp"), scatter_dimension=0, tiled=True
    )
    stacked = jnp.stack([seg_term, cross_term])
    grad_qkv = stacked[:, :, : 3 * model_width]
    grad_out = stacked[:, :, 3 * model_width : 4 * model_width]
    grad_in = stacked[:, :, 4 * model_width : 4 * model_width + hidden_width]
    grad_back = jnp.transpose(stacked[:, :, 4 * model_width + hidden_width :], (0, 2, 1))
    gain_all = jnp.stack([seg_smalls[0], cross_smalls[0]])
    bias_all = jnp.stack([seg_smalls[1], cross_smalls[1]])
    grad_gain, grad_bias, pos_shard = (
        lax.psum_scatter(gain_all, ("dp", "fsdp"), scatter_dimension=2, tiled=True),
        lax.psum_scatter(bias_all, ("dp", "fsdp"), scatter_dimension=2, tiled=True),
        lax.psum_scatter(grad_pos, ("dp", "fsdp"), scatter_dimension=1, tiled=True),
    )
    return (
        output,
        grad_tokens,
        pos_shard,
        grad_qkv,
        grad_out,
        grad_in,
        grad_back,
        grad_gain,
        grad_bias,
    )


def solution(mesh):
    return jax.shard_map(
        body,
        mesh=mesh,
        in_specs=(
            P("dp", "fsdp", None),
            P("dp", None),
            P(None, ("dp", "fsdp")),
            P(None, ("dp", "fsdp"), None),
            P(None, ("dp", "fsdp"), None),
            P(None, ("dp", "fsdp"), None),
            P(None, None, ("dp", "fsdp")),
            P(None, None, ("dp", "fsdp")),
            P(None, None, ("dp", "fsdp")),
            P("dp", "fsdp", None),
        ),
        out_specs=(
            P("dp", "fsdp", None),
            P("dp", "fsdp", None),
            P(None, ("dp", "fsdp")),
            P(None, ("dp", "fsdp"), None),
            P(None, ("dp", "fsdp"), None),
            P(None, ("dp", "fsdp"), None),
            P(None, None, ("dp", "fsdp")),
            P(None, None, ("dp", "fsdp")),
            P(None, None, ("dp", "fsdp")),
        ),
        check_vma=False,
    )
```

profile of v0, /device:TPU:1, one launch (start us, length us, event | category | flops | bytes accessed | tf_op | source)
XLA Modules:
  0.0 1816.4 jit_solution(10321339943711136478)
XLA Ops:
  17.5 46.0 %all-gather.3 = bf16[1,2,768]{1,0,2:T(2,128)(2,1)S(1)} all-gather(bf16[1,2,24]{1,0,2:T(2,128)(2,1)S(1)} %copy.267), channel_id=5, replica_groups=mesh['dp'=4,'fsdp'=8] {'dp','fsdp'}, dimensions={2}, use_global_device_ids=true | all-gather | bytes 3168 | tf_op jit(solution)/shard_map/all_gather | solution.py:230
  68.6 38.5 %all-gather.2 = bf16[1,2,768]{1,0,2:T(2,128)(2,1)S(1)} all-gather(bf16[1,2,24]{1,0,2:T(2,128)(2,1)S(1)} %copy.266), channel_id=4, replica_groups=mesh['dp'=4,'fsdp'=8] {'dp','fsdp'}, dimensions={2}, use_global_device_ids=true | all-gather | bytes 3168 | tf_op jit(solution)/shard_map/all_gather | solution.py:229
  112.2 40.4 %all-gather.9 = bf16[1,2,768]{1,0,2:T(2,128)(2,1)S(1)} all-gather(bf16[1,2,24]{1,0,2:T(2,128)(2,1)S(1)} %copy.269), channel_id=11, replica_groups=mesh['dp'=4,'fsdp'=8] {'dp','fsdp'}, dimensions={2}, use_global_device_ids=true | all-gather | bytes 3168 | tf_op jit(solution)/shard_map/all_gather | solution.py:241
  157.7 39.5 %all-gather.8 = bf16[1,2,768]{1,0,2:T(2,128)(2,1)S(1)} all-gather(bf16[1,2,24]{1,0,2:T(2,128)(2,1)S(1)} %copy.268), channel_id=10, replica_groups=mesh['dp'=4,'fsdp'=8] {'dp','fsdp'}, dimensions={2}, use_global_device_ids=true | all-gather | bytes 3168 | tf_op jit(solution)/shard_map/all_gather | solution.py:240
  202.1 38.8 %all-gather.24 = bf16[32,24,16]{1,2,0:T(8,128)(2,1)S(1)} all-gather(bf16[1,24,16]{1,2,0:T(8,128)(2,1)S(1)} %bitcast.310), channel_id=1, replica_groups=mesh['dp'=4,'fsdp'=8] {'dp','fsdp'}, dimensions={0}, use_global_device_ids=true | all-gather | bytes 25344 | tf_op jit(solution)/shard_map/all_gather | solution.py:242
  257.4 9.3 fusion.114
  266.7 19.3 %fusion.370 = (f32[4,128]{1,0:T(4,128)S(1)}, f32[4,128,768]{2,1,0:T(8,128)S(1)}) fusion(bf16[1,3072,768]{1,2,0:T(8,128)(2,1)} %all-gather.49.cloned.1.call-done, f32[4,128,3072]{2,1,0:T(8,128)} %get-tuple-element.108, u8[128,3072]{1,0:T(8,128)(4,1)S(1)} %get-tuple-element.28, u8[128,3072]{1,0:T(8,128)(4,1)S(1)} %get-tuple-element.27, ...), kind=kOutput, calls=%fused_computation.523 | convolution fusion | flops 2528378368 | bytes 14954496 | tf_op jit(solution)/shard_map/glf,fd->gld/dot_general | solution.py:18
  286.8 39.2 %all-gather.51.cloned.1.call-done = bf16[1,768,2304]{2,1,0:T(8,128)(2,1)} async-done(((bf16[1,24,2304]{2,1,0:T(8,128)(2,1)}), bf16[1,768,2304]{2,1,0:T(8,128)(2,1)}) %all-gather.51.cloned.1.call-update) | async-done | bytes 3538960 | tf_op jit(solution)/shard_map/all_gather | solution.py:236
  328.7 14.0 all_gather.92
  344.0 37.9 %all-gather.53.cloned.1.call-done = bf16[1,768,768]{2,1,0:T(8,128)(2,1)} async-done(((bf16[1,24,768]{2,1,0:T(8,128)(2,1)}), bf16[1,768,768]{2,1,0:T(8,128)(2,1)}) %all-gather.53.cloned.1.call-update) | async-done | bytes 1179664 | tf_op jit(solution)/shard_map/all_gather | solution.py:237
  383.8 64.4 %all-gather.55.cloned.1.call-done = bf16[1,768,3072]{2,1,0:T(8,128)(2,1)} async-done(((bf16[1,24,3072]{2,1,0:T(8,128)(2,1)}), bf16[1,768,3072]{2,1,0:T(8,128)(2,1)}) %all-gather.55.cloned.1.call-update) | async-done | bytes 4718608 | tf_op jit(solution)/shard_map/all_gather | solution.py:238
  451.3 62.9 %all-gather.57.cloned.1.call-done = bf16[1,3072,768]{1,2,0:T(8,128)(2,1)} async-done(((bf16[1,3072,24]{1,2,0:T(8,128)(2,1)}), bf16[1,3072,768]{1,2,0:T(8,128)(2,1)}) %all-gather.57.cloned.1.call-update) | async-done | bytes 4718608 | tf_op jit(solution)/shard_map/all_gather | solution.py:239
  528.4 42.1 %all-gather.14 = bf16[1,2,768]{1,0,2:T(2,128)(2,1)S(1)} all-gather(bf16[1,2,24]{1,0,2:T(2,128)(2,1)S(1)} %get-tuple-element.99), channel_id=16, replica_groups=mesh['dp'=4,'fsdp'=8] {'dp','fsdp'}, dimensions={2}, use_global_device_ids=true | all-gather | bytes 3168 | tf_op jit(solution)/shard_map/all_gather | solution.py:229
  571.0 38.7 %all-gather.15 = bf16[1,2,768]{1,0,2:T(2,128)(2,1)S(1)} all-gather(bf16[1,2,24]{1,0,2:T(2,128)(2,1)S(1)} %get-tuple-element.97), channel_id=17, replica_groups=mesh['dp'=4,'fsdp'=8] {'dp','fsdp'}, dimensions={2}, use_global_device_ids=true | all-gather | bytes 3168 | tf_op jit(solution)/shard_map/all_gather | solution.py:230
  610.1 38.4 %all-gather.25 = bf16[32,24,16]{1,2,0:T(8,128)(2,1)S(1)} all-gather(bf16[1,24,16]{1,2,0:T(8,128)(2,1)S(1)} %bitcast.311), channel_id=1, replica_groups=mesh['dp'=4,'fsdp'=8] {'dp','fsdp'}, dimensions={0}, use_global_device_ids=true | all-gather | bytes 25344 | tf_op jit(solution)/shard_map/all_gather | solution.py:242
  648.7 39.2 %all-gather.20 = bf16[1,2,768]{1,0,2:T(2,128)(2,1)S(1)} all-gather(bf16[1,2,24]{1,0,2:T(2,128)(2,1)S(1)} %get-tuple-element.98), channel_id=22, replica_groups=mesh['dp'=4,'fsdp'=8] {'dp','fsdp'}, dimensions={2}, use_global_device_ids=true | all-gather | bytes 3168 | tf_op jit(solution)/shard_map/all_gather | solution.py:240
  693.8 40.1 %all-gather.21 = bf16[1,2,768]{1,0,2:T(2,128)(2,1)S(1)} all-gather(bf16[1,2,24]{1,0,2:T(2,128)(2,1)S(1)} %get-tuple-element.96), channel_id=23, replica_groups=mesh['dp'=4,'fsdp'=8] {'dp','fsdp'}, dimensions={2}, use_global_device_ids=true | all-gather | bytes 3168 | tf_op jit(solution)/shard_map/all_gather | solution.py:241
  761.4 7.3 fusion.115
  771.4 15.2 fusion.7
  786.6 6.5 fusion.375
  795.0 36.5 %all-gather.67.cloned.1.call-done = bf16[1,768,2304]{2,1,0:T(8,128)(2,1)} async-done(((bf16[1,24,2304]{2,1,0:T(8,128)(2,1)}), bf16[1,768,2304]{2,1,0:T(8,128)(2,1)}) %all-gather.67.cloned.1.call-update) | async-done | bytes 3538960 | tf_op jit(solution)/shard_map/all_gather | solution.py:236
  834.1 14.0 all_gather.106
  850.9 36.4 %all-gather.69.cloned.1.call-done = bf16[1,768,768]{2,1,0:T(8,128)(2,1)} async-done(((bf16[1,24,768]{2,1,0:T(8,128)(2,1)}), bf16[1,768,768]{2,1,0:T(8,128)(2,1)}) %all-gather.69.cloned.1.call-update) | async-done | bytes 1179664 | tf_op jit(solution)/shard_map/all_gather | solution.py:237
  889.8 63.6 %all-gather.71.cloned.1.call-done = bf16[1,768,3072]{2,1,0:T(8,128)(2,1)} async-done(((bf16[1,24,3072]{2,1,0:T(8,128)(2,1)}), bf16[1,768,3072]{2,1,0:T(8,128)(2,1)}) %all-gather.71.cloned.1.call-update) | async-done | bytes 4718608 | tf_op jit(solution)/shard_map/all_gather | solution.py:238
  956.6 62.7 %all-gather.73.cloned.1.call-done = bf16[1,3072,768]{1,2,0:T(8,128)(2,1)} async-done(((bf16[1,3072,24]{1,2,0:T(8,128)(2,1)}), bf16[1,3072,768]{1,2,0:T(8,128)(2,1)}) %all-gather.73.cloned.1.call-update) | async-done | bytes 4718608 | tf_op jit(solution)/shard_map/all_gather | solution.py:239
  1039.9 45.7 %all-reduce.8.cloned.1.call-done = bf16[2,16,1536]{2,1,0:T(8,128)(2,1)} async-done(((bf16[2,16,1536]{2,1,0:T(8,128)(2,1)}), bf16[2,16,1536]{2,1,0:T(8,128)(2,1)}) %all-reduce.8.cloned.1.call-update) | async-done | bytes 98320
  1093.2 7.4 fusion.12
  1145.2 18.9 %pad_maximum_fusion = f32[768,9216]{1,0:T(8,128)} fusion(f32[768,3072]{1,0:T(8,128)} %convolution_bitcast_fusion.4, f32[768,3072]{1,0:T(8,128)} %convolution_bitcast_fusion.5, f32[768,768]{1,0:T(8,128)S(1)} %convolution_bitcast_fusion.7, f32[768,2304]{1,0:T(8,128)} %convolution_bitcast_fusion), kind=kLoop, calls=%fused_computation.2 | loop fusion | flops 21233664 | bytes 56623104 | tf_op jit(solution)/shard_map/concatenate | solution.py:220
  1179.8 18.7 %pad_maximum_fusion.1 = f32[768,9216]{1,0:T(8,128)} fusion(f32[768,3072]{1,0:T(8,128)} %convolution_bitcast_fusion.2, f32[768,3072]{1,0:T(8,128)} %convolution_bitcast_fusion.3, f32[768,768]{1,0:T(8,128)S(1)} %convolution_bitcast_fusion.6, f32[768,2304]{1,0:T(8,128)} %convolution_bitcast_fusion.1), kind=kLoop, calls=%fused_computation.3 | loop fusion | flops 21233664 | bytes 56623104 | tf_op jit(solution)/shard_map/concatenate | solution.py:220
  1205.4 56.0 %all-reduce.10.cloned.1.call-done = (f32[16,768]{1,0:T(8,128)}, f32[2,2,768]{2,1,0:T(2,128)}, f32[2,2,768]{2,1,0:T(2,128)}) async-done(((f32[16,768]{1,0:T(8,128)}, f32[2,2,768]{2,1,0:T(2,128)}, f32[2,2,768]{2,1,0:T(2,128)}), (f32[16,768]{1,0:T(8,128)}, f32[2,2,768]{2,1,0:T(2,128)}, f32[2,2,768]{2,1,0:T(2,128)})) %all-reduce.10.cloned.1.call-update) | async-done | bytes 73744
  1265.5 268.4 %reduce-scatter.7.cloned.1.call-done = f32[24,9216]{1,0:T(8,128)} async-done(((f32[768,9216]{1,0:T(8,128)}), f32[24,9216]{1,0:T(8,128)}) %reduce-scatter.7.cloned.1.call-update) | async-done | bytes 884752 | tf_op jit(solution)/shard_map/reduce_scatter | solution.py:308
  1533.9 270.8 %reduce-scatter.9.cloned.1.call-done = f32[24,9216]{1,0:T(8,128)} async-done(((f32[768,9216]{1,0:T(8,128)}), f32[24,9216]{1,0:T(8,128)}) %reduce-scatter.9.cloned.1.call-update) | async-done | bytes 884752 | tf_op jit(solution)/shard_map/reduce_scatter | solution.py:311
  (396 shorter events, 223.0 us)
Async XLA Ops:
  7.2 61.3 %copy-start.60 = (bf16[2,2,24]{2,1,0:T(2,128)(2,1)S(1)}, bf16[2,2,24]{2,1,0:T(2,128)(2,1)}, u32[]{:S(2)}) copy-start(bf16[2,2,24]{2,1,0:T(2,128)(2,1)} %param.17) | copy-start | bytes 580
  7.2 234.2 %all-gather.43.cloned.1.call-start = ((), (), s32[]{:S(2)}) async-start(), calls=%async_computation.4 | async-start | bytes 3649536 | tf_op jit(solution)/shard_map/all_gather | solution.py:225
  8.9 246.0 %all-gather.45.cloned.1.call-start = ((), (), s32[]{:S(2)}) async-start(), calls=%async_computation.5 | async-start | bytes 1216512 | tf_op jit(solution)/shard_map/all_gather | solution.py:226
  10.4 247.0 %all-gather.47.cloned.1.call-start = ((), (), s32[]{:S(2)}) async-start(), calls=%async_computation.6 | async-start | bytes 4866048 | tf_op jit(solution)/shard_map/all_gather | solution.py:227
  12.2 254.5 %all-gather.49.cloned.1.call-start = ((), (), s32[]{:S(2)}) async-start(), calls=%async_computation.7 | async-start | bytes 4866048 | tf_op jit(solution)/shard_map/all_gather | solution.py:228
  14.0 312.1 %all-gather.51.cloned.1.call-start = ((), (), s32[]{:S(2)}) async-start(), calls=%async_computation.8 | async-start | bytes 3649536 | tf_op jit(solution)/shard_map/all_gather | solution.py:236
  14.6 367.4 %all-gather.53.cloned.1.call-start = ((), (), s32[]{:S(2)}) async-start(), calls=%async_computation.9 | async-start | bytes 1216512 | tf_op jit(solution)/shard_map/all_gather | solution.py:237
  15.1 433.0 %all-gather.55.cloned.1.call-start = ((), (), s32[]{:S(2)}) async-start(), calls=%async_computation.10 | async-start | bytes 4866048 | tf_op jit(solution)/shard_map/all_gather | solution.py:238
  15.9 498.4 %all-gather.57.cloned.1.call-start = ((), (), s32[]{:S(2)}) async-start(), calls=%async_computation.11 | async-start | bytes 4866048 | tf_op jit(solution)/shard_map/all_gather | solution.py:239
  16.6 728.2 %all-gather.59.cloned.1.call-start = ((), (), s32[]{:S(2)}) async-start(), calls=%async_computation.12 | async-start | bytes 3649536 | tf_op jit(solution)/shard_map/all_gather | solution.py:225
  63.9 138.3 %copy-start.51 = (bf16[16,24]{1,0:T(8,128)(2,1)S(1)}, bf16[16,24]{1,0:T(8,128)(2,1)}, u32[]{:S(2)}) copy-start(bf16[16,24]{1,0:T(8,128)(2,1)} %param.12) | copy-start | bytes 2308
  63.9 177.3 %copy-start.59 = (s32[2,16]{1,0:T(2,128)S(1)}, s32[2,16]{1,0:T(2,128)}, u32[]{:S(2)}) copy-start(s32[2,16]{1,0:T(2,128)} %param.11) | copy-start | bytes 388
  63.9 177.5 %copy-start.12 = (bf16[2,256,768]{2,1,0:T(8,128)(2,1)S(1)}, bf16[2,256,768]{2,1,0:T(8,128)(2,1)}, u32[]{:S(2)}) copy-start(bf16[2,256,768]{2,1,0:T(8,128)(2,1)} %param.10) | copy-start | bytes 2359300
  520.4 236.9 %all-gather.61.cloned.1.call-start = ((), (), s32[]{:S(2)}) async-start(), calls=%async_computation.13 | async-start | bytes 1216512 | tf_op jit(solution)/shard_map/all_gather | solution.py:226
  521.2 240.2 %all-gather.63.cloned.1.call-start = ((), (), s32[]{:S(2)}) async-start(), calls=%async_computation.14 | async-start | bytes 4866048 | tf_op jit(solution)/shard_map/all_gather | solution.py:227
  522.0 264.6 %all-gather.65.cloned.1.call-start = ((), (), s32[]{:S(2)}) async-start(), calls=%async_computation.15 | async-start | bytes 4866048 | tf_op jit(solution)/shard_map/all_gather | solution.py:228
  522.8 308.7 %all-gather.67.cloned.1.call-start = ((), (), s32[]{:S(2)}) async-start(), calls=%async_computation.16 | async-start | bytes 3649536 | tf_op jit(solution)/shard_map/all_gather | solution.py:236
  523.5 363.8 %all-gather.69.cloned.1.call-start = ((), (), s32[]{:S(2)}) async-start(), calls=%async_computation.17 | async-start | bytes 1216512 | tf_op jit(solution)/shard_map/all_gather | solution.py:237
  524.1 429.3 %all-gather.71.cloned.1.call-start = ((), (), s32[]{:S(2)}) async-start(), calls=%async_computation.18 | async-start | bytes 4866048 | tf_op jit(solution)/shard_map/all_gather | solution.py:238
  524.7 494.7 %all-gather.73.cloned.1.call-start = ((), (), s32[]{:S(2)}) async-start(), calls=%async_computation.19 | async-start | bytes 4866048 | tf_op jit(solution)/shard_map/all_gather | solution.py:239
  744.6 341.0 %all-reduce.8.cloned.1.call-start = ((), (), s32[]{:S(2)}) async-start(), calls=%async_computation.20 | async-start | bytes 196608
  849.2 104.2 %copy-start.52 = (bf16[2,2,12,64]{3,2,1,0:T(8,128)(2,1)}, bf16[2,2,12,64]{3,2,1,0:T(8,128)(2,1)S(1)}, u32[]{:S(2)}) copy-start(bf16[2,2,12,64]{3,2,1,0:T(8,128)(2,1)S(1)} %reshape.323) | copy-start | bytes 18436
  849.5 107.1 %copy-start.35 = (f32[2,12,2,16]{3,2,1,0:T(2,128)}, f32[2,12,2,16]{3,2,1,0:T(2,128)S(1)}, u32[]{:S(2)}) copy-start(f32[2,12,2,16]{3,2,1,0:T(2,128)S(1)} %get-tuple-element.124) | copy-start | bytes 9220
  850.9 105.7 %copy-start.36 = (bf16[2,2,768]{2,1,0:T(2,128)(2,1)}, bf16[2,2,768]{2,1,0:T(2,128)(2,1)S(1)}, u32[]{:S(2)}) copy-start(bf16[2,2,768]{2,1,0:T(2,128)(2,1)S(1)} %convert_element_type.222) | copy-start | bytes 18436
  889.2 138.2 %copy-start.40 = (f32[2,2]{1,0:T(2,128)}, f32[2,2]{1,0:T(2,128)S(1)}, u32[]{:S(2)}) copy-start(f32[2,2]{1,0:T(2,128)S(1)} %add_rsqrt_fusion.5) | copy-start | bytes 52
  956.6 66.9 %copy-start.42 = (u8[2,3072]{1,0:T(4,128)(4,1)}, u8[2,3072]{1,0:T(4,128)(4,1)S(1)}, u32[]{:S(2)}) copy-start(u8[2,3072]{1,0:T(4,128)(4,1)S(1)} %get-tuple-element.53) | copy-start | bytes 18436
  956.6 66.9 %copy-start.44 = (u8[2,3072]{1,0:T(4,128)(4,1)}, u8[2,3072]{1,0:T(4,128)(4,1)S(1)}, u32[]{:S(2)}) copy-start(u8[2,3072]{1,0:T(4,128)(4,1)S(1)} %get-tuple-element.54) | copy-start | bytes 18436
  1036.0 56.5 %copy-start.47 = (f32[4,128]{1,0:T(4,128)S(1)}, f32[4,128]{1,0:T(4,128)}, u32[]{:S(2)}) copy-start(f32[4,128]{1,0:T(4,128)} %copy-done.46) | copy-start | bytes 6148
  1036.1 225.4 %all-reduce.10.cloned.1.call-start = ((), (), s32[]{:S(2)}) async-start(), calls=%async_computation.21 | async-start | bytes 147456
  1138.7 395.2 %reduce-scatter.7.cloned.1.call-start = ((), (), s32[]{:S(2)}) async-start(), calls=%async_computation.2 | async-start | bytes 29196288 | tf_op jit(solution)/shard_map/reduce_scatter | solution.py:308
  1164.2 640.5 %reduce-scatter.9.cloned.1.call-start = ((), (), s32[]{:S(2)}) async-start(), calls=%async_computation.3 | async-start | bytes 29196288 | tf_op jit(solution)/shard_map/reduce_scatter | solution.py:311
  1533.9 274.3 %copy-start.7 = (f32[24,9216]{1,0:T(8,128)S(1)}, f32[24,9216]{1,0:T(8,128)}, u32[]{:S(2)}) copy-start(f32[24,9216]{1,0:T(8,128)} %reduce-scatter.7.cloned.1.call-done) | copy-start | bytes 2654212
  (57 other events, 502.0 us)
Sparse Core Ops, SparseCore 0:
  11.6 63.5 all-gather.42
  78.3 52.6 all-gather.44
  134.5 62.9 all-gather.46
  200.9 63.1 all-gather.48
  267.0 59.0 all-gather.50
  328.9 52.9 all-gather.52
  385.5 62.5 all-gather.54
  451.7 62.4 all-gather.56
  520.6 59.3 all-gather.58
  582.8 53.1 all-gather.60
  639.6 63.7 all-gather.62
  706.8 62.4 all-gather.64
  772.4 59.0 all-gather.66
  834.3 52.9 all-gather.68
  890.8 62.5 all-gather.70
  956.9 62.4 all-gather.72
  1036.2 49.3 all-reduce.7
  1138.8 122.6 all-reduce.9
  1269.0 264.8 reduce-scatter.6
  1541.3 263.3 reduce-scatter.8
where the time goes:
time: 1830 us; the launch traced here: 1820 us
  waiting for transfers between devices  1050 us (57%)
  blocking collectives  430 us (23%)
  matrix products  160 us (9%)
  local copies, waits for them, and re-layouts  82.3 us (4%)
  other arithmetic  77.5 us (4%)
    reduce_scatter x1, waiting for transfers between devices, body(): lax.psum_scatter(weight_terms(cross_factors), ('dp', 'fsdp'), scatter_dim...  271 us
    reduce_scatter x1, waiting for transfers between devices, body(): lax.psum_scatter(weight_terms(seg_factors), ('dp', 'fsdp'), scatter_dimen...  268 us
    dot_general x47, matrix products, matmul(): return jnp.einsum(form, left, right, preferred_element_type=jnp.float32)  156 us
    all_gather x2, waiting for transfers between devices, gather_cross(): lax.all_gather(w_in[1], ('dp', 'fsdp'), axis=0, tiled=True)  128 us
    all_gather x2, waiting for transfers between devices, gather_cross(): lax.all_gather(w_back[1], ('dp', 'fsdp'), axis=1, tiled=True)  126 us
    unnamed x22, waiting for transfers between devices  106 us
    all_gather x2, blocking collectives, gather_segment(): lax.all_gather(norm_bias[0], ('dp', 'fsdp'), axis=1, tiled=True)  84.7 us
    all_gather x2, blocking collectives, gather_segment(): lax.all_gather(norm_gain[0], ('dp', 'fsdp'), axis=1, tiled=True)  80.5 us
  transfers between devices with their start and end apart: 20, of which 12 were waited for; matrix products, arithmetic and copies ran while one was open for 13% of the time, Pallas kernels for 0%

commit v1 on v0

--- a/solution.py
+++ b/solution.py
@@ -3,6 +3,8 @@
 import jax
 import jax.numpy as jnp
 from jax import lax
+from jax.experimental import pallas as pl
+from jax.experimental.pallas import tpu as pltpu
 from jax.sharding import PartitionSpec as P
 
 HEADS = 12
@@ -12,6 +14,813 @@
 epsilon = 1e-05
 root_half = 0.7071067811865476
 inv_root_tau = 0.3989422804014327
+
+bf16 = jnp.bfloat16
+f32 = jnp.float32
+MESH = pl.DeviceIdType.MESH
+VM = pltpu.VMEM
+MIB = 1024 * 1024
+ROWS = 48
+LANES = 128
+
+
+class Place:
+    def __init__(self):
+        self.dp = lax.axis_index("dp")
+        self.fsdp = lax.axis_index("fsdp")
+        self.y, self.x = self.dp // 2, self.dp % 2
+        self.z, self.core = self.fsdp // 2, self.fsdp % 2
+
+    def at(self, dp, z, core):
+        return (dp, z * 2 + core)
+
+    @property
+    def sib(self):
+        return (self.dp, self.z * 2 + 1 - self.core)
+
+    @property
+    def xdp(self):
+        return self.y * 2 + 1 - self.x
+
+    @property
+    def ydp(self):
+        return (1 - self.y) * 2 + self.x
+
+    @property
+    def xnbr(self):
+        return (self.xdp, self.fsdp)
+
+    @property
+    def ynbr(self):
+        return (self.ydp, self.fsdp)
+
+
+def greet(devices):
+    barrier = pltpu.get_barrier_semaphore()
+    for device in devices:
+        pl.semaphore_signal(barrier, inc=1, device_id=device, device_id_type=MESH)
+    pl.semaphore_wait(barrier, len(devices))
+
+
+def remote(src, dst, send, recv, device):
+    return pltpu.make_async_remote_copy(
+        src_ref=src, dst_ref=dst, send_sem=send, recv_sem=recv, device_id=device, device_id_type=MESH
+    )
+
+
+def lanes(start, size):
+    if isinstance(start, int):
+        return pl.ds(start, size)
+    return pl.ds(pl.multiple_of(start, LANES), size)
+
+
+def rows_at(start, size, unit):
+    return pl.ds(pl.multiple_of(start, unit), size)
+
+
+class Gather:
+    def __init__(self, place, out, block, start, width, index, sems, height2, slabs=False):
+        self.p, self.out, self.block, self.start, self.width = place, out, block, start, width
+        self.m, self.sems, self.h2, self.slabs = index, sems, height2, slabs
+        self.half = width // 2
+        tiles = self.half // LANES
+        self.a = (tiles + 1) // 2 * LANES
+        self.b = self.half - self.a
+        self.sent = []
+
+    def col(self, core, part):
+        base = core * self.half
+        if part == "A":
+            return base, self.a
+        if part == "B":
+            return base + self.a, self.b
+        return base, self.half
+
+    def dst(self, dp, z, core, part, count=1):
+        base, size = self.col(core, part)
+        return self.out.at[rows_at((dp * 4 + z) * self.h2, self.h2 * count, 16), lanes(base, size)]
+
+    def own(self, part, z=None):
+        base, size = self.col(self.p.core, part)
+        start = self.start + base
+        if self.slabs:
+            start = start + (self.p.z if z is None else z) * self.width
+        return self.block.at[:, lanes(start, size)]
+
+    def go(self, src, dst, slot, device, link=True):
+        send, recv = (self.sems[0], self.sems[1]) if link else (self.sems[2], self.sems[3])
+        copy = remote(src, dst, send.at[self.m, slot], recv.at[self.m, slot], device)
+        copy.start()
+        self.sent.append(copy)
+
+    def arrived(self, dst, slot, link=True):
+        send, recv = (self.sems[0], self.sems[1]) if link else (self.sems[2], self.sems[3])
+        remote(dst, dst, send.at[self.m, slot], recv.at[self.m, slot], self.p.sib).wait_recv()
+
+    def spread(self, src_of, z, d):
+        p = self.p
+        core = p.core
+        self.go(src_of("A"), self.dst(p.dp, z, core, "A"), 3 + d, p.xnbr)
+        if self.b:
+            self.go(src_of("B"), self.dst(p.dp, z, core, "B"), 15 + d, p.ynbr)
+        self.go(src_of("A"), self.dst(p.dp, z, core, "A"), 7 + d, p.ynbr)
+        if self.b:
+            self.go(src_of("B"), self.dst(p.dp, z, core, "B"), 19 + d, p.xnbr)
+
+    def send_own(self):
+        p = self.p
+        for d in (1, 3, 2):
+            z = (p.z + d) % 4
+            self.go(self.own("AB", z), self.dst(p.dp, p.z, p.core, "AB"), d - 1, p.at(p.dp, z, p.core))
+        self.spread(self.own, p.z, 0)
+
+    def pass_line(self):
+        p = self.p
+        for d in (1, 3, 2):
+            z = (p.z + 4 - d) % 4
+            self.arrived(self.dst(p.dp, z, p.core, "AB"), d - 1)
+            self.spread(lambda part: self.dst(p.dp, z, p.core, part), z, d)
+        line = self.dst(p.dp, 0, p.core, "AB", 4)
+        for d in (1, 2, 3):
+            z = (p.z + 4 - d) % 4
+            block = self.dst(p.dp, z, p.core, "AB")
+            self.go(block, block, 4 + d, p.sib, link=False)
+
+    def pass_plane(self):
+        p = self.p
+        for d in (0, 1, 3, 2):
+            z = (p.z + 4 - d) % 4
+            block = self.dst(p.xdp, z, p.core, "A")
+            self.arrived(block, 3 + d)
+            self.go(block, block, 11 + d, p.ynbr)
+            if self.b:
+                block = self.dst(p.ydp, z, p.core, "B")
+                self.arrived(block, 15 + d)
+                self.go(block, block, 23 + d, p.xnbr)
+        block = self.dst(p.xdp, 0, p.core, "A", 4)
+        self.go(block, block, 0, p.sib, link=False)
+        if self.b:
+            block = self.dst(p.ydp, 0, p.core, "B", 4)
+            self.go(block, block, 1, p.sib, link=False)
+
+    def last(self):
+        p = self.p
+        core, other = p.core, 1 - p.core
+        far = (1 - p.y) * 2 + 1 - p.x
+        for d in range(4):
+            z = (p.z + 4 - d) % 4
+            self.arrived(self.dst(p.ydp, z, core, "A"), 7 + d)
+            if self.b:
+                self.arrived(self.dst(p.xdp, z, core, "B"), 19 + d)
+        block = self.dst(p.ydp, 0, core, "A", 4)
+        self.go(block, block, 2, p.sib, link=False)
+        if self.b:
+            block = self.dst(p.xdp, 0, core, "B", 4)
+            self.go(block, block, 3, p.sib, link=False)
+        for d in range(4):
+            z = (p.z + 4 - d) % 4
+            self.arrived(self.dst(far, z, core, "A"), 11 + d)
+            if self.b:
+                self.arrived(self.dst(far, z, core, "B"), 23 + d)
+        block = self.dst(far, 0, core, "AB" if self.b else "A", 4)
+        self.go(block, block, 4, p.sib, link=False)
+
+    def drain(self):
+        p = self.p
+        other = 1 - p.core
+        far = (1 - p.y) * 2 + 1 - p.x
+        for d in (1, 2, 3):
+            z = (p.z + 4 - d) % 4
+            self.arrived(self.dst(p.dp, z, other, "AB"), 4 + d, link=False)
+        self.arrived(self.dst(p.xdp, 0, other, "A", 4), 0, link=False)
+        if self.b:
+            self.arrived(self.dst(p.ydp, 0, other, "B", 4), 1, link=False)
+        self.arrived(self.dst(p.ydp, 0, other, "A", 4), 2, link=False)
+        if self.b:
+            self.arrived(self.dst(p.xdp, 0, other, "B", 4), 3, link=False)
+        self.arrived(self.dst(far, 0, other, "AB" if self.b else "A", 4), 4, link=False)
+
+    def finish(self):
+        for copy in self.sent:
+            copy.wait_send()
+
+
+def run_gathers(gathers):
+    n = len(gathers)
+    for step in range(n + 3):
+        if step < n:
+            gathers[step].send_own()
+        if 0 <= step - 1 < n:
+            gathers[step - 1].pass_line()
+            gathers[step - 1].pass_plane()
+        if 0 <= step - 2 < n:
+            gathers[step - 2].last()
+        if 0 <= step - 3 < n:
+            gathers[step - 3].drain()
+    for g in gathers:
+        g.finish()
+
+
+def gather_peers(p):
+    peers = [p.sib, p.xnbr, p.ynbr]
+    for d in (1, 2, 3):
+        peers.append(p.at(p.dp, (p.z + d) % 4, p.core))
+    return peers
+
+
+def everyone(p):
+    return [
+        (lax.rem(p.dp + i, 4), lax.rem(p.fsdp + j, 8)) for i in range(4) for j in range(8) if i or j
+    ]
+
+
+GATHER_SEMS = lambda n: [
+    pltpu.SemaphoreType.DMA((n, 27)),
+    pltpu.SemaphoreType.DMA((n, 27)),
+    pltpu.SemaphoreType.DMA((n, 8)),
+    pltpu.SemaphoreType.DMA((n, 8)),
+]
+
+
+def pair_rows(p, own_ref, sib_ref, block_ref, send, recv):
+    copy = remote(own_ref, sib_ref, send, recv, p.sib)
+    copy.start()
+    copy.wait()
+    height, width = block_ref.shape[0] // 2, own_ref.shape[1]
+    step = 1024
+    first = p.core == 0
+
+    def chunk(at, size):
+        mine = own_ref[:, lanes(at, size)].astype(f32)[:height]
+        theirs = sib_ref[:, lanes(at, size)].astype(f32)[:height]
+        both = jnp.concatenate(
+            [jnp.where(first, mine, theirs), jnp.where(first, theirs, mine)], axis=0
+        )
+        block_ref[:, lanes(at, size)] = both.astype(bf16)
+
+    @pl.loop(0, width // step)
+    def _(i):
+        chunk(i * step, step)
+
+    if width % step:
+        chunk(width // step * step, width % step)
+
+
+def weights_kernel(widths, pack_ref, *refs):
+    n = len(widths)
+    outs, cross_out, wo_out = refs[:n], refs[n], refs[n + 1]
+    sib_buf, block, s0, s1, s2, s3, pair_send, pair_recv, wo_send, wo_recv, local = refs[n + 2 :]
+    p = Place()
+    greet(everyone(p))
+    pair_rows(p, pack_ref, sib_buf, block, pair_send, pair_recv)
+    sems = (s0, s1, s2, s3)
+    gathers, copies, at = [], [], 0
+    key = rows_at((p.dp * 4 + p.z) * ROWS, ROWS, 16)
+    for i, width in enumerate(widths):
+        gathers.append(Gather(p, outs[i], block, at, width, i, sems, ROWS))
+        copies.append((block.at[:, lanes(at, width)], outs[i].at[key]))
+        at += width
+    cw = cross_out.shape[1]
+    gathers.append(Gather(p, cross_out, block, at, cw, n, sems, ROWS, slabs=True))
+    copies.append((block.at[:, lanes(at + p.z * cw, cw)], cross_out.at[key]))
+    at += 4 * cw
+    for i, (src, dst) in enumerate(copies):
+        pltpu.make_async_copy(src, dst, local.at[i]).start()
+    width = wo_out.shape[1]
+    half = width // 2
+    wo_src = block.at[:, lanes(at + p.core * half, half)]
+    wo_dst = wo_out.at[rows_at(p.z * ROWS, ROWS, 16), lanes(p.core * half, half)]
+    for i in range(4):
+        copy = remote(wo_src, wo_dst, wo_send.at[i], wo_recv.at[p.z], p.at(i, p.dp, p.core))
+        here = jnp.logical_and(p.dp == i, p.dp == p.z)
+
+        @pl.when(jnp.logical_not(here))
+        def _():
+            copy.start()
+
+        @pl.when(here)
+        def _():
+            mine = pltpu.make_async_copy(wo_src, wo_dst, local.at[n + 1])
+            mine.start()
+            mine.wait()
+
+    run_gathers(gathers)
+    for i in range(4):
+        piece = wo_out.at[pl.ds(i * ROWS, ROWS), lanes(p.core * half, half)]
+        here = jnp.logical_and(p.z == p.dp, p.z == i)
+
+        @pl.when(jnp.logical_not(here))
+        def _():
+            remote(piece, piece, wo_send.at[i], wo_recv.at[i], p.sib).wait_recv()
+
+    mine = wo_out.at[:, lanes(p.core * half, half)]
+    theirs = wo_out.at[:, lanes((1 - p.core) * half, half)]
+    copy = remote(mine, mine, wo_send.at[4], wo_recv.at[4], p.sib)
+    copy.start()
+    remote(theirs, theirs, wo_send.at[4], wo_recv.at[4], p.sib).wait_recv()
+    copy.wait_send()
+    for i in range(4):
+        here = jnp.logical_and(p.dp == i, p.dp == p.z)
+
+        @pl.when(jnp.logical_not(here))
+        def _():
+            remote(wo_src, wo_dst, wo_send.at[i], wo_recv.at[p.z], p.at(i, p.dp, p.core)).wait_send()
+
+    for i, (src, dst) in enumerate(copies):
+        pltpu.make_async_copy(src, dst, local.at[i]).wait()
+
+
+def gather_weights(pack, widths, cross_width, wo_width):
+    n = len(widths)
+    rows = 16 * ROWS
+    outs = [jax.ShapeDtypeStruct((rows, w), bf16) for w in widths]
+    outs += [jax.ShapeDtypeStruct((rows, cross_width), bf16), jax.ShapeDtypeStruct((192, wo_width), bf16)]
+    height, total = pack.shape
+    return pl.pallas_call(
+        partial(weights_kernel, widths),
+        out_shape=outs,
+        in_specs=[pl.BlockSpec(memory_space=VM)],
+        out_specs=[pl.BlockSpec(memory_space=pl.ANY)] * len(outs),
+        scratch_shapes=[pltpu.VMEM((height, total), bf16), pltpu.VMEM((ROWS, total), bf16)]
+        + GATHER_SEMS(n + 1)
+        + [
+            pltpu.SemaphoreType.DMA,
+            pltpu.SemaphoreType.DMA,
+            pltpu.SemaphoreType.DMA((5,)),
+            pltpu.SemaphoreType.DMA((5,)),
+            pltpu.SemaphoreType.DMA((n + 2,)),
+        ],
+        compiler_params=pltpu.CompilerParams(
+            collective_id=0, has_side_effects=True, vmem_limit_bytes=32 * MIB
+        ),
+    )(pack)
+
+
+class Scatter:
+    def __init__(self, place, grad, out, index, sems, acc, pair, r1a, r1b, r2a, r2b, r3, give):
+        self.p, self.grad, self.out, self.m = place, grad, out, index
+        self.send, self.recv, self.local = sems
+        self.acc, self.pair, self.r1a, self.r1b = acc, pair, r1a, r1b
+        self.r2a, self.r2b, self.r3, self.give = r2a, r2b, r3, give
+        self.half = grad.shape[1] // 2
+        tiles = self.half // LANES
+        self.a = (tiles + 1) // 2 * LANES
+        self.b = self.half - self.a
+        self.sent = []
+        p = place
+        far = (1 - p.y) * 2 + 1 - p.x
+        self.groups = (far, p.ydp, p.xdp, p.dp)
+
+    def group(self, ref, dp):
+        return ref.at[rows_at(dp * 4 * ROWS, 4 * ROWS, 16)]
+
+    def go(self, src, dst, slot, device):
+        copy = remote(src, dst, self.send.at[self.m, slot], self.recv.at[self.m, slot], device)
+        copy.start()
+        self.sent.append(copy)
+
+    def arrived(self, dst, slot):
+        remote(dst, dst, self.send.at[self.m, slot], self.recv.at[self.m, slot], self.p.sib).wait_recv()
+
+    def load(self, i):
+        p = self.p
+        mine = self.group(self.grad, self.groups[i]).at[:, lanes(p.core * self.half, self.half)]
+        return pltpu.make_async_copy(mine, self.group(self.acc, self.groups[i]), self.local.at[self.m, i])
+
+    def start(self):
+        p = self.p
+        for i, dp in enumerate(self.groups):
+            theirs = self.group(self.grad, dp).at[:, lanes((1 - p.core) * self.half, self.half)]
+            self.go(theirs, self.group(self.pair, dp), i, p.sib)
+            self.load(i).start()
+
+    def add(self, dp, part, other, other_row=0):
+        at, size = {"A": (0, self.a), "B": (self.a, self.b), "AB": (0, self.half)}[part]
+        base = dp * 4 * ROWS
+
+        @pl.loop(0, 4)
+        def _(i):
+            key = (rows_at(base + i * ROWS, ROWS, 16), pl.ds(at, size))
+            more = other[rows_at(other_row + i * ROWS, ROWS, 16), :]
+            self.acc[key] = (self.acc[key].astype(f32) + more.astype(f32)).astype(bf16)
+
+    def side(self, dp, part):
+        at, size = (0, self.a) if part == "A" else (self.a, self.b)
+        return self.group(self.acc, dp).at[:, pl.ds(at, size)]
+
+    def one(self):
+        p = self.p
+        for i, dp in enumerate(self.groups):
+            self.arrived(self.group(self.pair, dp), i)
+            self.load(i).wait()
+            self.add(dp, "AB", self.pair, dp * 4 * ROWS)
+            if i == 0:
+                self.go(self.side(dp, "A"), self.r1a.at[pl.ds(0, 4 * ROWS)], 4, p.ynbr)
+                if self.b:
+                    self.go(self.side(dp, "B"), self.r1b.at[pl.ds(0, 4 * ROWS)], 6, p.xnbr)
+            if i == 1:
+                self.go(self.side(dp, "A"), self.r1a.at[pl.ds(4 * ROWS, 4 * ROWS)], 5, p.ynbr)
+            if i == 2 and self.b:
+                self.go(self.side(dp, "B"), self.r1b.at[pl.ds(4 * ROWS, 4 * ROWS)], 7, p.xnbr)
+
+    def two(self):
+        p = self.p
+        self.arrived(self.r1a.at[pl.ds(0, 4 * ROWS)], 4)
+        self.add(p.xdp, "A", self.r1a)
+        self.go(self.side(p.xdp, "A"), self.r2a, 8, p.xnbr)
+        if self.b:
+            self.arrived(self.r1b.at[pl.ds(0, 4 * ROWS)], 6)
+            self.add(p.ydp, "B", self.r1b)
+            self.go(self.side(p.ydp, "B"), self.r2b, 9, p.ynbr)
+        self.arrived(self.r1a.at[pl.ds(4 * ROWS, 4 * ROWS)], 5)
+        self.add(p.dp, "A", self.r1a, 4 * ROWS)
+        if self.b:
+            self.arrived(self.r1b.at[pl.ds(4 * ROWS, 4 * ROWS)], 7)
+            self.add(p.dp, "B", self.r1b, 4 * ROWS)
+
+    def three(self):
+        p = self.p
+        self.arrived(self.r2a, 8)
+        self.add(p.dp, "A", self.r2a)
+        if self.b:
+            self.arrived(self.r2b, 9)
+            self.add(p.dp, "B", self.r2b)
+        for d in (1, 3, 2):
+            z = (p.z + d) % 4
+            src = self.acc.at[rows_at((p.dp * 4 + z) * ROWS, ROWS, 16)]
+            self.go(src, self.r3.at[d - 1], 9 + d, p.at(p.dp, z, p.core))
+
+    def four(self):
+        p = self.p
+        for d in (1, 3, 2):
+            self.arrived(self.r3.at[d - 1], 9 + d)
+        rows = rows_at((p.dp * 4 + p.z) * ROWS, ROWS, 16)
+        step = self.a if self.b == self.a else self.half
+
+        def chunk(at, size):
+            cols = pl.ds(at, size)
+            total = self.acc[rows, cols].astype(f32)
+            for d in range(3):
+                total = total + self.r3[d, :, cols].astype(f32)
+            upper, lower = total[: ROWS // 2], total[ROWS // 2 :]
+            first = p.core == 0
+            self.give[:, cols] = jnp.where(first, lower, upper)
+            self.out[:, lanes(p.core * self.half + at, size)] = jnp.where(first, upper, lower)
+
+        for at in range(0, self.half, step):
+            chunk(at, step)
+        self.go(self.give, self.out.at[:, lanes(p.core * self.half, self.half)], 13, p.sib)
+
+    def five(self):
+        p = self.p
+        self.arrived(self.out.at[:, lanes((1 - p.core) * self.half, self.half)], 13)
+
+    def finish(self):
+        for copy in self.sent:
+            copy.wait_send()
+
+
+def scatter_kernel(n, *refs):
+    grads, outs = refs[:n], refs[n : 2 * n]
+    scratch = refs[2 * n :]
+    sems = scratch[:3]
+    p = Place()
+    greet(gather_peers(p))
+    jobs = []
+    for i in range(n):
+        bufs = scratch[3 + 8 * i : 11 + 8 * i]
+        jobs.append(Scatter(p, grads[i], outs[i], i, sems, *bufs))
+    for job in jobs:
+        job.start()
+    for step in range(n + 4):
+        for lag, name in enumerate(("one", "two", "three", "four", "five")):
+            if 0 <= step - lag < n:
+                getattr(jobs[step - lag], name)()
+    for job in jobs:
+        job.finish()
+
+
+def scatter_grads(grads):
+    n = len(grads)
+    bufs = []
+    for g in grads:
+        half = g.shape[1] // 2
+        tiles = half // LANES
+        a = (tiles + 1) // 2 * LANES
+        b = max(half - a, LANES)
+        rows = g.shape[0]
+        bufs += [
+            pltpu.VMEM((rows, half), bf16),
+            pltpu.VMEM((rows, half), bf16),
+            pltpu.VMEM((8 * ROWS, a), bf16),
+            pltpu.VMEM((8 * ROWS, b), bf16),
+            pltpu.VMEM((4 * ROWS, a), bf16),
+            pltpu.VMEM((4 * ROWS, b), bf16),
+            pltpu.VMEM((3, ROWS, half), bf16),
+            pltpu.VMEM((ROWS // 2, half), f32),
+        ]
+    return pl.pallas_call(
+        partial(scatter_kernel, n),
+        out_shape=[jax.ShapeDtypeStruct((ROWS // 2, g.shape[1]), f32) for g in grads],
+        in_specs=[pl.BlockSpec(memory_space=pl.ANY)] * n,
+        out_specs=[pl.BlockSpec(memory_space=VM)] * n,
+        scratch_shapes=[
+            pltpu.SemaphoreType.DMA((n, 14)),
+            pltpu.SemaphoreType.DMA((n, 14)),
+            pltpu.SemaphoreType.DMA((n, 4)),
+        ]
+        + bufs,
+        compiler_params=pltpu.CompilerParams(
+            collective_id=1, has_side_effects=True, vmem_limit_bytes=48 * MIB
+        ),
+    )(*grads)
+
+
+NEG = -1e30
+
+
+def mm(a, b, dims):
+    return lax.dot_general(a, b, (dims, ((), ())), preferred_element_type=f32)
+
+
+NN = ((1,), (0,))
+NT = ((1,), (1,))
+TN = ((0,), (0,))
+
+
+def norm_rows(summed, gain, bias):
+    centred = summed - jnp.mean(summed, axis=-1, keepdims=True)
+    variance = jnp.mean(centred * centred, axis=-1, keepdims=True)
+    inverse = lax.rsqrt(variance + epsilon)
+    scaled = centred * inverse
+    return scaled * gain + bias, scaled, inverse
+
+
+def norm_rows_back(grad, scaled, inverse, gain):
+    g = grad * gain
+    first = jnp.mean(g, axis=-1, keepdims=True)
+    second = jnp.mean(g * scaled, axis=-1, keepdims=True)
+    return inverse * (g - first - scaled * second)
+
+
+def gelu_parts(u):
+    cumulative = 0.5 * (1.0 + lax.erf(u * root_half))
+    return cumulative, cumulative + u * inv_root_tau * jnp.exp(-0.5 * u * u)
+
+
+def cross_kernel(
+    lead_ref, mask_ref, norm_ref, w_ref, wo_ref, home_ref, fac_ref, small_ref,
+    gbuf, lead, xbuf, ybuf, dpack, g_send, g_recv, x_send, x_recv, h_send, h_recv, local,
+):
+    p = Place()
+    group = [(p.dp, lax.rem(p.fsdp + j, 8)) for j in range(1, 8)]
+    greet(group)
+    width = lead_ref.shape[2] // 2
+    slab = width // 4
+    head = width // HEADS
+    heads = HEADS // 4
+
+    def lead_copy(z, j):
+        i = 2 * z + j
+        return remote(lead_ref.at[j], gbuf.at[p.fsdp], g_send.at[i], g_recv.at[p.fsdp], (p.dp, i))
+
+    for d in range(4):
+        z = (p.z + d) % 4
+        for j in range(2):
+            here = jnp.logical_and(p.z == z, p.core == j) if d == 0 else None
+            if d:
+                lead_copy(z, j).start()
+            else:
+
+                @pl.when(p.core != j)
+                def _():
+                    lead_copy(z, j).start()
+
+                @pl.when(p.core == j)
+                def _():
+                    mine = pltpu.make_async_copy(lead_ref.at[j], gbuf.at[p.fsdp], local)
+                    mine.start()
+                    mine.wait()
+
+    for d in range(1, 8):
+        i = lax.rem(p.fsdp + d, 8)
+        remote(gbuf.at[i], gbuf.at[i], g_send.at[i], g_recv.at[i], p.sib).wait_recv()
+    for i in range(8):
+        lead[2 * i : 2 * i + 2, :] = gbuf[i]
+    states = lead[:, :width]
+    cot = lead[:, width:]
+
+    def sum_z(e, partial_sum):
+        xbuf[e, p.z] = partial_sum.astype(bf16)
+        copies = []
+        for d in (1, 3, 2):
+            z = (p.z + d) % 4
+            copy = remote(
+                xbuf.at[e, p.z], xbuf.at[e, p.z], x_send.at[e, d - 1], x_recv.at[e, p.z],
+                p.at(p.dp, z, p.core),
+            )
+            copy.start()
+            copies.append(copy)
+        for d in (1, 3, 2):
+            z = (p.z + d) % 4
+            piece = xbuf.at[e, z]
+            remote(piece, piece, x_send.at[e, d - 1], x_recv.at[e, z], p.sib).wait_recv()
+        for copy in copies:
+            copy.wait_send()
+        return sum(xbuf[e, z].astype(f32) for z in range(4))
+
+    gain0, gain1 = norm_ref[0:1, :], norm_ref[1:2, :]
+    bias0, bias1 = norm_ref[2:3, :], norm_ref[3:4, :]
+    in_cols, back_cols = pl.ds(3 * slab, width), pl.ds(3 * slab + width, width)
+    qkv_cols = pl.ds(0, 3 * slab)
+    factor = head ** (-0.5)
+    allowed = mask_ref[...] > 0.5
+
+    xl = states.astype(bf16)
+    packed = mm(xl, w_ref[:, qkv_cols], NN).astype(bf16)
+    q = [packed[:, i * head : (i + 1) * head] for i in range(heads)]
+    k = [packed[:, slab + i * head : slab + (i + 1) * head] for i in range(heads)]
+    v = [packed[:, 2 * slab + i * head : 2 * slab + (i + 1) * head] for i in range(heads)]
+    att, context = [], []
+    for i in range(heads):
+        scores = jnp.where(allowed, mm(q[i], k[i], NT) * factor, NEG)
+        top = jnp.max(scores, axis=-1, keepdims=True)
+        terms = jnp.exp(scores - top)
+        a = terms / jnp.sum(terms, axis=-1, keepdims=True)
+        att.append(a)
+        context.append(mm(a.astype(bf16), v[i], NN))
+    context = jnp.concatenate(context, axis=1).astype(bf16)
+    branch = sum_z(0, mm(context, wo_ref[...], NN))
+    normed, z_one, r_one = norm_rows(states + branch, gain0, bias0)
+    nl = normed.astype(bf16)
+    hidden = mm(nl, w_ref[:, in_cols], NN)
+    phi, slope = gelu_parts(hidden)
+    active = (hidden * phi).astype(bf16)
+    feed = sum_z(1, mm(active, w_ref[:, back_cols], NT))
+    result, z_two, r_two = norm_rows(normed + feed, gain1, bias1)
+    d_two = norm_rows_back(cot, z_two, r_two, gain1)
+    df = d_two.astype(bf16)
+    du = (mm(df, w_ref[:, back_cols], NN) * slope).astype(bf16)
+    d_normed = d_two + sum_z(2, mm(du, w_ref[:, in_cols], NT))
+    d_one = norm_rows_back(d_normed, z_one, r_one, gain0)
+    db = d_one.astype(bf16)
+    dc = mm(db, wo_ref[...], NT).astype(bf16)
+    for i in range(heads):
+        a = att[i]
+        dci = dc[:, i * head : (i + 1) * head]
+        da = mm(dci, v[i], NT)
+        dv = mm(a.astype(bf16), dci, TN)
+        ds = (a * (da - jnp.sum(a * da, axis=-1, keepdims=True))).astype(bf16)
+        dq = mm(ds, k[i], NN) * factor
+        dk = mm(ds, q[i], TN) * factor
+        for j, piece in enumerate((dq, dk, dv)):
+            dpack[:, j * slab + i * head : j * slab + (i + 1) * head] = piece
+    dp = dpack[...].astype(bf16)
+    dx = d_one + sum_z(3, mm(dp, w_ref[:, qkv_cols], NT))
+    for i in range(8):
+        ybuf[i, :, :width] = result[2 * i : 2 * i + 2]
+        ybuf[i, :, width:] = dx[2 * i : 2 * i + 2]
+    home = remote(
+        ybuf.at[2 * p.z + 1 - p.core], home_ref.at[p.core], h_send, h_recv, p.sib
+    )
+    home.start()
+    home_ref[p.core] = ybuf[2 * p.z + p.core]
+
+    def part(full):
+        pieces = [full[:, i * slab : (i + 1) * slab] for i in range(4)]
+        out = pieces[0]
+        for i in range(1, 4):
+            out = jnp.where(p.z == i, pieces[i], out)
+        return out.astype(bf16)
+
+    fac_ref[:, :width] = active
+    fac_ref[:, width : 2 * width] = du
+    fac_ref[:, 2 * width :] = jnp.concatenate(
+        [dp, part(d_one), part(states), part(normed), part(d_two), context], axis=1
+    )
+    once = jnp.where(p.z == 0, 1.0, 0.0)
+    sums = [d_normed * z_one, cot * z_two, d_normed, cot]
+    small_ref[...] = jnp.zeros_like(small_ref)
+    for i, s in enumerate(sums):
+        small_ref[i : i + 1, :] = once * jnp.sum(s, axis=0, keepdims=True)
+    theirs = home_ref.at[1 - p.core]
+    remote(theirs, theirs, h_send, h_recv, p.sib).wait_recv()
+    home.wait_send()
+    for d in range(4):
+        z = (p.z + d) % 4
+        for j in range(2):
+            if d:
+                lead_copy(z, j).wait_send()
+            else:
+
+                @pl.when(p.core != j)
+                def _():
+                    lead_copy(z, j).wait_send()
+
+
+def cross_block(lead, mask, norms, weights, wo):
+    width = wo.shape[1]
+    segs = mask.shape[0]
+    return pl.pallas_call(
+        cross_kernel,
+        out_shape=[
+            jax.ShapeDtypeStruct((2, 2, 2 * width), f32),
+            jax.ShapeDtypeStruct((segs, 4 * width), bf16),
+            jax.ShapeDtypeStruct((8, width), f32),
+        ],
+        in_specs=[pl.BlockSpec(memory_space=VM)] * 5,
+        out_specs=[pl.BlockSpec(memory_space=VM)] * 3,
+        scratch_shapes=[
+            pltpu.VMEM((8, 2, 2 * width), f32),
+            pltpu.VMEM((segs, 2 * width), f32),
+            pltpu.VMEM((4, 4, segs, width), bf16),
+            pltpu.VMEM((8, 2, 2 * width), f32),
+            pltpu.VMEM((segs, 3 * width // 4), f32),
+            pltpu.SemaphoreType.DMA((8,)),
+            pltpu.SemaphoreType.DMA((8,)),
+            pltpu.SemaphoreType.DMA((4, 3)),
+            pltpu.SemaphoreType.DMA((4, 4)),
+            pltpu.SemaphoreType.DMA,
+            pltpu.SemaphoreType.DMA,
+            pltpu.SemaphoreType.DMA,
+        ],
+        compiler_params=pltpu.CompilerParams(
+            collective_id=2, has_side_effects=True, vmem_limit_bytes=32 * MIB
+        ),
+    )(lead, mask, norms, weights, wo)
+
+
+def factor_kernel(fac_ref, qkv_ref, out_ref, in_ref, back_ref, sib_buf, block, full, tmp, *sems):
+    p = Place()
+    greet(gather_peers(p))
+    lead2 = block.shape[0]
+    lead = lead2 // 2
+    copy = remote(fac_ref, sib_buf, sems[4], sems[5], p.sib)
+    copy.start()
+    copy.wait()
+    block[rows_at(p.core * lead, lead, 16), :] = fac_ref[...]
+    block[rows_at((1 - p.core) * lead, lead, 16), :] = sib_buf[...]
+    width = full.shape[1]
+    model = width // 4
+    slab = model // 4
+    key = rows_at((p.dp * 4 + p.z) * lead2, lead2, 16)
+    mine = pltpu.make_async_copy(block, full.at[key], sems[6])
+    mine.start()
+    run_gathers([Gather(p, full, block, 0, width, 0, sems[:4], lead2)])
+    mine.wait()
+
+    def rows_of(z, at, size):
+        return jnp.concatenate(
+            [full[rows_at((i * 4 + z) * lead2, lead2, 16), pl.ds(at, size)] for i in range(4)], axis=0
+        )
+
+    base = 2 * model + 3 * slab
+    mid = p.dp
+    xl = rows_of(mid, base + slab, slab)
+    nl = rows_of(mid, base + 2 * slab, slab)
+    df = rows_of(mid, base + 3 * slab, slab)
+    ctx = rows_of(mid, base + 4 * slab, slab)
+    own = rows_at(p.fsdp * (ROWS // 2), ROWS // 2, 8)
+    for z in range(4):
+        tmp[:, :model] = mm(df, rows_of(z, 0, model), TN)
+        back_ref[:, z * model : (z + 1) * model] = tmp[own, :model]
+        tmp[:, :model] = mm(nl, rows_of(z, model, model), TN)
+        in_ref[:, z * model : (z + 1) * model] = tmp[own, :model]
+        tmp[:, : 3 * slab] = mm(xl, rows_of(z, 2 * model, 3 * slab), TN)
+        got = tmp[own, : 3 * slab]
+        for j in range(3):
+            at = j * model + z * slab
+            qkv_ref[:, at : at + slab] = got[:, j * slab : (j + 1) * slab]
+        tmp[:, :slab] = mm(ctx, rows_of(z, base, slab), TN)
+        out_ref[:, z * slab : (z + 1) * slab] = tmp[own, :slab]
+
+
+def factor_grads(fac):
+    lead, width = fac.shape
+    model = width // 4
+    half = ROWS // 2
+    return pl.pallas_call(
+        factor_kernel,
+        out_shape=[
+            jax.ShapeDtypeStruct((half, 3 * model), f32),
+            jax.ShapeDtypeStruct((half, model), f32),
+            jax.ShapeDtypeStruct((half, width), f32),
+            jax.ShapeDtypeStruct((half, width), f32),
+        ],
+        in_specs=[pl.BlockSpec(memory_space=VM)],
+        out_specs=[pl.BlockSpec(memory_space=VM)] * 4,
+        scratch_shapes=[
+            pltpu.VMEM((lead, width), bf16),
+            pltpu.VMEM((2 * lead, width), bf16),
+            pltpu.VMEM((32 * lead, width), bf16),
+            pltpu.VMEM((model // 4, model), f32),
+        ]
+        + GATHER_SEMS(1)
+        + [pltpu.SemaphoreType.DMA, pltpu.SemaphoreType.DMA, pltpu.SemaphoreType.DMA],
+        compiler_params=pltpu.CompilerParams(
+            collective_id=3, has_side_effects=True, vmem_limit_bytes=32 * MIB
+        ),
+    )(fac)
 
 
 def matmul(left, right, form):
@@ -292,14 +1101,6 @@
         pos_embed, w_qkv, w_out, w_in, w_back, norm_gain, norm_bias
     )
     output, kept = layer_forward(tokens, doc_ids, seg_weights, cross_weights, pos_full)
-    shards = lax.optimization_barrier(
-        (output, tokens, pos_embed, w_qkv, w_out, w_in, w_back, norm_gain, norm_bias)
-    )
-    seg_weights = gather_segment(shards[3], shards[4], shards[5], shards[6], shards[7], shards[8])
-    cross_weights, pos_full = gather_cross(
-        shards[2], shards[3], shards[4], shards[5], shards[6], shards[7], shards[8]
-    )
-    recomputed, kept = layer_forward(shards[1], doc_ids, seg_weights, cross_weights, pos_full)
     grad_tokens, seg_factors, cross_factors, seg_smalls, cross_smalls, grad_pos = layer_backward(
         cotangent, doc_ids, kept, seg_weights, cross_weights
     )
@@ -336,9 +1137,110 @@
     )
 
 
+def block_backward_terms(factors):
+    (
+        states_low,
+        grad_packed,
+        context,
+        grad_branch,
+        normed_low,
+        grad_hidden,
+        grad_feed,
+        active_low,
+    ) = factors
+    return (
+        matmul(grad_feed, active_low, "gld,glf->df").astype(bf16),
+        matmul(normed_low, grad_hidden, "gld,glf->df").astype(bf16),
+        matmul(context, grad_branch, "gld,gle->de").astype(bf16),
+        matmul(states_low, grad_packed, "gld,gle->de").astype(bf16),
+    )
+
+
+def make_pack(pos_embed, w_qkv, w_out, w_in, w_back, norm_gain, norm_bias):
+    own, width = w_out.shape[1:]
+    slab = width // 4
+    items = jnp.concatenate([norm_gain[0], norm_bias[0], norm_gain[1], norm_bias[1], pos_embed], axis=0)
+    small = jnp.pad(items.T, ((0, 0), (0, 256 - items.shape[0])))
+    cross = jnp.concatenate(
+        [
+            w_qkv[1].reshape(own, 3, 4, slab).transpose(0, 2, 1, 3).reshape(own, 4, 3 * slab),
+            w_in[1].reshape(own, 4, width),
+            w_back[1].T.reshape(own, 4, width),
+            jnp.zeros((own, 4, slab), bf16),
+        ],
+        axis=2,
+    ).reshape(own, 12 * width)
+    pack = jnp.concatenate(
+        [w_qkv[0], small, w_out[0], w_in[0], w_back[0].T, cross, w_out[1]], axis=1
+    )
+    return jnp.pad(pack, ((0, 32 - own), (0, 0)))
+
+
+def fast_body(tokens, doc_ids, pos_embed, w_qkv, w_out, w_in, w_back, norm_gain, norm_bias, cotangent):
+    rows, local_len, width = tokens.shape
+    seg_count = local_len // SEG_LEN
+    hidden = w_in.shape[2]
+    pack = make_pack(pos_embed, w_qkv, w_out, w_in, w_back, norm_gain, norm_bias)
+    seg_qkv, small, seg_out_w, seg_in, seg_back, cross_w, cross_wo = gather_weights(
+        pack, (3 * width, 256, width, hidden, hidden), 3 * width, width
+    )
+    items = small.T.astype(f32)
+    seg_weights = (seg_qkv, seg_out_w, seg_in, seg_back.T, items[0:2], items[2:4])
+    cross_norms = jnp.concatenate([items[4:8], jnp.zeros((4, width), f32)], axis=0)
+    pos_full = items[8 : 8 + doc_ids.shape[1]]
+
+    segments = tokens.reshape(rows * seg_count, SEG_LEN, width).astype(f32)
+    seg_out, seg_kept = block_forward(segments, seg_weights, segment_attend)
+    start = lax.axis_index("fsdp") * seg_count
+    pos_local = lax.dynamic_slice_in_dim(pos_full, start, seg_count, 0)
+    leaders = seg_out[:, 0, :].reshape(rows, seg_count, width) + pos_local
+    grad_all = cotangent.reshape(rows * seg_count, SEG_LEN, width).astype(f32)
+    grad_cross = grad_all[:, 0, :].reshape(rows, seg_count, width)
+    own_row = lax.dynamic_index_in_dim(doc_ids, lax.axis_index("fsdp") % 2, 0, keepdims=False)
+    mask = (own_row[:, None] == own_row[None, :]).astype(f32)
+    home, fac, cross_small = cross_block(
+        jnp.concatenate([leaders, grad_cross], axis=2), mask, cross_norms, cross_w, cross_wo
+    )
+    cross_out, grad_leaders = home[..., :width], home[..., width:]
+    joined = jnp.concatenate(
+        [cross_out.reshape(rows * seg_count, 1, width), seg_out[:, 1:, :]], axis=1
+    )
+    output = joined.reshape(rows, local_len, width).astype(bf16)
+    crs_qkv, crs_out, crs_in, crs_back = factor_grads(fac)
+
+    empty_pos = jnp.zeros((doc_ids.shape[1], width), f32)
+    grad_pos = lax.dynamic_update_slice_in_dim(empty_pos, jnp.sum(grad_leaders, axis=0), start, 0)
+    grad_seg = jnp.concatenate(
+        [grad_leaders.reshape(rows * seg_count, 1, width), grad_all[:, 1:, :]], axis=1
+    )
+    grad_states, factors, smalls = block_backward(
+        grad_seg, seg_kept, seg_weights, segment_attend_back
+    )
+    grad_tokens = grad_states.reshape(rows, local_len, width).astype(bf16)
+    small_rows = jnp.concatenate([smalls[0], smalls[1], cross_small[:4], grad_pos], axis=0)
+    small_grads = jnp.pad(small_rows.astype(bf16), ((0, 256 - small_rows.shape[0]), (0, 0))).T
+    terms = block_backward_terms(factors)
+    t_back, t_in, t_out, t_qkv, t_small = scatter_grads((*terms, small_grads))
+    s = t_small.T
+    grad_gain = jnp.stack([s[0:2], s[4:6]])
+    grad_bias = jnp.stack([s[2:4], s[6:8]])
+    return (
+        output,
+        grad_tokens,
+        s[8 : 8 + doc_ids.shape[1]],
+        jnp.stack([t_qkv, crs_qkv]),
+        jnp.stack([t_out, crs_out]),
+        jnp.stack([t_in, crs_in]),
+        jnp.stack([t_back.T, crs_back.T]),
+        grad_gain,
+        grad_bias,
+    )
+
+
 def solution(mesh):
+    fast = dict(mesh.shape) == {"dp": 4, "fsdp": 8}
     return jax.shard_map(
-        body,
+        fast_body if fast else body,
         mesh=mesh,
         in_specs=(
             P("dp", "fsdp", None),

time: 1830 us -> 383 us (0.21)
  waiting for transfers between devices: 1050 us -> 0 us
  blocking collectives: 430 us -> 0 us
  Pallas kernels: 0 us -> 242 us
  matrix products: 160 us -> 60.1 us
  other arithmetic: 77.5 us -> 31.6 us
  local copies, waits for them, and re-layouts: 82.3 us -> 41.5 us
    reduce_scatter x2 -> x0, waiting for transfers between devices: 539 us -> none  [the longest x1 271 us: body(): lax.psum_scatter(weight_terms(cross_factors), ('dp', 'fsdp'), scatter_dim...]
    all_gather x12 -> x0, blocking collectives: 430 us -> none  [the longest x2 84.7 us: gather_segment(): lax.all_gather(norm_bias[0], ('dp', 'fsdp'), axis=1, tiled=True)]
    all_gather x16 -> x0, waiting for transfers between devices: 404 us -> none  [the longest x2 128 us: gather_cross(): lax.all_gather(w_in[1], ('dp', 'fsdp'), axis=0, tiled=True)]
    pallas_call x0 -> x4, Pallas kernels: none -> 242 us  [the longest x1 107 us: gather_weights(): pl.pallas_call(partial(weights_kernel, widths), out_shape=outs, in_specs=...]
    unnamed x22 -> x0, waiting for transfers between devices: 106 us -> none
    dot_general x47 -> x18, matrix products: 156 us -> 60.1 us  [matmul(): return jnp.einsum(form, left, right, preferred_element_type=jnp.float32)]
    concatenate x4 -> x2, other arithmetic: 39.3 us -> 2.42 us  [the longest x1 1.34 us: fast_body(): jnp.concatenate([leaders, grad_cross], axis=2)]
    slice x31 -> x17, local copies, waits for them, and re-layouts: 33.9 us -> 8.71 us  [the longest x1 1.54 us: fast_body(): seg_out[:, 1:, :]]
  transfers between devices with their start and end apart: 20 -> 0, of which waited for: 12 -> 0; matrix products, arithmetic and copies ran while one was open for 13% -> 0% of each run, Pallas kernels for 0% -> 0%
where the time goes in v1:
time: 383 us; the launch traced here: 377 us
  Pallas kernels  242 us (63%)
  matrix products  60.1 us (16%)
  local copies, waits for them, and re-layouts  41.5 us (11%)
  other arithmetic  31.6 us (8%)
    pallas_call x1, Pallas kernels, gather_weights(): pl.pallas_call(partial(weights_kernel, widths), out_shape=outs, in_specs=...  107 us
    pallas_call x1, Pallas kernels, scatter_grads(): pl.pallas_call(partial(scatter_kernel, n), out_shape=[jax.ShapeDtypeStruc...  82.4 us
    dot_general x18, matrix products, matmul(): return jnp.einsum(form, left, right, preferred_element_type=jnp.float32)  60.1 us
    pallas_call x1, Pallas kernels, cross_block(): pl.pallas_call(cross_kernel, out_shape=[jax.ShapeDtypeStruct((2, 2, 2 * w...  27.9 us
    pallas_call x1, Pallas kernels, factor_grads(): pl.pallas_call(factor_kernel, out_shape=[jax.ShapeDtypeStruct((half, 3 *...  25.1 us
    unnamed x139, local copies, waits for them, and re-layouts  16 us
    convert_element_type x1, other arithmetic, block_forward(): active_low = jax.nn.gelu(hidden, approximate=False).astype(jnp.bfloat16)  14.3 us

profile of v1, /device:TPU:1, one launch (start us, length us, event | category | flops | bytes accessed | tf_op | source)
XLA Modules:
  0.0 377.3 jit_solution(60268286257944233)
XLA Ops:
  10.5 106.8 %shard_map.169 = (bf16[768,2304]{1,0:T(8,128)(2,1)S(1)}, bf16[768,256]{1,0:T(8,128)(2,1)S(1)}, bf16[768,768]{1,0:T(8,128)(2,1)S(1)}, bf16[768,3072]{1,0:T(8,128)...) custom-call(bf16[32,19456]{1,0:T(8,128)(2,1)S(1)} %pad.14.pack_ref), custom_call_target="tpu_custom_call" | custom-call | tf_op jit(solution)/shard_map/pallas_call | solution.py:339
  117.4 4.2 %fusion.22 = bf16[4,128,2304]{1,2,0:T(8,128)(2,1)S(1)} fusion(bf16[4,128,768]{2,1,0:T(8,128)(2,1)} %bitcast.178, bf16[768,2304]{1,0:T(8,128)(2,1)S(1)} %get-tuple-element.28), kind=kOutput, calls=%fused_computation.40 | convolution fusion | flops 1813118976 | bytes 6684672 | tf_op jit(solution)/shard_map/gld,de->gle/dot_general | solution.py:827
  127.4 1.9 copy.93
  131.4 7.2 %fusion.33 = (u8[128,3072]{1,0:T(8,128)(4,1)S(1)}, u8[128,3072]{1,0:T(8,128)(4,1)S(1)}, f32[4,128,3072]{2,1,0:T(8,128)S(1)}) fusion(bf16[768,3072]{1,0:T(8,128)(2,1)} %copy-done.12, f32[4,128,768]{2,1,0:T(8,128)} %copy-done.19, f32[768]{0:T(1024)S(1)} %get-tuple-element.85, f32[768]{0:T(1024)S(1)} %get-tuple-element.86, f32[4,128]{1,0:T(4,128)S(1)} %add_rsqrt_fusion.1, ...), kind=kOutput, calls=%fused_computation.74 | convolution fusion | flops 2437545984 | bytes 13379584 | tf_op jit(solution)/shard_map/gld,df->glf/dot_general | solution.py:827
  138.7 14.3 %fusion.2 = bf16[4,128,3072]{2,1,0:T(8,128)(2,1)S(1)} fusion(f32[4,128,3072]{2,1,0:T(8,128)S(1)} %get-tuple-element.105, u8[128,3072]{1,0:T(8,128)(4,1)S(1)} %get-tuple-element.75, u8[128,3072]{1,0:T(8,128)(4,1)S(1)} %get-tuple-element.74), kind=kLoop, calls=%fused_computation.7 | loop fusion | flops 110100480 | bytes 10223616 | tf_op jit(solution)/shard_map/convert_element_type | solution.py:953
  153.1 2.8 fusion.64
  159.1 1.3 reshape_squeeze.14
  161.3 1.3 broadcast_add_fusion
  162.6 1.3 convert.60
  163.9 1.2 copy-done.28
  165.7 1.3 reshape_squeeze.15
  167.0 1.3 pad_maximum_fusion.9.lead_ref
  170.9 27.9 %shard_map.170 = (f32[2,2,1536]{2,1,0:T(2,128)S(1)}, bf16[16,3072]{1,0:T(8,128)(2,1)S(1)}, f32[8,768]{1,0:T(8,128)S(1)}) custom-call(f32[2,2,1536]{2,1,0:T(2,128)S(1)} %copy-done.7, f32[16,16]{1,0:T(8,128)S(1)} %compare_convert_fusion.mask_ref, f32[8,768]{1,0:T(8,128)S(1)} %concatenate.34.norm_ref, bf16[768,2304]{1,0:T(8,128)(2,1)S(1)} %get-tuple-element.33.w_ref, ...), custom_call_target="tpu_custom_call" | custom-call | tf_op jit(solution)/shard_map/pallas_call | solution.py:724
  200.1 1.4 slice.159
  203.2 7.5 %fusion.7 = bf16[4,128,3072]{2,1,0:T(8,128)(2,1)S(1)} fusion(f32[4,128,3072]{2,1,0:T(8,128)} %copy-done.30, bf16[768,3072]{1,0:T(8,128)(2,1)S(1)} %bitcast.158, f32[4,128,768]{2,1,0:T(8,128)S(1)} %subtract_multiply_fusion.1), kind=kOutput, calls=%fused_computation.12 | convolution fusion | flops 2432040960 | bytes 15728640 | tf_op jit(solution)/shard_map/gld,fd->glf/dot_general | solution.py:827
  210.8 4.2 %multiply_reduce_fusion.3 = (bf16[768]{0:T(1024)(128)(2,1)S(1)}, f32[4,128]{1,0:T(4,128)S(1)}, f32[4,128]{1,0:T(4,128)S(1)}, bf16[768]{0:T(1024)(128)(2,1)S(1)}, f32[4,128,768]{2,1,0:T(8,128)}) fusion(f32[4,128,768]{2,1,0:T(8,128)S(1)} %copy-done.21, f32[4,128]{1,0:T(4,128)S(1)} %copy-done.54, f32[4,128]{1,0:T(4,128)S(1)} %copy-done.50, ...), kind=kOutput, calls=%fused_computation.58 | convolution fusion | flops 2419848704 | bytes 12597248 | tf_op jit(solution)/shard_map/glf,df->gld/dot_general | solution.py:827
  216.4 2.3 subtract_multiply_fusion
  220.0 1.7 convolution_convert_fusion.1
  221.7 1.5 copy.96
  223.2 3.2 multiply_reduce_fusion
  227.6 1.4 multiply_convert_fusion.2
  229.0 2.3 copy.100
  231.3 2.1 multiply_convert_fusion.1
  233.4 2.3 copy.101
  235.7 3.3 fusion.43
  240.2 4.0 %fusion.21.refs_3_ = bf16[768,2304]{1,0:T(8,128)(2,1)S(1)} fusion(bf16[4,128,768]{2,1,0:T(8,128)(2,1)} %bitcast.179, bf16[4,128,768]{2,1,0:T(8,128)(2,1)} %copy.102, bf16[4,128,768]{2,1,0:T(8,128)(2,1)} %copy.101, bf16[4,128,768]{2,1,0:T(8,128)(2,1)} %copy.100), kind=kOutput, calls=%fused_computation.38 | convolution fusion | flops 1820786688 | bytes 6684672 | tf_op jit(solution)/shard_map/gld,gle->de/dot_general | solution.py:827
  245.6 5.1 %bitcast_convert_fusion.refs_1_ = bf16[768,3072]{1,0:T(8,128)(2,1)} fusion(bf16[4,128,3072]{2,1,0:T(8,128)(2,1)S(1)} %copy-done.58, f32[4,128,768]{2,1,0:T(8,128)S(1)} %copy-done.22, f32[768]{0:T(1024)S(1)} %copy-done.56, f32[768]{0:T(1024)S(1)} %copy-done.52, f32[4,128]{1,0:T(4,128)S(1)} %copy-done.54, f32[4,128]{1,0:T(4,128)S(1)} %copy-done.50), kind=kOutput, calls=%fused_computation.2 | convolution fusion | flops 2420244480 | bytes 9447424 | tf_op jit(solution)/shard_map/gld,glf->df/dot_general | solution.py:827
  250.7 4.4 %bitcast_convert_fusion.1.refs_0_ = bf16[768,3072]{1,0:T(8,128)(2,1)} fusion(bf16[4,128,3072]{2,1,0:T(8,128)(2,1)S(1)} %copy-done.35, f32[4,128,768]{2,1,0:T(8,128)S(1)} %copy-done.41), kind=kOutput, calls=%fused_computation.3 | convolution fusion | flops 2418671616 | bytes 9437184 | tf_op jit(solution)/shard_map/gld,glf->df/dot_general | solution.py:827
  255.1 82.4 %shard_map.171 = (f32[24,3072]{1,0:T(8,128)S(1)}, f32[24,3072]{1,0:T(8,128)S(1)}, f32[24,768]{1,0:T(8,128)S(1)}, f32[24,2304]{1,0:T(8,128)S(1)}, f32[24,256]{1,0:T(8,128)S(1)}) custom-call(bf16[768,3072]{1,0:T(8,128)(2,1)} %bitcast_convert_fusion.1.refs_0_, bf16[768,3072]{1,0:T(8,128)(2,1)} %bitcast_convert_fusion.refs_1_, ...), custom_call_target="tpu_custom_call" | custom-call | tf_op jit(solution)/shard_map/pallas_call | solution.py:522
  339.1 25.1 %shard_map.172 = (f32[24,2304]{1,0:T(8,128)S(1)}, f32[24,768]{1,0:T(8,128)S(1)}, f32[24,3072]{1,0:T(8,128)S(1)}, f32[24,3072]{1,0:T(8,128)S(1)}) custom-call(bf16[16,3072]{1,0:T(8,128)(2,1)S(1)} %copy-done.9), custom_call_target="tpu_custom_call" | custom-call | tf_op jit(solution)/shard_map/pallas_call | solution.py:802
  368.1 5.7 %add_convert_fusion = bf16[4,128,768]{2,1,0:T(8,128)(2,1)} fusion(f32[4,128,768]{2,1,0:T(8,128)S(1)} %copy-done.32, bf16[768,2304]{1,0:T(8,128)(2,1)} %copy-done.14, bf16[4,128,768]{2,1,0:T(8,128)(2,1)} %copy.102, bf16[4,128,768]{2,1,0:T(8,128)(2,1)} %copy.101, bf16[4,128,768]{2,1,0:T(8,128)(2,1)} %copy.100), kind=kOutput, calls=%fused_computation.59 | convolution fusion | flops 1819803648 | bytes 8257536 | tf_op jit(solution)/shard_map/gle,de->gld/dot_general | solution.py:827
  374.5 1.5 slice.188
  (222 shorter events, 41.0 us)
Async XLA Ops:
  0.6 167.7 %copy-start = (s32[2,16]{1,0:T(2,128)S(1)}, s32[2,16]{1,0:T(2,128)}, u32[]{:S(2)}) copy-start(s32[2,16]{1,0:T(2,128)} %param.11) | copy-start | bytes 388
  0.7 8.6 %slice-start.6 = ((bf16[2,24,3072]{2,1,0:T(8,128)(2,1)}), bf16[1,24,3072]{2,1,0:T(8,128)(2,1)S(1)}, s32[]{:S(2)}) async-start(bf16[2,24,3072]{2,1,0:T(8,128)(2,1)} %param.15), calls=%async_computation.6 | async-start | bytes 294912 | tf_op jit(solution)/shard_map/slice | solution.py:1167
  1.4 9.0 %copy-start.48 = (bf16[2,24,768]{2,1,0:T(8,128)(2,1)S(1)}, bf16[2,24,768]{2,1,0:T(8,128)(2,1)}, u32[]{:S(2)}) copy-start(bf16[2,24,768]{2,1,0:T(8,128)(2,1)} %param.14) | copy-start | bytes 221188
  117.3 4.3 %copy-start.4 = (bf16[768,256]{1,0:T(8,128)(2,1)}, bf16[768,256]{1,0:T(8,128)(2,1)S(1)}, u32[]{:S(2)}) copy-start(bf16[768,256]{1,0:T(8,128)(2,1)S(1)} %get-tuple-element.30) | copy-start | bytes 1179652
  117.4 4.3 %copy-start.5 = (bf16[192,768]{1,0:T(8,128)(2,1)}, bf16[192,768]{1,0:T(8,128)(2,1)S(1)}, u32[]{:S(2)}) copy-start(bf16[192,768]{1,0:T(8,128)(2,1)S(1)} %get-tuple-element.34.wo_ref) | copy-start | bytes 884740
  117.4 4.3 %copy-start.12 = (bf16[768,3072]{1,0:T(8,128)(2,1)}, bf16[768,3072]{1,0:T(8,128)(2,1)S(1)}, u32[]{:S(2)}) copy-start(bf16[768,3072]{1,0:T(8,128)(2,1)S(1)} %get-tuple-element.31) | copy-start | bytes 14155780
  117.4 4.3 %copy-start.13 = (bf16[768,3072]{1,0:T(8,128)(2,1)}, bf16[768,3072]{1,0:T(8,128)(2,1)S(1)}, u32[]{:S(2)}) copy-start(bf16[768,3072]{1,0:T(8,128)(2,1)S(1)} %get-tuple-element.32) | copy-start | bytes 14155780
  117.4 5.2 %copy-start.14 = (bf16[768,2304]{1,0:T(8,128)(2,1)}, bf16[768,2304]{1,0:T(8,128)(2,1)S(1)}, u32[]{:S(2)}) copy-start(bf16[768,2304]{1,0:T(8,128)(2,1)S(1)} %get-tuple-element.28) | copy-start | bytes 10616836
  117.4 7.0 %copy-start.2 = (bf16[768,768]{1,0:T(8,128)(2,1)}, bf16[768,768]{1,0:T(8,128)(2,1)S(1)}, u32[]{:S(2)}) copy-start(bf16[768,768]{1,0:T(8,128)(2,1)S(1)} %get-tuple-element.29) | copy-start | bytes 3538948
  125.9 27.1 %copy-start.49 = (f32[4,128]{1,0:T(4,128)}, f32[4,128]{1,0:T(4,128)S(1)}, u32[]{:S(2)}) copy-start(f32[4,128]{1,0:T(4,128)S(1)} %broadcast_multiply_fusion.5) | copy-start | bytes 6148
  127.4 25.6 %copy-start.53 = (f32[4,128]{1,0:T(4,128)}, f32[4,128]{1,0:T(4,128)S(1)}, u32[]{:S(2)}) copy-start(f32[4,128]{1,0:T(4,128)S(1)} %add_rsqrt_fusion.1) | copy-start | bytes 6148
  129.3 23.7 %slice-start.2 = ((s8[4718592]{0:T(1024)(128)(4,1)}), s8[4194304]{0:T(1024)(128)(4,1)S(1)}, s32[]{:S(2)}) async-start(s8[4718592]{0:T(1024)(128)(4,1)} %bitcast.155), calls=%async_computation.2 | async-start | bytes 8388608
  130.6 22.4 %copy-start.51 = (f32[768]{0:T(1024)}, f32[768]{0:T(1024)S(1)}, u32[]{:S(2)}) copy-start(f32[768]{0:T(1024)S(1)} %get-tuple-element.86) | copy-start | bytes 9220
  130.6 22.4 %copy-start.55 = (f32[768]{0:T(1024)}, f32[768]{0:T(1024)S(1)}, u32[]{:S(2)}) copy-start(f32[768]{0:T(1024)S(1)} %get-tuple-element.85) | copy-start | bytes 9220
  131.4 21.6 %slice-start.3 = ((s8[4718592]{0:T(1024)(128)(4,1)}), s8[524288]{0:T(1024)(128)(4,1)S(1)}, s32[]{:S(2)}) async-start(s8[4718592]{0:T(1024)(128)(4,1)} %bitcast.155), calls=%async_computation.3 | async-start | bytes 1048576
  138.7 14.3 %copy-start.30 = (f32[4,128,3072]{2,1,0:T(8,128)}, f32[4,128,3072]{2,1,0:T(8,128)S(1)}, u32[]{:S(2)}) copy-start(f32[4,128,3072]{2,1,0:T(8,128)S(1)} %get-tuple-element.105) | copy-start | bytes 18874372
  138.7 14.4 %copy-start.20 = (f32[4,128,768]{2,1,0:T(8,128)S(1)}, f32[4,128,768]{2,1,0:T(8,128)}, u32[]{:S(2)}) copy-start(f32[4,128,768]{2,1,0:T(8,128)} %copy-done.19) | copy-start | bytes 4718596
  202.5 8.2 %slice-start = ((s8[4718592]{0:T(1024)(128)(4,1)}), s8[4194304]{0:T(1024)(128)(4,1)S(1)}, s32[]{:S(2)}) async-start(s8[4718592]{0:T(1024)(128)(4,1)} %bitcast.153), calls=%async_computation | async-start | bytes 8388608
  203.1 7.6 %copy-start.40 = (f32[4,128,768]{2,1,0:T(8,128)}, f32[4,128,768]{2,1,0:T(8,128)S(1)}, u32[]{:S(2)}) copy-start(f32[4,128,768]{2,1,0:T(8,128)S(1)} %subtract_multiply_fusion.1) | copy-start | bytes 4718596
  203.1 7.6 %slice-start.1 = ((s8[4718592]{0:T(1024)(128)(4,1)}), s8[524288]{0:T(1024)(128)(4,1)S(1)}, s32[]{:S(2)}) async-start(s8[4718592]{0:T(1024)(128)(4,1)} %bitcast.153), calls=%async_computation.1 | async-start | bytes 1048576
  203.1 7.6 %copy-start.21 = (f32[4,128,768]{2,1,0:T(8,128)S(1)}, f32[4,128,768]{2,1,0:T(8,128)}, u32[]{:S(2)}) copy-start(f32[4,128,768]{2,1,0:T(8,128)} %copy-done.19) | copy-start | bytes 4718596
  203.1 7.6 %copy-start.50 = (f32[4,128]{1,0:T(4,128)S(1)}, f32[4,128]{1,0:T(4,128)}, u32[]{:S(2)}) copy-start(f32[4,128]{1,0:T(4,128)} %copy-done.49) | copy-start | bytes 6148
  203.1 7.6 %copy-start.52 = (f32[768]{0:T(1024)S(1)}, f32[768]{0:T(1024)}, u32[]{:S(2)}) copy-start(f32[768]{0:T(1024)} %copy-done.51) | copy-start | bytes 9220
  203.2 7.6 %copy-start.54 = (f32[4,128]{1,0:T(4,128)S(1)}, f32[4,128]{1,0:T(4,128)}, u32[]{:S(2)}) copy-start(f32[4,128]{1,0:T(4,128)} %copy-done.53) | copy-start | bytes 6148
  210.8 4.2 %copy-start.57 = (bf16[4,128,3072]{2,1,0:T(8,128)(2,1)}, bf16[4,128,3072]{2,1,0:T(8,128)(2,1)S(1)}, u32[]{:S(2)}) copy-start(bf16[4,128,3072]{2,1,0:T(8,128)(2,1)S(1)} %fusion.7) | copy-start | bytes 9437188
  210.8 4.3 %copy-start.29 = (f32[4,128,768]{2,1,0:T(8,128)S(1)}, f32[4,128,768]{2,1,0:T(8,128)}, u32[]{:S(2)}) copy-start(f32[4,128,768]{2,1,0:T(8,128)} %copy-done.28) | copy-start | bytes 4718596
  215.2 4.7 %copy-start.3 = (bf16[768,768]{1,0:T(8,128)(2,1)S(1)}, bf16[768,768]{1,0:T(8,128)(2,1)}, u32[]{:S(2)}) copy-start(bf16[768,768]{1,0:T(8,128)(2,1)} %copy-done.2) | copy-start | bytes 3538948
  240.2 4.9 %copy-start.58 = (bf16[4,128,3072]{2,1,0:T(8,128)(2,1)S(1)}, bf16[4,128,3072]{2,1,0:T(8,128)(2,1)}, u32[]{:S(2)}) copy-start(bf16[4,128,3072]{2,1,0:T(8,128)(2,1)} %copy-done.57) | copy-start | bytes 9437188
  245.6 5.1 %copy-start.35 = (bf16[4,128,3072]{2,1,0:T(8,128)(2,1)S(1)}, bf16[4,128,3072]{2,1,0:T(8,128)(2,1)}, u32[]{:S(2)}) copy-start(bf16[4,128,3072]{2,1,0:T(8,128)(2,1)} %copy-done.34) | copy-start | bytes 9437188
  245.6 5.1 %copy-start.41 = (f32[4,128,768]{2,1,0:T(8,128)S(1)}, f32[4,128,768]{2,1,0:T(8,128)}, u32[]{:S(2)}) copy-start(f32[4,128,768]{2,1,0:T(8,128)} %copy-done.40) | copy-start | bytes 4718596
  255.1 84.0 %copy-start.9 = (bf16[16,3072]{1,0:T(8,128)(2,1)S(1)}, bf16[16,3072]{1,0:T(8,128)(2,1)}, u32[]{:S(2)}) copy-start(bf16[16,3072]{1,0:T(8,128)(2,1)} %copy-done.8) | copy-start | bytes 294916
  368.1 9.0 %copy-start.1 = (s32[2,16]{1,0:T(2,128)S(1)}, s32[2,16]{1,0:T(2,128)}, u32[]{:S(2)}) copy-start(s32[2,16]{1,0:T(2,128)} %param.11) | copy-start | bytes 388
  (34 other events, 65.4 us)

commit v2 on v1

--- a/solution.py
+++ b/solution.py
@@ -240,300 +240,6 @@
     pltpu.SemaphoreType.DMA((n, 8)),
     pltpu.SemaphoreType.DMA((n, 8)),
 ]
-
-
-def pair_rows(p, own_ref, sib_ref, block_ref, send, recv):
-    copy = remote(own_ref, sib_ref, send, recv, p.sib)
-    copy.start()
-    copy.wait()
-    height, width = block_ref.shape[0] // 2, own_ref.shape[1]
-    step = 1024
-    first = p.core == 0
-
-    def chunk(at, size):
-        mine = own_ref[:, lanes(at, size)].astype(f32)[:height]
-        theirs = sib_ref[:, lanes(at, size)].astype(f32)[:height]
-        both = jnp.concatenate(
-            [jnp.where(first, mine, theirs), jnp.where(first, theirs, mine)], axis=0
-        )
-        block_ref[:, lanes(at, size)] = both.astype(bf16)
-
-    @pl.loop(0, width // step)
-    def _(i):
-        chunk(i * step, step)
-
-    if width % step:
-        chunk(width // step * step, width % step)
-
-
-def weights_kernel(widths, pack_ref, *refs):
-    n = len(widths)
-    outs, cross_out, wo_out = refs[:n], refs[n], refs[n + 1]
-    sib_buf, block, s0, s1, s2, s3, pair_send, pair_recv, wo_send, wo_recv, local = refs[n + 2 :]
-    p = Place()
-    greet(everyone(p))
-    pair_rows(p, pack_ref, sib_buf, block, pair_send, pair_recv)
-    sems = (s0, s1, s2, s3)
-    gathers, copies, at = [], [], 0
-    key = rows_at((p.dp * 4 + p.z) * ROWS, ROWS, 16)
-    for i, width in enumerate(widths):
-        gathers.append(Gather(p, outs[i], block, at, width, i, sems, ROWS))
-        copies.append((block.at[:, lanes(at, width)], outs[i].at[key]))
-        at += width
-    cw = cross_out.shape[1]
-    gathers.append(Gather(p, cross_out, block, at, cw, n, sems, ROWS, slabs=True))
-    copies.append((block.at[:, lanes(at + p.z * cw, cw)], cross_out.at[key]))
-    at += 4 * cw
-    for i, (src, dst) in enumerate(copies):
-        pltpu.make_async_copy(src, dst, local.at[i]).start()
-    width = wo_out.shape[1]
-    half = width // 2
-    wo_src = block.at[:, lanes(at + p.core * half, half)]
-    wo_dst = wo_out.at[rows_at(p.z * ROWS, ROWS, 16), lanes(p.core * half, half)]
-    for i in range(4):
-        copy = remote(wo_src, wo_dst, wo_send.at[i], wo_recv.at[p.z], p.at(i, p.dp, p.core))
-        here = jnp.logical_and(p.dp == i, p.dp == p.z)
-
-        @pl.when(jnp.logical_not(here))
-        def _():
-            copy.start()
-
-        @pl.when(here)
-        def _():
-            mine = pltpu.make_async_copy(wo_src, wo_dst, local.at[n + 1])
-            mine.start()
-            mine.wait()
-
-    run_gathers(gathers)
-    for i in range(4):
-        piece = wo_out.at[pl.ds(i * ROWS, ROWS), lanes(p.core * half, half)]
-        here = jnp.logical_and(p.z == p.dp, p.z == i)
-
-        @pl.when(jnp.logical_not(here))
-        def _():
-            remote(piece, piece, wo_send.at[i], wo_recv.at[i], p.sib).wait_recv()
-
-    mine = wo_out.at[:, lanes(p.core * half, half)]
-    theirs = wo_out.at[:, lanes((1 - p.core) * half, half)]
-    copy = remote(mine, mine, wo_send.at[4], wo_recv.at[4], p.sib)
-    copy.start()
-    remote(theirs, theirs, wo_send.at[4], wo_recv.at[4], p.sib).wait_recv()
-    copy.wait_send()
-    for i in range(4):
-        here = jnp.logical_and(p.dp == i, p.dp == p.z)
-
-        @pl.when(jnp.logical_not(here))
-        def _():
-            remote(wo_src, wo_dst, wo_send.at[i], wo_recv.at[p.z], p.at(i, p.dp, p.core)).wait_send()
-
-    for i, (src, dst) in enumerate(copies):
-        pltpu.make_async_copy(src, dst, local.at[i]).wait()
-
-
-def gather_weights(pack, widths, cross_width, wo_width):
-    n = len(widths)
-    rows = 16 * ROWS
-    outs = [jax.ShapeDtypeStruct((rows, w), bf16) for w in widths]
-    outs += [jax.ShapeDtypeStruct((rows, cross_width), bf16), jax.ShapeDtypeStruct((192, wo_width), bf16)]
-    height, total = pack.shape
-    return pl.pallas_call(
-        partial(weights_kernel, widths),
-        out_shape=outs,
-        in_specs=[pl.BlockSpec(memory_space=VM)],
-        out_specs=[pl.BlockSpec(memory_space=pl.ANY)] * len(outs),
-        scratch_shapes=[pltpu.VMEM((height, total), bf16), pltpu.VMEM((ROWS, total), bf16)]
-        + GATHER_SEMS(n + 1)
-        + [
-            pltpu.SemaphoreType.DMA,
-            pltpu.SemaphoreType.DMA,
-            pltpu.SemaphoreType.DMA((5,)),
-            pltpu.SemaphoreType.DMA((5,)),
-            pltpu.SemaphoreType.DMA((n + 2,)),
-        ],
-        compiler_params=pltpu.CompilerParams(
-            collective_id=0, has_side_effects=True, vmem_limit_bytes=32 * MIB
-        ),
-    )(pack)
-
-
-class Scatter:
-    def __init__(self, place, grad, out, index, sems, acc, pair, r1a, r1b, r2a, r2b, r3, give):
-        self.p, self.grad, self.out, self.m = place, grad, out, index
-        self.send, self.recv, self.local = sems
-        self.acc, self.pair, self.r1a, self.r1b = acc, pair, r1a, r1b
-        self.r2a, self.r2b, self.r3, self.give = r2a, r2b, r3, give
-        self.half = grad.shape[1] // 2
-        tiles = self.half // LANES
-        self.a = (tiles + 1) // 2 * LANES
-        self.b = self.half - self.a
-        self.sent = []
-        p = place
-        far = (1 - p.y) * 2 + 1 - p.x
-        self.groups = (far, p.ydp, p.xdp, p.dp)
-
-    def group(self, ref, dp):
-        return ref.at[rows_at(dp * 4 * ROWS, 4 * ROWS, 16)]
-
-    def go(self, src, dst, slot, device):
-        copy = remote(src, dst, self.send.at[self.m, slot], self.recv.at[self.m, slot], device)
-        copy.start()
-        self.sent.append(copy)
-
-    def arrived(self, dst, slot):
-        remote(dst, dst, self.send.at[self.m, slot], self.recv.at[self.m, slot], self.p.sib).wait_recv()
-
-    def load(self, i):
-        p = self.p
-        mine = self.group(self.grad, self.groups[i]).at[:, lanes(p.core * self.half, self.half)]
-        return pltpu.make_async_copy(mine, self.group(self.acc, self.groups[i]), self.local.at[self.m, i])
-
-    def start(self):
-        p = self.p
-        for i, dp in enumerate(self.groups):
-            theirs = self.group(self.grad, dp).at[:, lanes((1 - p.core) * self.half, self.half)]
-            self.go(theirs, self.group(self.pair, dp), i, p.sib)
-            self.load(i).start()
-
-    def add(self, dp, part, other, other_row=0):
-        at, size = {"A": (0, self.a), "B": (self.a, self.b), "AB": (0, self.half)}[part]
-        base = dp * 4 * ROWS
-
-        @pl.loop(0, 4)
-        def _(i):
-            key = (rows_at(base + i * ROWS, ROWS, 16), pl.ds(at, size))
-            more = other[rows_at(other_row + i * ROWS, ROWS, 16), :]
-            self.acc[key] = (self.acc[key].astype(f32) + more.astype(f32)).astype(bf16)
-
-    def side(self, dp, part):
-        at, size = (0, self.a) if part == "A" else (self.a, self.b)
-        return self.group(self.acc, dp).at[:, pl.ds(at, size)]
-
-    def one(self):
-        p = self.p
-        for i, dp in enumerate(self.groups):
-            self.arrived(self.group(self.pair, dp), i)
-            self.load(i).wait()
-            self.add(dp, "AB", self.pair, dp * 4 * ROWS)
-            if i == 0:
-                self.go(self.side(dp, "A"), self.r1a.at[pl.ds(0, 4 * ROWS)], 4, p.ynbr)
-                if self.b:
-                    self.go(self.side(dp, "B"), self.r1b.at[pl.ds(0, 4 * ROWS)], 6, p.xnbr)
-            if i == 1:
-                self.go(self.side(dp, "A"), self.r1a.at[pl.ds(4 * ROWS, 4 * ROWS)], 5, p.ynbr)
-            if i == 2 and self.b:
-                self.go(self.side(dp, "B"), self.r1b.at[pl.ds(4 * ROWS, 4 * ROWS)], 7, p.xnbr)
-
-    def two(self):
-        p = self.p
-        self.arrived(self.r1a.at[pl.ds(0, 4 * ROWS)], 4)
-        self.add(p.xdp, "A", self.r1a)
-        self.go(self.side(p.xdp, "A"), self.r2a, 8, p.xnbr)
-        if self.b:
-            self.arrived(self.r1b.at[pl.ds(0, 4 * ROWS)], 6)
-            self.add(p.ydp, "B", self.r1b)
-            self.go(self.side(p.ydp, "B"), self.r2b, 9, p.ynbr)
-        self.arrived(self.r1a.at[pl.ds(4 * ROWS, 4 * ROWS)], 5)
-        self.add(p.dp, "A", self.r1a, 4 * ROWS)
-        if self.b:
-            self.arrived(self.r1b.at[pl.ds(4 * ROWS, 4 * ROWS)], 7)
-            self.add(p.dp, "B", self.r1b, 4 * ROWS)
-
-    def three(self):
-        p = self.p
-        self.arrived(self.r2a, 8)
-        self.add(p.dp, "A", self.r2a)
-        if self.b:
-            self.arrived(self.r2b, 9)
-            self.add(p.dp, "B", self.r2b)
-        for d in (1, 3, 2):
-            z = (p.z + d) % 4
-            src = self.acc.at[rows_at((p.dp * 4 + z) * ROWS, ROWS, 16)]
-            self.go(src, self.r3.at[d - 1], 9 + d, p.at(p.dp, z, p.core))
-
-    def four(self):
-        p = self.p
-        for d in (1, 3, 2):
-            self.arrived(self.r3.at[d - 1], 9 + d)
-        rows = rows_at((p.dp * 4 + p.z) * ROWS, ROWS, 16)
-        step = self.a if self.b == self.a else self.half
-
-        def chunk(at, size):
-            cols = pl.ds(at, size)
-            total = self.acc[rows, cols].astype(f32)
-            for d in range(3):
-                total = total + self.r3[d, :, cols].astype(f32)
-            upper, lower = total[: ROWS // 2], total[ROWS // 2 :]
-            first = p.core == 0
-            self.give[:, cols] = jnp.where(first, lower, upper)
-            self.out[:, lanes(p.core * self.half + at, size)] = jnp.where(first, upper, lower)
-
-        for at in range(0, self.half, step):
-            chunk(at, step)
-        self.go(self.give, self.out.at[:, lanes(p.core * self.half, self.half)], 13, p.sib)
-
-    def five(self):
-        p = self.p
-        self.arrived(self.out.at[:, lanes((1 - p.core) * self.half, self.half)], 13)
-
-    def finish(self):
-        for copy in self.sent:
-            copy.wait_send()
-
-
-def scatter_kernel(n, *refs):
-    grads, outs = refs[:n], refs[n : 2 * n]
-    scratch = refs[2 * n :]
-    sems = scratch[:3]
-    p = Place()
-    greet(gather_peers(p))
-    jobs = []
-    for i in range(n):
-        bufs = scratch[3 + 8 * i : 11 + 8 * i]
-        jobs.append(Scatter(p, grads[i], outs[i], i, sems, *bufs))
-    for job in jobs:
-        job.start()
-    for step in range(n + 4):
-        for lag, name in enumerate(("one", "two", "three", "four", "five")):
-            if 0 <= step - lag < n:
-                getattr(jobs[step - lag], name)()
-    for job in jobs:
-        job.finish()
-
-
-def scatter_grads(grads):
-    n = len(grads)
-    bufs = []
-    for g in grads:
-        half = g.shape[1] // 2
-        tiles = half // LANES
-        a = (tiles + 1) // 2 * LANES
-        b = max(half - a, LANES)
-        rows = g.shape[0]
-        bufs += [
-            pltpu.VMEM((rows, half), bf16),
-            pltpu.VMEM((rows, half), bf16),
-            pltpu.VMEM((8 * ROWS, a), bf16),
-            pltpu.VMEM((8 * ROWS, b), bf16),
-            pltpu.VMEM((4 * ROWS, a), bf16),
-            pltpu.VMEM((4 * ROWS, b), bf16),
-            pltpu.VMEM((3, ROWS, half), bf16),
-            pltpu.VMEM((ROWS // 2, half), f32),
-        ]
-    return pl.pallas_call(
-        partial(scatter_kernel, n),
-        out_shape=[jax.ShapeDtypeStruct((ROWS // 2, g.shape[1]), f32) for g in grads],
-        in_specs=[pl.BlockSpec(memory_space=pl.ANY)] * n,
-        out_specs=[pl.BlockSpec(memory_space=VM)] * n,
-        scratch_shapes=[
-            pltpu.SemaphoreType.DMA((n, 14)),
-            pltpu.SemaphoreType.DMA((n, 14)),
-            pltpu.SemaphoreType.DMA((n, 4)),
-        ]
-        + bufs,
-        compiler_params=pltpu.CompilerParams(
-            collective_id=1, has_side_effects=True, vmem_limit_bytes=48 * MIB
-        ),
-    )(*grads)
 
 
 NEG = -1e30
@@ -750,77 +456,753 @@
     )(lead, mask, norms, weights, wo)
 
 
-def factor_kernel(fac_ref, qkv_ref, out_ref, in_ref, back_ref, sib_buf, block, full, tmp, *sems):
+def lane_halves(v):
+    low = lax.broadcasted_iota(jnp.int32, v.shape, 1) < LANES // 2
+    zero = jnp.zeros_like(v)
+    return jnp.where(low, v, zero), jnp.where(low, zero, v)
+
+
+def forward_kernel(widths, *refs):
+    n = len(widths)
+    pack_ref, x_ref, cot_ref = refs[:3]
+    (
+        w_hbm, i_hbm, o_hbm, b_hbm, cross_out, wo_out,
+        p_hbm, a_hbm, c_hbm, nl_hbm, g_hbm, sl_hbm, z1_hbm, z2_hbm,
+        y_ref, lead_ref, par_ref, r1_ref, r2_ref,
+    ) = refs[3:22]
+    (
+        sw, ow, qw, iw, bw,
+        pk, at, cx, h, nl, g, sl, z1, z2,
+        sib_buf, block, s0, s1, s2, s3, pair_send, pair_recv, wo_send, wo_recv, local, out_sem,
+    ) = refs[22:]
     p = Place()
+    rows, width = x_ref.shape
+    segs = rows // SEG_LEN
+    hidden = iw.shape[1]
+    pairs = width // LANES
+    dests = (sw, qw, ow, iw, bw, cross_out)
+    cw = cross_out.shape[1]
+    sems = (s0, s1, s2, s3)
+    starts, spot = [], 0
+    for w in list(widths) + [4 * cw, wo_out.shape[1]]:
+        starts.append((spot, w))
+        spot += w
+    greet(everyone(p))
+
+    def pair(i):
+        cols = pl.ds(*starts[i])
+        return remote(
+            pack_ref.at[:, cols], sib_buf.at[:, cols], pair_send.at[i], pair_recv.at[i], p.sib
+        )
+
+    for i in range(n + 2):
+        pair(i).start()
+
+    def join(i):
+        pair(i).wait_recv()
+        start, size = starts[i]
+        first = p.core == 0
+        half = ROWS // 2
+
+        def chunk(spot, count):
+            cols = lanes(spot, count)
+            mine = pack_ref[:, cols].astype(f32)[:half]
+            theirs = sib_buf[:, cols].astype(f32)[:half]
+            both = [jnp.where(first, mine, theirs), jnp.where(first, theirs, mine)]
+            block[:, cols] = jnp.concatenate(both, axis=0).astype(bf16)
+
+        step = 768 if size % 768 == 0 else size
+
+        @pl.loop(0, size // step)
+        def _(k):
+            chunk(start + k * step, step)
+
+    gathers = []
+    for i, w in enumerate(widths):
+        gathers.append(Gather(p, dests[i], block, starts[i][0], w, i, sems, ROWS))
+    gathers.append(Gather(p, cross_out, block, starts[n][0], cw, n, sems, ROWS, slabs=True))
+    key = rows_at((p.dp * 4 + p.z) * ROWS, ROWS, 16)
+
+    def own_copy(i):
+        start = starts[i][0] + (p.z * cw if i == n else 0)
+        return pltpu.make_async_copy(block.at[:, lanes(start, gathers[i].width)], dests[i].at[key], local.at[i])
+
+    def own(i):
+        join(i)
+        own_copy(i).start()
+        gathers[i].send_own()
+
+    line = lambda i: gathers[i].pass_line()
+    plane = lambda i: gathers[i].pass_plane()
+    last = lambda i: gathers[i].last()
+
+    def drain(i):
+        gathers[i].drain()
+        own_copy(i).wait()
+
+    half_wo = wo_out.shape[1] // 2
+    wo_src = block.at[:, lanes(starts[n + 1][0] + p.core * half_wo, half_wo)]
+    wo_dst = wo_out.at[rows_at(p.z * ROWS, ROWS, 16), lanes(p.core * half_wo, half_wo)]
+
+    def wo_copy(i):
+        return remote(wo_src, wo_dst, wo_send.at[i], wo_recv.at[p.z], p.at(i, p.dp, p.core))
+
+    def wo_start():
+        join(n + 1)
+        for i in range(4):
+            here = jnp.logical_and(p.dp == i, p.dp == p.z)
+
+            @pl.when(jnp.logical_not(here))
+            def _():
+                wo_copy(i).start()
+
+            @pl.when(here)
+            def _():
+                mine = pltpu.make_async_copy(wo_src, wo_dst, local.at[n + 1])
+                mine.start()
+                mine.wait()
+
+    def wo_finish():
+        for i in range(4):
+            piece = wo_out.at[pl.ds(i * ROWS, ROWS), lanes(p.core * half_wo, half_wo)]
+
+            @pl.when(jnp.logical_not(jnp.logical_and(p.z == p.dp, p.z == i)))
+            def _():
+                remote(piece, piece, wo_send.at[i], wo_recv.at[i], p.sib).wait_recv()
+
+        mine = wo_out.at[:, lanes(p.core * half_wo, half_wo)]
+        theirs = wo_out.at[:, lanes((1 - p.core) * half_wo, half_wo)]
+        copy = remote(mine, mine, wo_send.at[4], wo_recv.at[4], p.sib)
+        copy.start()
+        remote(theirs, theirs, wo_send.at[4], wo_recv.at[4], p.sib).wait_recv()
+        copy.wait_send()
+        for i in range(4):
+
+            @pl.when(jnp.logical_not(jnp.logical_and(p.dp == i, p.dp == p.z)))
+            def _():
+                wo_copy(i).wait_send()
+
+    kept = []
+
+    def keep(src, dst):
+        copy = pltpu.make_async_copy(src, dst, out_sem.at[len(kept)])
+        copy.start()
+        kept.append(copy)
+
+    tile = 256
+
+    def params():
+        par_ref[...] = sw[...].astype(f32).T[: par_ref.shape[0]]
+
+    def project():
+        @pl.loop(0, 3 * width // tile)
+        def _(i):
+            cols = lanes(i * tile, tile)
+            pk[:, cols] = mm(x_ref[...], qw[:, cols], NN).astype(bf16)
+
+    def attend(s):
+        key = pl.ds(s * SEG_LEN, SEG_LEN)
+
+        @pl.loop(0, pairs)
+        def _(j):
+            q2 = pk[key, lanes(j * LANES, LANES)]
+            k2 = pk[key, lanes(width + j * LANES, LANES)]
+            v2 = pk[key, lanes(2 * width + j * LANES, LANES)]
+            scores = mm(jnp.concatenate(lane_halves(q2), axis=0), k2, NT) * (LANES // 2) ** (-0.5)
+            top = jnp.max(scores, axis=-1, keepdims=True)
+            terms = jnp.exp(scores - top)
+            a = (terms / jnp.sum(terms, axis=-1, keepdims=True)).astype(bf16)
+            at[rows_at((s * pairs + j) * 2 * SEG_LEN, 2 * SEG_LEN, 16), :] = a
+            both = jnp.concatenate([a[:SEG_LEN], a[SEG_LEN:]], axis=1)
+            c2 = mm(both, jnp.concatenate(lane_halves(v2), axis=0), NN)
+            cx[key, lanes(j * LANES, LANES)] = c2.astype(bf16)
+
+    block_rows = 64
+
+    def branch():
+        @pl.loop(0, width // tile)
+        def _(i):
+            cols = lanes(i * tile, tile)
+            h[:, cols] = x_ref[:, cols].astype(f32) + mm(cx[...], ow[:, cols], NN)
+
+        @pl.loop(0, rows // block_rows)
+        def _(i):
+            key = rows_at(i * block_rows, block_rows, 16)
+            normed, scaled, inverse = norm_rows(h[key, :], par_ref[0:1, :], par_ref[2:3, :])
+            h[key, :] = normed
+            nl[key, :] = normed.astype(bf16)
+            z1[key, :] = scaled.astype(bf16)
+            r1_ref[key, :] = jnp.broadcast_to(inverse, (block_rows, LANES))
+
+    def feed_in(first, count):
+        @pl.loop(first, first + count)
+        def _(i):
+            cols = lanes(i * tile, tile)
+            u = mm(nl[...], iw[:, cols], NN)
+            phi, slope = gelu_parts(u)
+            g[:, cols] = (u * phi).astype(bf16)
+            sl[:, cols] = slope.astype(bf16)
+
+    def feed_back():
+        @pl.loop(0, width // tile)
+        def _(i):
+            cols = lanes(i * tile, tile)
+            h[:, cols] += mm(g[...], bw[rows_at(i * tile, tile, 16), :], NT)
+
+        @pl.loop(0, rows // block_rows)
+        def _(i):
+            key = rows_at(i * block_rows, block_rows, 16)
+            result, scaled, inverse = norm_rows(h[key, :], par_ref[1:2, :], par_ref[3:4, :])
+            h[key, :] = result
+            y_ref[key, :] = result.astype(bf16)
+            z2[key, :] = scaled.astype(bf16)
+            r2_ref[key, :] = jnp.broadcast_to(inverse, (block_rows, LANES))
+
+        for s in range(segs):
+            pos = par_ref[pl.ds(8 + p.fsdp * 2 + s % 2, 1), :]
+            lead_ref[s // 2, s % 2 : s % 2 + 1, :width] = h[s * SEG_LEN : s * SEG_LEN + 1, :] + pos
+            lead_ref[s // 2, s % 2 : s % 2 + 1, width:] = cot_ref[s * SEG_LEN : s * SEG_LEN + 16, :].astype(f32)[:1]
+
+    chunks = hidden // tile
+    own(0)
+    own(1)
+    own(2)
+    line(0), plane(0)
+    line(1), plane(1)
+    own(3)
+    line(2), plane(2)
+    last(0), last(1), drain(0), drain(1)
+    params()
+    line(3)
+    own(4)
+    project()
+    keep(qw, w_hbm), keep(pk, p_hbm)
+    plane(3)
+    attend(0)
+    last(2), drain(2)
+    line(4)
+    attend(1)
+    own(5)
+    plane(4)
+    attend(2)
+    wo_start()
+    line(5)
+    attend(3)
+    last(3)
+    plane(5)
+    keep(at, a_hbm), keep(cx, c_hbm)
+    branch()
+    keep(ow, o_hbm), keep(nl, nl_hbm), keep(z1, z1_hbm)
+    drain(3)
+    feed_in(0, chunks // 2)
+    last(4)
+    feed_in(chunks // 2, chunks - chunks // 2)
+    keep(iw, i_hbm), keep(g, g_hbm), keep(sl, sl_hbm)
+    drain(4)
+    feed_back()
+    keep(bw, b_hbm), keep(z2, z2_hbm)
+    last(5)
+    drain(5)
+    wo_finish()
+    for gather in gathers:
+        gather.finish()
+    for i in range(n + 2):
+        pair(i).wait_send()
+    for copy in kept:
+        copy.wait()
+
+
+def segment_forward(pack, x, cot, widths, cross_width, wo_width):
+    n = len(widths)
+    wrows = 16 * ROWS
+    height, total = pack.shape
+    rows, width = x.shape
+    segs = rows // SEG_LEN
+    hidden = widths[3]
+    hbm, vm = pl.BlockSpec(memory_space=pl.ANY), pl.BlockSpec(memory_space=VM)
+    arr = jax.ShapeDtypeStruct
+    att_rows = segs * HEADS * SEG_LEN
+    big = [
+        arr((wrows, 3 * width), bf16), arr((wrows, hidden), bf16), arr((wrows, width), bf16),
+        arr((wrows, hidden), bf16), arr((wrows, cross_width), bf16), arr((192, wo_width), bf16),
+        arr((rows, 3 * width), bf16), arr((att_rows, SEG_LEN), bf16), arr((rows, width), bf16),
+        arr((rows, width), bf16), arr((rows, hidden), bf16), arr((rows, hidden), bf16),
+        arr((rows, width), bf16), arr((rows, width), bf16),
+    ]
+    near = [
+        arr((rows, width), bf16), arr((2, 2, 2 * width), f32), arr((24, width), f32),
+        arr((rows, LANES), f32), arr((rows, LANES), f32),
+    ]
+    return pl.pallas_call(
+        partial(forward_kernel, widths),
+        out_shape=big + near,
+        in_specs=[vm] * 3,
+        out_specs=[hbm] * len(big) + [vm] * len(near),
+        scratch_shapes=[
+            VM((wrows, 256), bf16), VM((wrows, width), bf16), VM((wrows, 3 * width), bf16),
+            VM((wrows, hidden), bf16), VM((wrows, hidden), bf16),
+            VM((rows, 3 * width), bf16), VM((att_rows, SEG_LEN), bf16), VM((rows, width), bf16),
+            VM((rows, width), f32), VM((rows, width), bf16), VM((rows, hidden), bf16),
+            VM((rows, hidden), bf16), VM((rows, width), bf16), VM((rows, width), bf16),
+            VM((height, total), bf16), VM((ROWS, total), bf16),
+        ]
+        + GATHER_SEMS(n + 1)
+        + [
+            pltpu.SemaphoreType.DMA((n + 2,)),
+            pltpu.SemaphoreType.DMA((n + 2,)),
+            pltpu.SemaphoreType.DMA((5,)),
+            pltpu.SemaphoreType.DMA((5,)),
+            pltpu.SemaphoreType.DMA((n + 2,)),
+            pltpu.SemaphoreType.DMA((12,)),
+        ],
+        compiler_params=pltpu.CompilerParams(
+            collective_id=0, has_side_effects=True, vmem_limit_bytes=60 * MIB
+        ),
+    )(pack, x, cot)
+
+
+class Scatter:
+    def __init__(self, place, grad, out, index, sems, pair, r1a, r1b, r2a, r2b, r3, give):
+        self.p, self.grad, self.out, self.m = place, grad, out, index
+        self.send, self.recv = sems
+        self.pair, self.r1a, self.r1b = pair, r1a, r1b
+        self.r2a, self.r2b, self.r3, self.give = r2a, r2b, r3, give
+        self.half = grad.shape[1] // 2
+        tiles = self.half // LANES
+        self.a = (tiles + 1) // 2 * LANES
+        self.b = self.half - self.a
+        self.sent = []
+        p = place
+        far = (1 - p.y) * 2 + 1 - p.x
+        self.groups = (far, p.ydp, p.xdp, p.dp)
+
+    def go(self, src, dst, slot, device):
+        copy = remote(src, dst, self.send.at[self.m, slot], self.recv.at[self.m, slot], device)
+        copy.start()
+        self.sent.append(copy)
+
+    def arrived(self, dst, slot):
+        remote(dst, dst, self.send.at[self.m, slot], self.recv.at[self.m, slot], self.p.sib).wait_recv()
+
+    def cols(self, at, size, core=None):
+        core = self.p.core if core is None else core
+        return lanes(core * self.half + at, size)
+
+    def group(self, dp):
+        return rows_at(dp * 4 * ROWS, 4 * ROWS, 16)
+
+    def start(self):
+        p = self.p
+        for i, dp in enumerate(self.groups):
+            theirs = self.grad.at[self.group(dp), self.cols(0, self.half, 1 - p.core)]
+            self.go(theirs, self.pair.at[self.group(dp)], i, p.sib)
+
+    def add(self, dp, part, other, other_row=0):
+        at, size = {"A": (0, self.a), "B": (self.a, self.b), "AB": (0, self.half)}[part]
+        base = dp * 4 * ROWS
+
+        @pl.loop(0, 4)
+        def _(i):
+            key = (rows_at(base + i * ROWS, ROWS, 16), self.cols(at, size))
+            more = other[rows_at(other_row + i * ROWS, ROWS, 16), :]
+            self.grad[key] = (self.grad[key].astype(f32) + more.astype(f32)).astype(bf16)
+
+    def side(self, dp, part):
+        at, size = (0, self.a) if part == "A" else (self.a, self.b)
+        return self.grad.at[self.group(dp), self.cols(at, size)]
+
+    def one(self):
+        p = self.p
+        near, farther = pl.ds(0, 4 * ROWS), pl.ds(4 * ROWS, 4 * ROWS)
+        for i, dp in enumerate(self.groups):
+            self.arrived(self.pair.at[self.group(dp)], i)
+            self.add(dp, "AB", self.pair, dp * 4 * ROWS)
+            if i == 0:
+                self.go(self.side(dp, "A"), self.r1a.at[near], 4, p.ynbr)
+                if self.b:
+                    self.go(self.side(dp, "B"), self.r1b.at[near], 6, p.xnbr)
+            if i == 1:
+                self.go(self.side(dp, "A"), self.r1a.at[farther], 5, p.ynbr)
+            if i == 2 and self.b:
+                self.go(self.side(dp, "B"), self.r1b.at[farther], 7, p.xnbr)
+
+    def two(self):
+        p = self.p
+        near, farther = pl.ds(0, 4 * ROWS), pl.ds(4 * ROWS, 4 * ROWS)
+        self.arrived(self.r1a.at[near], 4)
+        self.add(p.xdp, "A", self.r1a)
+        self.go(self.side(p.xdp, "A"), self.r2a, 8, p.xnbr)
+        if self.b:
+            self.arrived(self.r1b.at[near], 6)
+            self.add(p.ydp, "B", self.r1b)
+            self.go(self.side(p.ydp, "B"), self.r2b, 9, p.ynbr)
+        self.arrived(self.r1a.at[farther], 5)
+        self.add(p.dp, "A", self.r1a, 4 * ROWS)
+        if self.b:
+            self.arrived(self.r1b.at[farther], 7)
+            self.add(p.dp, "B", self.r1b, 4 * ROWS)
+
+    def three(self):
+        p = self.p
+        self.arrived(self.r2a, 8)
+        self.add(p.dp, "A", self.r2a)
+        if self.b:
+            self.arrived(self.r2b, 9)
+            self.add(p.dp, "B", self.r2b)
+        for d in (1, 3, 2):
+            z = (p.z + d) % 4
+            src = self.grad.at[rows_at((p.dp * 4 + z) * ROWS, ROWS, 16), self.cols(0, self.half)]
+            self.go(src, self.r3.at[d - 1], 9 + d, p.at(p.dp, z, p.core))
+
+    def four(self):
+        p = self.p
+        for d in (1, 3, 2):
+            self.arrived(self.r3.at[d - 1], 9 + d)
+        rows = rows_at((p.dp * 4 + p.z) * ROWS, ROWS, 16)
+        first = p.core == 0
+        step = 384 if self.half % 384 == 0 else LANES
+
+        @pl.loop(0, self.half // step)
+        def _(i):
+            cols = lanes(i * step, step)
+            total = self.grad[rows, self.cols(i * step, step)].astype(f32)
+            for d in range(3):
+                total = total + self.r3[d, :, cols].astype(f32)
+            upper, lower = total[: ROWS // 2], total[ROWS // 2 :]
+            self.give[:, cols] = jnp.where(first, lower, upper)
+            self.out[:, self.cols(i * step, step)] = jnp.where(first, upper, lower)
+
+        self.go(self.give, self.out.at[:, self.cols(0, self.half)], 13, p.sib)
+
+    def five(self):
+        p = self.p
+        self.arrived(self.out.at[:, self.cols(0, self.half, 1 - p.core)], 13)
+
+    def finish(self):
+        for copy in self.sent:
+            copy.wait_send()
+
+
+def scatter_buffers(width):
+    half = width // 2
+    tiles = half // LANES
+    a = (tiles + 1) // 2 * LANES
+    b = max(half - a, LANES)
+    b_rows = 1 if half > a else 0
+    return [
+        VM((16 * ROWS, half), bf16),
+        VM((8 * ROWS, a), bf16),
+        VM((8 * ROWS if b_rows else 16, b), bf16),
+        VM((4 * ROWS, a), bf16),
+        VM((4 * ROWS if b_rows else 16, b), bf16),
+        VM((3, ROWS, half), bf16),
+        VM((ROWS // 2, half), f32),
+    ]
+
+
+def backward_kernel(*refs):
+    (
+        cot_ref, x_ref, home_ref, par_ref, r1_ref, r2_ref, z2_ref, fac_ref, csmall_ref,
+        p_hbm, a_hbm, c_hbm, nl_hbm, g_hbm, sl_hbm, z1_hbm, w_hbm, o_hbm, i_hbm, b_hbm,
+    ) = refs[:20]
+    gt_ref, gq_ref, go_ref, gi_ref, gb_ref, gs_ref = refs[20:26]
+    (
+        pk, at, cx, nl, g, sl, z1, qw, ow, fw,
+        h, df, tr, dwb, dwi, dwo, dwq, dws, small,
+        sib_buf, block, full, tmp,
+        s0, s1, s2, s3, pair_send, pair_recv, local, load, rs_send, rs_recv,
+    ) = refs[26:59]
+    bufs = refs[59:]
+    p = Place()
+    rows, width = x_ref.shape
+    segs = rows // SEG_LEN
+    hidden = g.shape[1]
+    pairs = width // LANES
+    tile = 256
+    chunks = hidden // tile
+
+    loads = {}
+    order = [
+        ("g", g_hbm, g), ("b", b_hbm, fw), ("sl", sl_hbm, sl), ("nl", nl_hbm, nl), ("z1", z1_hbm, z1),
+        ("c", c_hbm, cx), ("o", o_hbm, ow), ("p", p_hbm, pk), ("a", a_hbm, at), ("w", w_hbm, qw),
+        ("i", i_hbm, fw),
+    ]
+    for i, (name, src, dst) in enumerate(order):
+        loads[name] = pltpu.make_async_copy(src, dst, load.at[i])
+    for name, _, _ in order[:-1]:
+        loads[name].start()
     greet(gather_peers(p))
+
     lead2 = block.shape[0]
     lead = lead2 // 2
-    copy = remote(fac_ref, sib_buf, sems[4], sems[5], p.sib)
-    copy.start()
-    copy.wait()
-    block[rows_at(p.core * lead, lead, 16), :] = fac_ref[...]
-    block[rows_at((1 - p.core) * lead, lead, 16), :] = sib_buf[...]
-    width = full.shape[1]
-    model = width // 4
-    slab = model // 4
-    key = rows_at((p.dp * 4 + p.z) * lead2, lead2, 16)
-    mine = pltpu.make_async_copy(block, full.at[key], sems[6])
-    mine.start()
-    run_gathers([Gather(p, full, block, 0, width, 0, sems[:4], lead2)])
+    key_f = rows_at((p.dp * 4 + p.z) * lead2, lead2, 16)
+    swap = remote(fac_ref, sib_buf, pair_send, pair_recv, p.sib)
+    swap.start()
+    mine = pltpu.make_async_copy(block, full.at[key_f], local)
+    factors = Gather(p, full, block, 0, 4 * width, 0, (s0, s1, s2, s3), lead2)
+
+    def factor_own():
+        swap.wait_recv()
+        block[rows_at(p.core * lead, lead, 16), :] = fac_ref[...]
+        block[rows_at((1 - p.core) * lead, lead, 16), :] = sib_buf[...]
+        mine.start()
+        factors.send_own()
+
+    def factor_grads():
+        slab = width // 4
+
+        def rows_of(z, at_col, size):
+            return jnp.concatenate(
+                [full[rows_at((i * 4 + z) * lead2, lead2, 16), pl.ds(at_col, size)] for i in range(4)],
+                axis=0,
+            )
+
+        base = 2 * width + 3 * slab
+        own = rows_at(p.fsdp * (ROWS // 2), ROWS // 2, 8)
+        xl = rows_of(p.dp, base + slab, slab)
+        nlf = rows_of(p.dp, base + 2 * slab, slab)
+        dff = rows_of(p.dp, base + 3 * slab, slab)
+        ctx = rows_of(p.dp, base + 4 * slab, slab)
+        for z in range(4):
+            tmp[:, :width] = mm(dff, rows_of(z, 0, width), TN)
+            gb_ref[1, :, z * width : (z + 1) * width] = tmp[own, :width]
+            tmp[:, :width] = mm(nlf, rows_of(z, width, width), TN)
+            gi_ref[1, :, z * width : (z + 1) * width] = tmp[own, :width]
+            tmp[:, : 3 * slab] = mm(xl, rows_of(z, 2 * width, 3 * slab), TN)
+            got = tmp[own, : 3 * slab]
+            for j in range(3):
+                spot = j * width + z * slab
+                gq_ref[1, :, spot : spot + slab] = got[:, j * slab : (j + 1) * slab]
+            tmp[:, :slab] = mm(ctx, rows_of(z, base, slab), TN)
+            go_ref[1, :, z * slab : (z + 1) * slab] = tmp[own, :slab]
+
+    jobs = []
+    for i, (grad, out) in enumerate(
+        ((dwb, gb_ref.at[0]), (dwi, gi_ref.at[0]), (dwo, go_ref.at[0]), (dws, gs_ref), (dwq, gq_ref.at[0]))
+    ):
+        jobs.append(Scatter(p, grad, out, i, (rs_send, rs_recv), *bufs[7 * i : 7 * i + 7]))
+    back, inn, out, sml, qkv = jobs
+
+    block_rows = 64
+
+    def norm_back(z_ref, r_ref, gain_row, low_ref, sums):
+        def step(i, acc):
+            key = rows_at(i * block_rows, block_rows, 16)
+            dy = h[key, :]
+            z = z_ref[key, :].astype(f32)
+            r = jnp.concatenate([r_ref[key, :]] * (width // LANES), axis=1)
+            e = dy * par_ref[gain_row : gain_row + 1, :]
+            first = jnp.mean(e, axis=-1, keepdims=True)
+            second = jnp.mean(e * z, axis=-1, keepdims=True)
+            d = r * (e - first - z * second)
+            h[key, :] = d
+            low_ref[key, :] = d.astype(bf16)
+            fold = lambda v: jnp.sum(v.reshape(block_rows // 8, 8, width), axis=0)
+            return acc[0] + fold(dy * z), acc[1] + fold(dy)
+
+        zero = jnp.zeros((8, width), f32)
+        gain, bias = lax.fori_loop(0, rows // block_rows, step, (zero, zero))
+        small[sums : sums + 1, :] = jnp.sum(gain, axis=0, keepdims=True)
+        small[sums + 2 : sums + 3, :] = jnp.sum(bias, axis=0, keepdims=True)
+
+    def turn(ref):
+        @pl.loop(0, width // tile)
+        def _(i):
+            tr[rows_at(i * tile, tile, 16), :] = ref[:, lanes(i * tile, tile)].T
+
+    def outer(dst, src, first, count):
+        @pl.loop(first, first + count)
+        def _(i):
+            cols = lanes(i * tile, tile)
+            dst[:, cols] = mm(tr[...], src[:, cols], NN).astype(bf16)
+
+    def norm_two():
+        @pl.loop(0, rows // block_rows)
+        def _(i):
+            key = rows_at(i * block_rows, block_rows, 16)
+            h[key, :] = cot_ref[key, :].astype(f32)
+
+        for s in range(segs):
+            h[s * SEG_LEN : s * SEG_LEN + 1, :] = home_ref[s // 2, s % 2 : s % 2 + 1, width:]
+        small[...] = jnp.zeros_like(small)
+        small[4:8, :] = csmall_ref[0:4, :]
+        for s in range(2):
+            row = home_ref[0, s : s + 1, width:] + home_ref[1, s : s + 1, width:]
+            small[pl.ds(8 + p.fsdp * 2 + s, 1), :] = row
+        norm_back(z2_ref, r2_ref, 1, df, 1)
+        turn(df)
+
+    def active_back(first, count):
+        @pl.loop(first, first + count)
+        def _(i):
+            cols = lanes(i * tile, tile)
+            d = mm(df[...], fw[:, cols], NN) * sl[:, cols].astype(f32)
+            sl[:, cols] = d.astype(bf16)
+
+    def add_back(src, weight):
+        @pl.loop(0, width // tile)
+        def _(i):
+            h[:, lanes(i * tile, tile)] += mm(src[...], weight[rows_at(i * tile, tile, 16), :], NT)
+
+    def context_back():
+        @pl.loop(0, width // tile)
+        def _(i):
+            d = mm(df[...], ow[rows_at(i * tile, tile, 16), :], NT)
+            cx[:, lanes(i * tile, tile)] = d.astype(bf16)
+
+    def attend_back(s):
+        key = pl.ds(s * SEG_LEN, SEG_LEN)
+        factor = (LANES // 2) ** (-0.5)
+
+        @pl.loop(0, pairs)
+        def _(j):
+            a = at[rows_at((s * pairs + j) * 2 * SEG_LEN, 2 * SEG_LEN, 16), :]
+            q_cols = lanes(j * LANES, LANES)
+            k_cols = lanes(width + j * LANES, LANES)
+            v_cols = lanes(2 * width + j * LANES, LANES)
+            qs = jnp.concatenate(lane_halves(pk[key, q_cols]), axis=0)
+            ks = jnp.concatenate(lane_halves(pk[key, k_cols]), axis=0)
+            ds_in = jnp.concatenate(lane_halves(cx[key, q_cols]), axis=0)
+            da = mm(ds_in, pk[key, v_cols], NT)
+            af = a.astype(f32)
+            ds = (af * (da - jnp.sum(af * da, axis=-1, keepdims=True))).astype(bf16)
+            dv = mm(a, ds_in, TN)
+            both = jnp.concatenate([ds[:SEG_LEN], ds[SEG_LEN:]], axis=1)
+            dq = mm(both, ks, NN) * factor
+            dk = mm(ds, qs, TN) * factor
+            pk[key, q_cols] = dq.astype(bf16)
+            pk[key, k_cols] = dk.astype(bf16)
+            pk[key, v_cols] = dv.astype(bf16)
+
+    def result():
+        @pl.loop(0, width // tile)
+        def _(i):
+            cols = lanes(i * tile, tile)
+            d = h[:, cols] + mm(pk[...], qw[rows_at(i * tile, tile, 16), :], NT)
+            gt_ref[:, cols] = d.astype(bf16)
+
+    def smalls():
+        dws[:, :LANES] = small[...].T.astype(bf16)
+        dws[:, LANES:] = jnp.zeros((dws.shape[0], LANES), bf16)
+
+    factor_own()
+    norm_two()
+    factors.pass_line()
+    loads["g"].wait()
+    outer(dwb, g, 0, chunks)
+    back.start()
+    factors.pass_plane()
+    loads["b"].wait()
+    loads["sl"].wait()
+    active_back(0, chunks // 2)
+    back.one()
+    active_back(chunks // 2, chunks - chunks // 2)
+    loads["i"].start()
+    loads["nl"].wait()
+    turn(nl)
+    factors.last()
+    outer(dwi, sl, 0, chunks)
+    inn.start()
+    back.two()
+    loads["i"].wait()
+    add_back(sl, fw)
+    inn.one()
+    loads["z1"].wait()
+    norm_back(z1, r1_ref, 0, df, 0)
+    smalls()
+    sml.start()
+    back.three()
+    loads["c"].wait()
+    turn(cx)
+    outer(dwo, df, 0, width // tile)
+    out.start()
+    factors.drain()
     mine.wait()
-
-    def rows_of(z, at, size):
-        return jnp.concatenate(
-            [full[rows_at((i * 4 + z) * lead2, lead2, 16), pl.ds(at, size)] for i in range(4)], axis=0
-        )
-
-    base = 2 * model + 3 * slab
-    mid = p.dp
-    xl = rows_of(mid, base + slab, slab)
-    nl = rows_of(mid, base + 2 * slab, slab)
-    df = rows_of(mid, base + 3 * slab, slab)
-    ctx = rows_of(mid, base + 4 * slab, slab)
-    own = rows_at(p.fsdp * (ROWS // 2), ROWS // 2, 8)
-    for z in range(4):
-        tmp[:, :model] = mm(df, rows_of(z, 0, model), TN)
-        back_ref[:, z * model : (z + 1) * model] = tmp[own, :model]
-        tmp[:, :model] = mm(nl, rows_of(z, model, model), TN)
-        in_ref[:, z * model : (z + 1) * model] = tmp[own, :model]
-        tmp[:, : 3 * slab] = mm(xl, rows_of(z, 2 * model, 3 * slab), TN)
-        got = tmp[own, : 3 * slab]
-        for j in range(3):
-            at = j * model + z * slab
-            qkv_ref[:, at : at + slab] = got[:, j * slab : (j + 1) * slab]
-        tmp[:, :slab] = mm(ctx, rows_of(z, base, slab), TN)
-        out_ref[:, z * slab : (z + 1) * slab] = tmp[own, :slab]
-
-
-def factor_grads(fac):
-    lead, width = fac.shape
-    model = width // 4
-    half = ROWS // 2
+    loads["o"].wait()
+    context_back()
+    inn.two()
+    out.one()
+    loads["p"].wait()
+    loads["a"].wait()
+    attend_back(0)
+    sml.one()
+    back.four()
+    attend_back(1)
+    inn.three()
+    out.two()
+    attend_back(2)
+    sml.two()
+    inn.four()
+    attend_back(3)
+    turn(x_ref)
+    outer(dwq, pk, 0, 3 * width // tile)
+    qkv.start()
+    out.three()
+    sml.three()
+    back.five()
+    qkv.one()
+    loads["w"].wait()
+    result()
+    qkv.two()
+    inn.five()
+    out.four()
+    sml.four()
+    factor_grads()
+    qkv.three()
+    out.five()
+    sml.five()
+    qkv.four()
+    qkv.five()
+    swap.wait_send()
+    factors.finish()
+    for job in jobs:
+        job.finish()
+
+
+def segment_backward(near, far):
+    cot, x = near[0], near[1]
+    rows, width = x.shape
+    packed, att, context, nl, g = far[:5]
+    hidden = g.shape[1]
+    hbm, vm = pl.BlockSpec(memory_space=pl.ANY), pl.BlockSpec(memory_space=VM)
+    arr = jax.ShapeDtypeStruct
+    own = ROWS // 2
+    lead = near[7].shape[0]
+    like = lambda v: VM(v.shape, v.dtype)
+    wrows = 16 * ROWS
+    widths = (hidden, hidden, width, 256, 3 * width)
+    bufs = []
+    for w in widths:
+        bufs += scatter_buffers(w)
+    DMA = pltpu.SemaphoreType.DMA
     return pl.pallas_call(
-        factor_kernel,
+        backward_kernel,
         out_shape=[
-            jax.ShapeDtypeStruct((half, 3 * model), f32),
-            jax.ShapeDtypeStruct((half, model), f32),
-            jax.ShapeDtypeStruct((half, width), f32),
-            jax.ShapeDtypeStruct((half, width), f32),
+            arr((rows, width), bf16),
+            arr((2, own, 3 * width), f32),
+            arr((2, own, width), f32),
+            arr((2, own, hidden), f32),
+            arr((2, own, hidden), f32),
+            arr((own, 256), f32),
         ],
-        in_specs=[pl.BlockSpec(memory_space=VM)],
-        out_specs=[pl.BlockSpec(memory_space=VM)] * 4,
+        in_specs=[vm] * len(near) + [hbm] * len(far),
+        out_specs=[vm] * 6,
         scratch_shapes=[
-            pltpu.VMEM((lead, width), bf16),
-            pltpu.VMEM((2 * lead, width), bf16),
-            pltpu.VMEM((32 * lead, width), bf16),
-            pltpu.VMEM((model // 4, model), f32),
+            like(packed), like(att), like(context), like(nl), like(g), like(g), like(nl),
+            VM((wrows, 3 * width), bf16), VM((wrows, width), bf16), VM((wrows, hidden), bf16),
+            VM((rows, width), f32), VM((rows, width), bf16), VM((width, rows), bf16),
+            VM((wrows, hidden), bf16), VM((wrows, hidden), bf16), VM((wrows, width), bf16),
+            VM((wrows, 3 * width), bf16), VM((wrows, 256), bf16), VM((LANES, width), f32),
+            VM((lead, 4 * width), bf16), VM((2 * lead, 4 * width), bf16), VM((32 * lead, 4 * width), bf16),
+            VM((width // 4, width), f32),
         ]
         + GATHER_SEMS(1)
-        + [pltpu.SemaphoreType.DMA, pltpu.SemaphoreType.DMA, pltpu.SemaphoreType.DMA],
+        + [DMA, DMA, DMA, DMA((11,)), DMA((5, 14)), DMA((5, 14))]
+        + bufs,
         compiler_params=pltpu.CompilerParams(
-            collective_id=3, has_side_effects=True, vmem_limit_bytes=32 * MIB
+            collective_id=1, has_side_effects=True, vmem_limit_bytes=63 * MIB
         ),
-    )(fac)
+    )(*near, *far)
 
 
 def matmul(left, right, form):
@@ -1137,25 +1519,6 @@
     )
 
 
-def block_backward_terms(factors):
-    (
-        states_low,
-        grad_packed,
-        context,
-        grad_branch,
-        normed_low,
-        grad_hidden,
-        grad_feed,
-        active_low,
-    ) = factors
-    return (
-        matmul(grad_feed, active_low, "gld,glf->df").astype(bf16),
-        matmul(normed_low, grad_hidden, "gld,glf->df").astype(bf16),
-        matmul(context, grad_branch, "gld,gle->de").astype(bf16),
-        matmul(states_low, grad_packed, "gld,gle->de").astype(bf16),
-    )
-
-
 def make_pack(pos_embed, w_qkv, w_out, w_in, w_back, norm_gain, norm_bias):
     own, width = w_out.shape[1:]
     slab = width // 4
@@ -1171,69 +1534,48 @@
         axis=2,
     ).reshape(own, 12 * width)
     pack = jnp.concatenate(
-        [w_qkv[0], small, w_out[0], w_in[0], w_back[0].T, cross, w_out[1]], axis=1
+        [small, w_qkv[0], w_out[0], w_in[0], w_back[0].T, cross, w_out[1]], axis=1
     )
     return jnp.pad(pack, ((0, 32 - own), (0, 0)))
 
 
 def fast_body(tokens, doc_ids, pos_embed, w_qkv, w_out, w_in, w_back, norm_gain, norm_bias, cotangent):
-    rows, local_len, width = tokens.shape
-    seg_count = local_len // SEG_LEN
+    nrows, local_len, width = tokens.shape
+    rows = nrows * local_len
+    segs = rows // SEG_LEN
     hidden = w_in.shape[2]
     pack = make_pack(pos_embed, w_qkv, w_out, w_in, w_back, norm_gain, norm_bias)
-    seg_qkv, small, seg_out_w, seg_in, seg_back, cross_w, cross_wo = gather_weights(
-        pack, (3 * width, 256, width, hidden, hidden), 3 * width, width
-    )
-    items = small.T.astype(f32)
-    seg_weights = (seg_qkv, seg_out_w, seg_in, seg_back.T, items[0:2], items[2:4])
-    cross_norms = jnp.concatenate([items[4:8], jnp.zeros((4, width), f32)], axis=0)
-    pos_full = items[8 : 8 + doc_ids.shape[1]]
-
-    segments = tokens.reshape(rows * seg_count, SEG_LEN, width).astype(f32)
-    seg_out, seg_kept = block_forward(segments, seg_weights, segment_attend)
-    start = lax.axis_index("fsdp") * seg_count
-    pos_local = lax.dynamic_slice_in_dim(pos_full, start, seg_count, 0)
-    leaders = seg_out[:, 0, :].reshape(rows, seg_count, width) + pos_local
-    grad_all = cotangent.reshape(rows * seg_count, SEG_LEN, width).astype(f32)
-    grad_cross = grad_all[:, 0, :].reshape(rows, seg_count, width)
+    x = tokens.reshape(rows, width)
+    cot = cotangent.reshape(rows, width)
+    (
+        s_qkv, s_in, s_out, s_back, cross_w, cross_wo,
+        packed, att, context, nl, act, slope, z_one, z_two,
+        y, lead, par, r_one, r_two,
+    ) = segment_forward(pack, x, cot, (256, 3 * width, width, hidden, hidden), 3 * width, width)
+    norms = par[4:8]
     own_row = lax.dynamic_index_in_dim(doc_ids, lax.axis_index("fsdp") % 2, 0, keepdims=False)
     mask = (own_row[:, None] == own_row[None, :]).astype(f32)
     home, fac, cross_small = cross_block(
-        jnp.concatenate([leaders, grad_cross], axis=2), mask, cross_norms, cross_w, cross_wo
-    )
-    cross_out, grad_leaders = home[..., :width], home[..., width:]
-    joined = jnp.concatenate(
-        [cross_out.reshape(rows * seg_count, 1, width), seg_out[:, 1:, :]], axis=1
-    )
-    output = joined.reshape(rows, local_len, width).astype(bf16)
-    crs_qkv, crs_out, crs_in, crs_back = factor_grads(fac)
-
-    empty_pos = jnp.zeros((doc_ids.shape[1], width), f32)
-    grad_pos = lax.dynamic_update_slice_in_dim(empty_pos, jnp.sum(grad_leaders, axis=0), start, 0)
-    grad_seg = jnp.concatenate(
-        [grad_leaders.reshape(rows * seg_count, 1, width), grad_all[:, 1:, :]], axis=1
-    )
-    grad_states, factors, smalls = block_backward(
-        grad_seg, seg_kept, seg_weights, segment_attend_back
-    )
-    grad_tokens = grad_states.reshape(rows, local_len, width).astype(bf16)
-    small_rows = jnp.concatenate([smalls[0], smalls[1], cross_small[:4], grad_pos], axis=0)
-    small_grads = jnp.pad(small_rows.astype(bf16), ((0, 256 - small_rows.shape[0]), (0, 0))).T
-    terms = block_backward_terms(factors)
-    t_back, t_in, t_out, t_qkv, t_small = scatter_grads((*terms, small_grads))
+        lead, mask, jnp.pad(norms, ((0, 4), (0, 0))), cross_w, cross_wo
+    )
+    cross_out = home[..., :width]
+    output = y.reshape(segs, SEG_LEN, width).at[:, 0].set(cross_out.reshape(segs, width).astype(bf16))
+    output = output.reshape(tokens.shape)
+    grad_tokens, g_qkv, g_out, g_in, g_back, t_small = segment_backward(
+        (cot, x, home, par, r_one, r_two, z_two, fac, cross_small),
+        (packed, att, context, nl, act, slope, z_one, s_qkv, s_out, s_in, s_back),
+    )
     s = t_small.T
-    grad_gain = jnp.stack([s[0:2], s[4:6]])
-    grad_bias = jnp.stack([s[2:4], s[6:8]])
     return (
         output,
-        grad_tokens,
+        grad_tokens.reshape(tokens.shape),
         s[8 : 8 + doc_ids.shape[1]],
-        jnp.stack([t_qkv, crs_qkv]),
-        jnp.stack([t_out, crs_out]),
-        jnp.stack([t_in, crs_in]),
-        jnp.stack([t_back.T, crs_back.T]),
-        grad_gain,
-        grad_bias,
+        g_qkv,
+        g_out,
+        g_in,
+        jnp.swapaxes(g_back, 1, 2),
+        jnp.stack([s[0:2], s[4:6]]),
+        jnp.stack([s[2:4], s[6:8]]),
     )
 
 

time: 383 us -> 288 us (0.75); the launches traced: 377 us -> 288 us
  matrix products: 60.1 us -> 0 us
  other arithmetic: 31.6 us -> 0.68 us
  Pallas kernels: 242 us -> 259 us
  local copies, waits for them, and re-layouts: 41.5 us -> 26.8 us
    dot_general x18 -> x0, matrix products: 60.1 us -> none  [matmul(): return jnp.einsum(form, left, right, preferred_element_type=jnp.float32)]
    convert_element_type x4 -> x0, other arithmetic: 17.8 us -> none  [the longest x1 14.3 us: block_forward(): active_low = jax.nn.gelu(hidden, approximate=False).astype(jnp.bfloat16)]
    pallas_call x3 -> x2, Pallas kernels: 214 us -> 227 us  [the longest x1 118 us: segment_backward(): pl.pallas_call(backward_kernel, out_shape=[arr((rows, width), bf16), arr(...]
    slice x15 -> x7, local copies, waits for them, and re-layouts: 7.92 us -> 2.05 us  [the longest x2 1.07 us: fast_body(): s[2:4]]
    reshape x5 -> x0, local copies, waits for them, and re-layouts: 5.8 us -> none  [the longest x3 5.76 us: join_heads(): return split_part.reshape(groups, length, heads_count * head_size)]
    unnamed x139 -> x41, local copies, waits for them, and re-layouts: 16 us -> 16.3 us
where the time goes in v2:
time: 288 us
  Pallas kernels  259 us (90%)
  local copies, waits for them, and re-layouts  26.8 us (9%)
    pallas_call x1, Pallas kernels, segment_backward(): pl.pallas_call(backward_kernel, out_shape=[arr((rows, width), bf16), arr(...  118 us
    pallas_call x1, Pallas kernels, segment_forward(): pl.pallas_call(partial(forward_kernel, widths), out_shape=big + near, in_...  109 us
    pallas_call x1, Pallas kernels, cross_block(): pl.pallas_call(cross_kernel, out_shape=[jax.ShapeDtypeStruct((2, 2, 2 * w...  31.7 us
    unnamed x41, local copies, waits for them, and re-layouts  16.3 us

profile of v2, /device:TPU:1, one launch (start us, length us, event | category | flops | bytes accessed | tf_op | source)
XLA Modules:
  0.0 287.6 jit_solution(16484404128536688517)
XLA Ops:
  0.7 0.7 slice_bitcast_fusion.2
  1.4 0.7 slice_bitcast_fusion.1
  2.4 0.8 copy.35
  3.3 0.9 bitcast_dynamic-update-slice_fusion.2
  4.2 0.8 bitcast_dynamic-update-slice_fusion.4
  5.0 0.9 bitcast_dynamic-update-slice_fusion.1
  5.9 0.9 bitcast_dynamic-update-slice_fusion
  6.8 0.9 slice.86
  8.2 0.9 slice.87
  9.2 0.9 slice_bitcast_fusion
  10.3 0.9 concatenate.12
  11.3 1.1 pad.15.refs_0_
  12.4 109.3 %shard_map.169 = (bf16[768,2304]{1,0:T(8,128)(2,1)}, bf16[768,3072]{1,0:T(8,128)(2,1)}, bf16[768,768]{1,0:T(8,128)(2,1)}, bf16[768,3072]{1,0:T(8,128)(2,1)}, bf1...) custom-call(bf16[32,19456]{1,0:T(8,128)(2,1)} %pad.15.refs_0_, ...), custom_call_target="tpu_custom_call" | custom-call | tf_op jit(solution)/shard_map/pallas_call | solution.py:736
  121.9 0.7 slice.90
  122.6 2.0 copy-done.1
  124.6 1.0 copy-done.2
  125.6 0.7 copy-done.5
  126.3 31.7 %shard_map.170 = (f32[2,2,1536]{2,1,0:T(2,128)S(1)}, bf16[16,3072]{1,0:T(8,128)(2,1)S(1)}, f32[8,768]{1,0:T(8,128)S(1)}) custom-call(f32[2,2,1536]{2,1,0:T(2,128)S(1)} %copy-done.5, f32[16,16]{1,0:T(8,128)S(1)} %compare_convert_fusion.mask_ref, f32[8,768]{1,0:T(8,128)S(1)} %pad.16.norm_ref, bf16[768,2304]{1,0:T(8,128)(2,1)S(1)} %copy-done.1, ...), custom_call_target="tpu_custom_call" | custom-call | tf_op jit(solution)/shard_map/pallas_call | solution.py:430
  158.0 0.6 copy-done.3
  158.7 0.6 copy-done.6
  159.6 0.3 copy-done.4
  159.9 118.2 %shard_map.171 = (bf16[512,768]{1,0:T(8,128)(2,1)}, f32[2,24,2304]{2,1,0:T(8,128)}, f32[2,24,768]{2,1,0:T(8,128)}, f32[2,24,3072]{2,1,0:T(8,128)}, f32[2,24,3072]{2,1,0:T(8,128)}, /*index=5*/f32[24,256]{1,0:T(8,128)}) custom-call(bf16[512,768]{1,0:T(8,128)(2,1)} %bitcast.48, bf16[512,768]{1,0:T(8,128)(2,1)} %bitcast.46, f32[2,2,1536]{2,1,0:T(2,128)} %copy-done.4, ...), custom_call_target="tpu_custom_call" | custom-call | tf_op jit(solution)/shard_map/pallas_call | solution.py:1178
  278.1 0.9 slice.98
  279.0 0.7 copy.43
  279.7 1.0 fusion
  281.0 0.6 pad_maximum_fusion
  281.6 0.9 copy.60
  282.5 2.1 copy.61
  284.5 0.8 copy.62
  285.3 0.7 copy.63
  286.0 0.8 copy.64
  286.8 0.8 copy.65
  (46 shorter events, 2.0 us)
Async XLA Ops:
  0.6 121.1 %copy-start = (s32[2,16]{1,0:T(2,128)S(1)}, s32[2,16]{1,0:T(2,128)}, u32[]{:S(2)}) copy-start(s32[2,16]{1,0:T(2,128)} %param.13) | copy-start | bytes 388
  1.3 9.9 %copy-start.12 = (bf16[2,24,768]{2,1,0:T(8,128)(2,1)S(1)}, bf16[2,24,768]{2,1,0:T(8,128)(2,1)}, u32[]{:S(2)}) copy-start(bf16[2,24,768]{2,1,0:T(8,128)(2,1)} %param.16) | copy-start | bytes 221188
  122.6 2.0 copy-start.1
  124.6 1.0 copy-start.2
  125.6 0.7 copy-start.5
  126.3 33.0 %copy-start.7 = (bf16[512,768]{1,0:T(8,128)(2,1)S(1)}, bf16[512,768]{1,0:T(8,128)(2,1)}, u32[]{:S(2)}) copy-start(bf16[512,768]{1,0:T(8,128)(2,1)} %get-tuple-element.49) | copy-start | bytes 2359300
  158.0 0.6 copy-start.3
  158.7 0.6 copy-start.6
  159.3 0.6 copy-start.4
  278.1 6.5 %copy-start.10 = (f32[2,24,2304]{2,1,0:T(8,128)S(1)}, f32[2,24,2304]{2,1,0:T(8,128)}, u32[]{:S(2)}) copy-start(f32[2,24,2304]{2,1,0:T(8,128)} %get-tuple-element.117) | copy-start | bytes 1327108
  278.1 7.2 %copy-start.11 = (f32[2,24,768]{2,1,0:T(8,128)S(1)}, f32[2,24,768]{2,1,0:T(8,128)}, u32[]{:S(2)}) copy-start(f32[2,24,768]{2,1,0:T(8,128)} %get-tuple-element.118) | copy-start | bytes 442372
  278.1 7.9 %copy-start.9 = (f32[2,24,3072]{2,1,0:T(8,128)S(1)}, f32[2,24,3072]{2,1,0:T(8,128)}, u32[]{:S(2)}) copy-start(f32[2,24,3072]{2,1,0:T(8,128)} %get-tuple-element.119) | copy-start | bytes 1769476
  278.1 8.7 %copy-start.8 = (f32[2,24,3072]{2,1,0:T(8,128)S(1)}, f32[2,24,3072]{2,1,0:T(8,128)}, u32[]{:S(2)}) copy-start(f32[2,24,3072]{2,1,0:T(8,128)} %get-tuple-element.76) | copy-start | bytes 1769476

commit v3 on v0

--- a/solution.py
+++ b/solution.py
@@ -3,6 +3,8 @@
 import jax
 import jax.numpy as jnp
 from jax import lax
+from jax.experimental import pallas as pl
+from jax.experimental.pallas import tpu as pltpu
 from jax.sharding import PartitionSpec as P
 
 HEADS = 12
@@ -12,6 +14,1175 @@
 epsilon = 1e-05
 root_half = 0.7071067811865476
 inv_root_tau = 0.3989422804014327
+
+bf16 = jnp.bfloat16
+f32 = jnp.float32
+MESH = pl.DeviceIdType.MESH
+VM = pltpu.VMEM
+MIB = 1024 * 1024
+ROWS = 48
+LANES = 128
+
+
+class Place:
+    def __init__(self):
+        self.dp = lax.axis_index("dp")
+        self.fsdp = lax.axis_index("fsdp")
+        self.y, self.x = self.dp // 2, self.dp % 2
+        self.z, self.core = self.fsdp // 2, self.fsdp % 2
+
+    def at(self, dp, z, core):
+        return (dp, z * 2 + core)
+
+    @property
+    def sib(self):
+        return (self.dp, self.z * 2 + 1 - self.core)
+
+    @property
+    def xdp(self):
+        return self.y * 2 + 1 - self.x
+
+    @property
+    def ydp(self):
+        return (1 - self.y) * 2 + self.x
+
+    @property
+    def xnbr(self):
+        return (self.xdp, self.fsdp)
+
+    @property
+    def ynbr(self):
+        return (self.ydp, self.fsdp)
+
+
+def greet(devices):
+    barrier = pltpu.get_barrier_semaphore()
+    for device in devices:
+        pl.semaphore_signal(barrier, inc=1, device_id=device, device_id_type=MESH)
+    pl.semaphore_wait(barrier, len(devices))
+
+
+def remote(src, dst, send, recv, device):
+    return pltpu.make_async_remote_copy(
+        src_ref=src, dst_ref=dst, send_sem=send, recv_sem=recv, device_id=device, device_id_type=MESH
+    )
+
+
+def lanes(start, size):
+    if isinstance(start, int):
+        return pl.ds(start, size)
+    return pl.ds(pl.multiple_of(start, LANES), size)
+
+
+def rows_at(start, size, unit):
+    return pl.ds(pl.multiple_of(start, unit), size)
+
+
+class Gather:
+    def __init__(self, place, out, off, width, source, index, sems, height2, wide_a=True):
+        self.p, self.out, self.off, self.source = place, out, off, source
+        self.m, self.sems, self.h2 = index, sems, height2
+        self.half = width // 2
+        tiles = self.half // LANES
+        self.a = ((tiles + 1) // 2 if wide_a else max(tiles // 2, 1)) * LANES
+        self.b = self.half - self.a
+        self.sent = []
+        self.far = (1 - place.y) * 2 + 1 - place.x
+
+    def cols(self, core, part="AB"):
+        at, size = {"A": (0, self.a), "B": (self.a, self.b), "AB": (0, self.half)}[part]
+        return lanes(self.off + core * self.half + at, size)
+
+    def block(self, z, core):
+        return self.out.at[rows_at((self.p.dp * 4 + z) * self.h2, self.h2, 16), self.cols(core)]
+
+    def group(self, dp, core, part="AB"):
+        return self.out.at[rows_at(dp * 4 * self.h2, self.h2 * 4, 16), self.cols(core, part)]
+
+    def go(self, src, dst, slot, device):
+        copy = remote(src, dst, self.sems[0].at[self.m, slot], self.sems[1].at[self.m, slot], device)
+        copy.start()
+        self.sent.append(copy)
+
+    def hand(self, ref, slot):
+        self.go(ref, ref, slot, self.p.sib)
+
+    def arrived(self, dst, slot):
+        remote(dst, dst, self.sems[0].at[self.m, slot], self.sems[1].at[self.m, slot], self.p.sib).wait_recv()
+
+    def own(self):
+        p = self.p
+        for d in (1, 3, 2):
+            z = (p.z + d) % 4
+            self.go(self.source(z), self.block(p.z, p.core), d - 1, p.at(p.dp, z, p.core))
+
+    def line(self):
+        p = self.p
+        for d in (1, 3, 2):
+            self.arrived(self.block((p.z + 4 - d) % 4, p.core), d - 1)
+        mine = self.group(p.dp, p.core)
+        self.go(mine, mine, 3, p.xnbr)
+        self.go(mine, mine, 4, p.ynbr)
+        self.hand(mine, 7)
+
+    def plane(self):
+        p = self.p
+        over_x, over_y = self.group(p.xdp, p.core), self.group(p.ydp, p.core)
+        self.arrived(over_x, 3)
+        part = self.group(p.xdp, p.core, "A")
+        self.go(part, part, 5, p.ynbr)
+        self.arrived(over_y, 4)
+        if self.b:
+            part = self.group(p.ydp, p.core, "B")
+            self.go(part, part, 6, p.xnbr)
+        self.hand(over_x, 8)
+        self.hand(over_y, 9)
+
+    def last(self):
+        p = self.p
+        self.arrived(self.group(self.far, p.core, "A"), 5)
+        if self.b:
+            self.arrived(self.group(self.far, p.core, "B"), 6)
+        self.hand(self.group(self.far, p.core), 10)
+
+    def drain(self):
+        p = self.p
+        for slot, dp in ((7, p.dp), (8, p.xdp), (9, p.ydp), (10, self.far)):
+            self.arrived(self.group(dp, 1 - p.core), slot)
+
+    def finish(self):
+        for copy in self.sent:
+            copy.wait_send()
+
+
+class Staged:
+    def __init__(self, units, order):
+        self.units, self.order, self.at = units, order, 0
+
+    def step(self, count=1):
+        for name, i in self.order[self.at : self.at + count]:
+            getattr(self.units[i], name)()
+        self.at += count
+
+    def upto(self, name, i):
+        spot = self.order.index((name, i)) + 1
+        if spot > self.at:
+            self.step(spot - self.at)
+
+    def finish(self):
+        self.step(len(self.order) - self.at)
+        for unit in self.units:
+            unit.finish()
+
+
+def staggered(count, lags, first=0):
+    order = []
+    for t in range(min(lags.values()), count + max(lags.values())):
+        for name, lag in lags.items():
+            if 0 <= t - lag < count and (t >= 0 or lag < 0):
+                order.append((name, t - lag + first))
+    return order
+
+
+def gather_peers(p):
+    peers = [p.sib, p.xnbr, p.ynbr]
+    for d in (1, 2, 3):
+        peers.append(p.at(p.dp, (p.z + d) % 4, p.core))
+    return peers
+
+
+def everyone(p):
+    return [
+        (lax.rem(p.dp + i, 4), lax.rem(p.fsdp + j, 8)) for i in range(4) for j in range(8) if i or j
+    ]
+
+
+NEG = -1e30
+
+
+def mm(a, b, dims):
+    return lax.dot_general(a, b, (dims, ((), ())), preferred_element_type=f32)
+
+
+NN = ((1,), (0,))
+NT = ((1,), (1,))
+TN = ((0,), (0,))
+
+
+def norm_rows(summed, gain, bias):
+    centred = summed - jnp.mean(summed, axis=-1, keepdims=True)
+    variance = jnp.mean(centred * centred, axis=-1, keepdims=True)
+    inverse = lax.rsqrt(variance + epsilon)
+    scaled = centred * inverse
+    return scaled * gain + bias, scaled, inverse
+
+
+def norm_rows_back(grad, scaled, inverse, gain):
+    g = grad * gain
+    first = jnp.mean(g, axis=-1, keepdims=True)
+    second = jnp.mean(g * scaled, axis=-1, keepdims=True)
+    return inverse * (g - first - scaled * second)
+
+
+def gelu_parts(u):
+    cumulative = 0.5 * (1.0 + lax.erf(u * root_half))
+    return cumulative, cumulative + u * inv_root_tau * jnp.exp(-0.5 * u * u)
+
+
+def lane_halves(v):
+    low = lax.broadcasted_iota(jnp.int32, v.shape, 1) < LANES // 2
+    zero = jnp.zeros_like(v)
+    return jnp.where(low, v, zero), jnp.where(low, zero, v)
+
+
+FORWARD_LAGS = {"own": -3, "line": 0, "plane": 1, "last": 2, "drain": 3}
+
+
+def forward_order(n_seg, n_cross):
+    n = n_seg + n_cross
+    order = staggered(n, FORWARD_LAGS)
+    stop = order.index(("line", n_seg))
+    head, rest = order[:stop], order[stop:]
+    head += [s for s in rest if s[0] == "own"]
+    done = set(head)
+    tail = [("plane", n_seg - 1), ("line", n_seg), ("line", n_seg + 1)]
+    for u in range(n_seg - 3, n_seg):
+        tail += [("last", u), ("drain", u)]
+    tail += [("plane", n_seg), ("line", n_seg + 2)]
+    for u in range(n_seg, n):
+        tail += [("last", u), ("plane", u + 1), ("drain", u)]
+    return head + [s for s in tail if s not in done and s[1] < n]
+
+
+def forward_kernel(*refs):
+    wq_ref, wo_ref, wi_ref, wb_ref, ws_ref, x_ref, cot_ref, mask_ref = refs[:8]
+    (
+        w_hbm, i_hbm, o_hbm, b_hbm,
+        p_hbm, a_hbm, c_hbm, nl_hbm, g_hbm, sl_hbm, z1_hbm, z2_hbm,
+        y_ref, par_ref, r1_ref, r2_ref, home_ref, fac_ref, small_ref,
+    ) = refs[8:27]
+    (
+        sw, ow, qw, iw, bw, cw, cwo,
+        pk, at, cx, h, nl, g, sl, z1, z2,
+        own_buf, sib_buf, block,
+        lead_out, gbuf, lead, xbuf, ybuf, dpack,
+        s_send, s_recv, pair_send, pair_recv, wo_send, wo_recv, local, out_sem,
+        g_send, g_recv, x_send, x_recv, h_send, h_recv, lead_sem,
+    ) = refs[27:]
+    p = Place()
+    rows, width = x_ref.shape
+    segs = rows // SEG_LEN
+    hidden = iw.shape[1]
+    pairs = width // LANES
+    slab = width // 4
+    cross_width = cw.shape[1]
+    half_rows = ROWS // 2
+    key_own = rows_at((p.dp * 4 + p.z) * ROWS, ROWS, 16)
+
+    sizes = [ws_ref.shape[1]] + [width] * (3 + 1 + 2 * (hidden // width)) + [4 * cross_width, width]
+    starts = [sum(sizes[:i]) for i in range(len(sizes))]
+    n_seg = len(sizes) - 2
+    part_cross, part_wo = n_seg, n_seg + 1
+
+    def put(start, value):
+        zero = jnp.zeros((own_buf.shape[0] - half_rows, value.shape[1]), f32)
+        full = jnp.concatenate([value.astype(f32), zero], axis=0).astype(bf16)
+        own_buf[:, pl.ds(start, value.shape[1])] = full
+
+    def pair(i):
+        cols = pl.ds(starts[i], sizes[i])
+        return remote(
+            own_buf.at[:, cols], sib_buf.at[:, cols], pair_send.at[i], pair_recv.at[i], p.sib
+        )
+
+    def stage(i):
+        spot = starts[i]
+        per = hidden // width
+        if i == 0:
+            put(spot, ws_ref[...])
+        elif i < 4:
+            put(spot, wq_ref[0, :, (i - 1) * width : i * width])
+        elif i == 4:
+            put(spot, wo_ref[0])
+        elif i < 5 + per:
+            put(spot, wi_ref[0, :, (i - 5) * width : (i - 4) * width])
+        elif i < 5 + 2 * per:
+            put(spot, wb_ref[0, :, (i - 5 - per) * width : (i - 4 - per) * width])
+        elif i == part_cross:
+            for z in range(4):
+                heads = [wq_ref[1, :, j * width + z * slab : j * width + (z + 1) * slab] for j in range(3)]
+                heads.append(heads[2])
+                put(spot, jnp.concatenate([v.astype(f32) for v in heads], axis=1).astype(bf16))
+                put(spot + width, wi_ref[1, :, z * width : (z + 1) * width])
+                put(spot + 2 * width, wb_ref[1, :, z * width : (z + 1) * width])
+                spot += cross_width
+        else:
+            put(spot, wo_ref[1])
+
+    def joined(start, size):
+        cols = lanes(start, size)
+        first = p.core == 0
+        mine = own_buf[:, cols].astype(f32)[:half_rows]
+        theirs = sib_buf[:, cols].astype(f32)[:half_rows]
+        both = [jnp.where(first, mine, theirs), jnp.where(first, theirs, mine)]
+        return jnp.concatenate(both, axis=0).astype(bf16)
+
+    ahead = 4
+
+    def begin(i):
+        if i < n_seg + 2:
+            stage(i)
+            pair(i).start()
+
+    stage(0)
+    greet(everyone(p))
+    pair(0).start()
+    for i in range(1, ahead):
+        begin(i)
+
+    sems = (s_send, s_recv)
+    dests = [(sw, 0)] + [(qw, i * width) for i in range(3)] + [(ow, 0)]
+    dests += [(iw, i * width) for i in range(hidden // width)]
+    dests += [(bw, i * width) for i in range(hidden // width)]
+
+    class SegUnit(Gather):
+        def __init__(self, i):
+            dst, off = dests[i]
+            mine = lambda z: dst.at[key_own, self.cols(p.core)]
+            super().__init__(p, dst, off, sizes[i], mine, i, sems, ROWS, i % 2 == 0)
+            self.i = i
+
+        def own(self):
+            pair(self.i).wait_recv()
+            self.out[key_own, self.cols(p.core)] = joined(
+                starts[self.i] + p.core * self.half, self.half
+            )
+            super().own()
+            begin(self.i + ahead)
+
+    class CrossUnit(Gather):
+        def __init__(self, i):
+            start = i * width
+            self.i = i
+
+            def mine(z):
+                spot = z * cross_width + start + p.core * self.half
+                return block.at[:, lanes(spot, self.half)]
+
+            super().__init__(p, cw, start, width, mine, n_seg + i, sems, ROWS, i % 2 == 0)
+
+        def own(self):
+            if self.i == 0:
+                pair(part_cross).wait_recv()
+
+                @pl.loop(0, 4 * cross_width // width)
+                def _(k):
+                    block[:, lanes(k * width, width)] = joined(starts[part_cross] + k * width, width)
+
+            spot = p.z * cross_width + self.i * width + p.core * self.half
+            self.out[key_own, self.cols(p.core)] = block[:, lanes(spot, self.half)]
+            super().own()
+
+    units = [SegUnit(i) for i in range(n_seg)] + [CrossUnit(i) for i in range(cross_width // width)]
+    n_cross = len(units) - n_seg
+    comm = Staged(units, forward_order(n_seg, n_cross))
+
+    def need(i):
+        comm.upto("drain", i)
+
+    def pump():
+        comm.step(5)
+
+    half_wo = width // 2
+    wo_block = block.at[:, pl.ds(4 * cross_width, width)]
+    wo_src = block.at[:, lanes(4 * cross_width + p.core * half_wo, half_wo)]
+    wo_dst = cwo.at[rows_at(p.z * ROWS, ROWS, 16), lanes(p.core * half_wo, half_wo)]
+
+    def wo_copy(i):
+        return remote(wo_src, wo_dst, wo_send.at[i], wo_recv.at[p.z], p.at(i, p.dp, p.core))
+
+    def wo_start():
+        pair(part_wo).wait_recv()
+        wo_block[...] = joined(starts[part_wo], width)
+        for i in range(4):
+            here = jnp.logical_and(p.dp == i, p.dp == p.z)
+
+            @pl.when(jnp.logical_not(here))
+            def _():
+                wo_copy(i).start()
+
+            @pl.when(here)
+            def _():
+                mine = pltpu.make_async_copy(wo_src, wo_dst, local)
+                mine.start()
+                mine.wait()
+
+    wo_mine = cwo.at[:, lanes(p.core * half_wo, half_wo)]
+    wo_theirs = cwo.at[:, lanes((1 - p.core) * half_wo, half_wo)]
+    wo_hand = remote(wo_mine, wo_mine, wo_send.at[4], wo_recv.at[4], p.sib)
+
+    def wo_middle():
+        for i in range(4):
+            piece = cwo.at[pl.ds(i * ROWS, ROWS), lanes(p.core * half_wo, half_wo)]
+
+            @pl.when(jnp.logical_not(jnp.logical_and(p.z == p.dp, p.z == i)))
+            def _():
+                remote(piece, piece, wo_send.at[i], wo_recv.at[i], p.sib).wait_recv()
+
+        wo_hand.start()
+
+    def wo_finish():
+        remote(wo_theirs, wo_theirs, wo_send.at[4], wo_recv.at[4], p.sib).wait_recv()
+        wo_hand.wait_send()
+        for i in range(4):
+
+            @pl.when(jnp.logical_not(jnp.logical_and(p.dp == i, p.dp == p.z)))
+            def _():
+                wo_copy(i).wait_send()
+
+    kept = []
+
+    def keep(src, dst):
+        copy = pltpu.make_async_copy(src, dst, out_sem.at[len(kept)])
+        copy.start()
+        kept.append(copy)
+
+    tile = 256
+
+    def params():
+        par_ref[...] = sw[...].astype(f32).T[: par_ref.shape[0]]
+
+    def project(first, count):
+        @pl.loop(first, first + count)
+        def _(i):
+            cols = lanes(i * tile, tile)
+            pk[:, cols] = mm(x_ref[...], qw[:, cols], NN).astype(bf16)
+
+    def attend(s):
+        key = pl.ds(s * SEG_LEN, SEG_LEN)
+
+        @pl.loop(0, pairs)
+        def _(j):
+            q2 = pk[key, lanes(j * LANES, LANES)]
+            k2 = pk[key, lanes(width + j * LANES, LANES)]
+            v2 = pk[key, lanes(2 * width + j * LANES, LANES)]
+            scores = mm(jnp.concatenate(lane_halves(q2), axis=0), k2, NT) * (LANES // 2) ** (-0.5)
+            top = jnp.max(scores, axis=-1, keepdims=True)
+            terms = jnp.exp(scores - top)
+            a = (terms / jnp.sum(terms, axis=-1, keepdims=True)).astype(bf16)
+            at[rows_at((s * pairs + j) * 2 * SEG_LEN, 2 * SEG_LEN, 16), :] = a
+            both = jnp.concatenate([a[:SEG_LEN], a[SEG_LEN:]], axis=1)
+            c2 = mm(both, jnp.concatenate(lane_halves(v2), axis=0), NN)
+            cx[key, lanes(j * LANES, LANES)] = c2.astype(bf16)
+
+    block_rows = 64
+
+    def branch():
+        @pl.loop(0, width // tile)
+        def _(i):
+            cols = lanes(i * tile, tile)
+            h[:, cols] = x_ref[:, cols].astype(f32) + mm(cx[...], ow[:, cols], NN)
+
+        @pl.loop(0, rows // block_rows)
+        def _(i):
+            key = rows_at(i * block_rows, block_rows, 16)
+            normed, scaled, inverse = norm_rows(h[key, :], par_ref[0:1, :], par_ref[2:3, :])
+            h[key, :] = normed
+            nl[key, :] = normed.astype(bf16)
+            z1[key, :] = scaled.astype(bf16)
+            r1_ref[key, :] = jnp.broadcast_to(inverse, (block_rows, LANES))
+
+    def feed_in(first, count):
+        @pl.loop(first, first + count)
+        def _(i):
+            cols = lanes(i * tile, tile)
+            u = mm(nl[...], iw[:, cols], NN)
+            phi, slope = gelu_parts(u)
+            g[:, cols] = (u * phi).astype(bf16)
+            sl[:, cols] = slope.astype(bf16)
+
+    def feed_back(part):
+        inner = pl.ds(part * width, width)
+
+        @pl.loop(0, width // tile)
+        def _(i):
+            cols = lanes(i * tile, tile)
+            h[:, cols] += mm(g[:, inner], bw[rows_at(i * tile, tile, 16), inner], NT)
+
+    def finish_block():
+        @pl.loop(0, rows // block_rows)
+        def _(i):
+            key = rows_at(i * block_rows, block_rows, 16)
+            result, scaled, inverse = norm_rows(h[key, :], par_ref[1:2, :], par_ref[3:4, :])
+            h[key, :] = result
+            y_ref[key, :] = result.astype(bf16)
+            z2[key, :] = scaled.astype(bf16)
+            r2_ref[key, :] = jnp.broadcast_to(inverse, (block_rows, LANES))
+
+    def leaders():
+        for s in range(segs):
+            pos = par_ref[pl.ds(8 + p.fsdp * 2 + s % 2, 1), :]
+            lead_out[s // 2, s % 2 : s % 2 + 1, :width] = h[s * SEG_LEN : s * SEG_LEN + 1, :] + pos
+            lead_out[s // 2, s % 2 : s % 2 + 1, width:] = cot_ref[s * SEG_LEN : s * SEG_LEN + 16, :].astype(f32)[:1]
+
+    def lead_copy(z, j):
+        i = 2 * z + j
+        return remote(lead_out.at[j], gbuf.at[p.fsdp], g_send.at[i], g_recv.at[p.fsdp], (p.dp, i))
+
+    per = hidden // width
+    head = width // HEADS
+    heads = HEADS // 4
+    n_tiles = width // tile
+    need(0)
+    params()
+    for i in range(3):
+        need(1 + i)
+        project(i * n_tiles, n_tiles)
+    for s in range(segs):
+        attend(s)
+        comm.upto("drain", 4 + s)
+    keep(qw, w_hbm), keep(pk, p_hbm), keep(at, a_hbm), keep(cx, c_hbm)
+    branch()
+    keep(ow, o_hbm), keep(nl, nl_hbm), keep(z1, z1_hbm)
+    for i in range(per):
+        need(8 + i)
+        feed_in(i * n_tiles, n_tiles)
+    wo_start()
+    keep(iw, i_hbm), keep(g, g_hbm), keep(sl, sl_hbm)
+    for i in range(per):
+        need(5 + per + i)
+        feed_back(i)
+    finish_block()
+    keep(bw, b_hbm), keep(z2, z2_hbm)
+    leaders()
+    for d in range(4):
+        z = (p.z + d) % 4
+        for j in range(2):
+            if d:
+                lead_copy(z, j).start()
+            else:
+
+                @pl.when(p.core != j)
+                def _():
+                    lead_copy(z, j).start()
+
+                @pl.when(p.core == j)
+                def _():
+                    mine = pltpu.make_async_copy(lead_out.at[j], gbuf.at[p.fsdp], lead_sem)
+                    mine.start()
+                    mine.wait()
+
+    need(n_seg)
+    wo_middle()
+    for d in range(1, 8):
+        i = lax.rem(p.fsdp + d, 8)
+        remote(gbuf.at[i], gbuf.at[i], g_send.at[i], g_recv.at[i], p.sib).wait_recv()
+    for i in range(8):
+        lead[2 * i : 2 * i + 2, :] = gbuf[i]
+    states = lead[:, :width]
+    cot = lead[:, width:]
+
+    def sum_z(e, partial_sum):
+        xbuf[e, p.z] = partial_sum.astype(bf16)
+        copies = []
+        for d in (1, 3, 2):
+            z = (p.z + d) % 4
+            copy = remote(
+                xbuf.at[e, p.z], xbuf.at[e, p.z], x_send.at[e, d - 1], x_recv.at[e, p.z],
+                p.at(p.dp, z, p.core),
+            )
+            copy.start()
+            copies.append(copy)
+        for d in (1, 3, 2):
+            z = (p.z + d) % 4
+            piece = xbuf.at[e, z]
+            remote(piece, piece, x_send.at[e, d - 1], x_recv.at[e, z], p.sib).wait_recv()
+        for copy in copies:
+            copy.wait_send()
+        return sum(xbuf[e, z].astype(f32) for z in range(4))
+
+    gain0, gain1 = par_ref[4:5, :], par_ref[5:6, :]
+    bias0, bias1 = par_ref[6:7, :], par_ref[7:8, :]
+    in_cols, back_cols = pl.ds(width, width), pl.ds(2 * width, width)
+    qkv_cols = pl.ds(0, 3 * slab)
+    factor = head ** (-0.5)
+    allowed = mask_ref[...] > 0.5
+
+    xl = states.astype(bf16)
+    packed = mm(xl, cw[:, qkv_cols], NN).astype(bf16)
+    q = [packed[:, i * head : (i + 1) * head] for i in range(heads)]
+    k = [packed[:, slab + i * head : slab + (i + 1) * head] for i in range(heads)]
+    v = [packed[:, 2 * slab + i * head : 2 * slab + (i + 1) * head] for i in range(heads)]
+    att, context = [], []
+    for i in range(heads):
+        scores = jnp.where(allowed, mm(q[i], k[i], NT) * factor, NEG)
+        top = jnp.max(scores, axis=-1, keepdims=True)
+        terms = jnp.exp(scores - top)
+        a = terms / jnp.sum(terms, axis=-1, keepdims=True)
+        att.append(a)
+        context.append(mm(a.astype(bf16), v[i], NN))
+    context = jnp.concatenate(context, axis=1).astype(bf16)
+    wo_finish()
+    branch = sum_z(0, mm(context, cwo[...], NN))
+    normed, z_one, r_one = norm_rows(states + branch, gain0, bias0)
+    nl = normed.astype(bf16)
+    need(n_seg + 1)
+    hidden = mm(nl, cw[:, in_cols], NN)
+    phi, slope = gelu_parts(hidden)
+    active = (hidden * phi).astype(bf16)
+    need(n_seg + 2)
+    feed = sum_z(1, mm(active, cw[:, back_cols], NT))
+    result, z_two, r_two = norm_rows(normed + feed, gain1, bias1)
+    d_two = norm_rows_back(cot, z_two, r_two, gain1)
+    df = d_two.astype(bf16)
+    du = (mm(df, cw[:, back_cols], NN) * slope).astype(bf16)
+    d_normed = d_two + sum_z(2, mm(du, cw[:, in_cols], NT))
+    d_one = norm_rows_back(d_normed, z_one, r_one, gain0)
+    db = d_one.astype(bf16)
+    dc = mm(db, cwo[...], NT).astype(bf16)
+    for i in range(heads):
+        a = att[i]
+        dci = dc[:, i * head : (i + 1) * head]
+        da = mm(dci, v[i], NT)
+        dv = mm(a.astype(bf16), dci, TN)
+        ds = (a * (da - jnp.sum(a * da, axis=-1, keepdims=True))).astype(bf16)
+        dq = mm(ds, k[i], NN) * factor
+        dk = mm(ds, q[i], TN) * factor
+        for j, piece in enumerate((dq, dk, dv)):
+            dpack[:, j * slab + i * head : j * slab + (i + 1) * head] = piece
+    dp = dpack[...].astype(bf16)
+    dx = d_one + sum_z(3, mm(dp, cw[:, qkv_cols], NT))
+    for i in range(8):
+        ybuf[i, :, :width] = result[2 * i : 2 * i + 2]
+        ybuf[i, :, width:] = dx[2 * i : 2 * i + 2]
+    home = remote(
+        ybuf.at[2 * p.z + 1 - p.core], home_ref.at[p.core], h_send, h_recv, p.sib
+    )
+    home.start()
+    home_ref[p.core] = ybuf[2 * p.z + p.core]
+
+    def part(full):
+        pieces = [full[:, i * slab : (i + 1) * slab] for i in range(4)]
+        out = pieces[0]
+        for i in range(1, 4):
+            out = jnp.where(p.z == i, pieces[i], out)
+        return out.astype(bf16)
+
+    fac_ref[:, :width] = active
+    fac_ref[:, width : 2 * width] = du
+    fac_ref[:, 2 * width :] = jnp.concatenate(
+        [dp, part(d_one), part(states), part(normed), part(d_two), context], axis=1
+    )
+    once = jnp.where(p.z == 0, 1.0, 0.0)
+    sums = [d_normed * z_one, cot * z_two, d_normed, cot]
+    small_ref[...] = jnp.zeros_like(small_ref)
+    for i, s in enumerate(sums):
+        small_ref[i : i + 1, :] = once * jnp.sum(s, axis=0, keepdims=True)
+    theirs = home_ref.at[1 - p.core]
+    remote(theirs, theirs, h_send, h_recv, p.sib).wait_recv()
+    home.wait_send()
+    for d in range(4):
+        z = (p.z + d) % 4
+        for j in range(2):
+            if d:
+                lead_copy(z, j).wait_send()
+            else:
+
+                @pl.when(p.core != j)
+                def _():
+                    lead_copy(z, j).wait_send()
+    comm.finish()
+    for i in range(n_seg + 2):
+        pair(i).wait_send()
+    for s in range(segs):
+        spot = pl.ds(s * SEG_LEN, 16)
+        old = y_ref[spot, :].astype(f32)
+        new = jnp.broadcast_to(home_ref[s // 2, s % 2 : s % 2 + 1, :width], old.shape)
+        top = lax.broadcasted_iota(jnp.int32, old.shape, 0) == 0
+        y_ref[spot, :] = jnp.where(top, new, old).astype(bf16)
+    for copy in kept:
+        copy.wait()
+
+
+def segment_forward(ws, wq, wo, wi, wb, x, cot, mask):
+    wrows = 16 * ROWS
+    rows, width = x.shape
+    segs = rows // SEG_LEN
+    leads = mask.shape[0]
+    hidden = wi.shape[2]
+    cross_width = 3 * width
+    total = ws.shape[1] + 3 * width + width + 2 * hidden + 4 * cross_width + width
+    parts = 5 + 2 * hidden // width + 2
+    n_units = parts - 2 + 3
+    hbm, vm = pl.BlockSpec(memory_space=pl.ANY), pl.BlockSpec(memory_space=VM)
+    arr = jax.ShapeDtypeStruct
+    DMA = pltpu.SemaphoreType.DMA
+    att_rows = segs * HEADS * SEG_LEN
+    big = [
+        arr((wrows, 3 * width), bf16), arr((wrows, hidden), bf16), arr((wrows, width), bf16),
+        arr((wrows, hidden), bf16),
+        arr((rows, 3 * width), bf16), arr((att_rows, SEG_LEN), bf16), arr((rows, width), bf16),
+        arr((rows, width), bf16), arr((rows, hidden), bf16), arr((rows, hidden), bf16),
+        arr((rows, width), bf16), arr((rows, width), bf16),
+    ]
+    near = [
+        arr((rows, width), bf16), arr((24, width), f32),
+        arr((rows, LANES), f32), arr((rows, LANES), f32),
+        arr((2, 2, 2 * width), f32), arr((leads, 4 * width), bf16), arr((8, width), f32),
+    ]
+    return pl.pallas_call(
+        forward_kernel,
+        out_shape=big + near,
+        in_specs=[vm] * 8,
+        out_specs=[hbm] * len(big) + [vm] * len(near),
+        scratch_shapes=[
+            VM((wrows, ws.shape[1]), bf16), VM((wrows, width), bf16), VM((wrows, 3 * width), bf16),
+            VM((wrows, hidden), bf16), VM((wrows, hidden), bf16),
+            VM((wrows, cross_width), bf16), VM((wrows // 4, width), bf16),
+            VM((rows, 3 * width), bf16), VM((att_rows, SEG_LEN), bf16), VM((rows, width), bf16),
+            VM((rows, width), f32), VM((rows, width), bf16), VM((rows, hidden), bf16),
+            VM((rows, hidden), bf16), VM((rows, width), bf16), VM((rows, width), bf16),
+            VM((32, total), bf16), VM((32, total), bf16), VM((ROWS, 4 * cross_width + width), bf16),
+            VM((2, 2, 2 * width), f32), VM((8, 2, 2 * width), f32), VM((leads, 2 * width), f32),
+            VM((4, 4, leads, width), bf16), VM((8, 2, 2 * width), f32), VM((leads, 3 * width // 4), f32),
+            DMA((n_units, 11)), DMA((n_units, 11)), DMA((parts,)), DMA((parts,)),
+            DMA((5,)), DMA((5,)), DMA, DMA((12,)),
+            DMA((8,)), DMA((8,)), DMA((4, 3)), DMA((4, 4)), DMA, DMA, DMA,
+        ],
+        compiler_params=pltpu.CompilerParams(
+            collective_id=0, has_side_effects=True, vmem_limit_bytes=60 * MIB
+        ),
+    )(wq, wo, wi, wb, ws, x, cot, mask)
+
+
+class Scatter:
+    def __init__(self, place, grad, off, width, out, index, sems, bufs, wide_a=True):
+        self.p, self.grad, self.off, self.out, self.m = place, grad, off, out, index
+        self.send, self.recv = sems
+        self.pair, self.r1a, self.r1b, self.rx, self.ry, self.r3, self.give = bufs
+        self.half = width // 2
+        self.a = split_half(width, wide_a)
+        self.b = self.half - self.a
+        self.sent = []
+        p = place
+        self.far = (1 - p.y) * 2 + 1 - p.x
+        self.groups = (self.far, p.xdp, p.ydp, p.dp)
+
+    def go(self, src, dst, slot, device):
+        copy = remote(src, dst, self.send.at[self.m, slot], self.recv.at[self.m, slot], device)
+        copy.start()
+        self.sent.append(copy)
+
+    def arrived(self, dst, slot):
+        remote(dst, dst, self.send.at[self.m, slot], self.recv.at[self.m, slot], self.p.sib).wait_recv()
+
+    def cols(self, part="AB", core=None):
+        at, size = {"A": (0, self.a), "B": (self.a, self.b), "AB": (0, self.half)}[part]
+        core = self.p.core if core is None else core
+        return lanes(self.off + core * self.half + at, size)
+
+    def group(self, dp):
+        return rows_at(dp * 4 * ROWS, 4 * ROWS, 16)
+
+    def side(self, dp, part="AB"):
+        return self.grad.at[self.group(dp), self.cols(part)]
+
+    def start(self):
+        p = self.p
+        for i, dp in enumerate(self.groups):
+            theirs = self.grad.at[self.group(dp), self.cols("AB", 1 - p.core)]
+            self.go(theirs, self.pair.at[self.group(dp)], i, p.sib)
+
+    def add(self, dp, part, other, other_row=0):
+        @pl.loop(0, 4)
+        def _(i):
+            key = (rows_at(dp * 4 * ROWS + i * ROWS, ROWS, 16), self.cols(part))
+            self.grad[key] = self.grad[key] + other[rows_at(other_row + i * ROWS, ROWS, 16), :]
+
+    def one(self):
+        p = self.p
+        for i, dp in enumerate(self.groups):
+            self.arrived(self.pair.at[self.group(dp)], i)
+            self.add(dp, "AB", self.pair, dp * 4 * ROWS)
+            if i == 0:
+                self.go(self.side(dp, "A"), self.r1a, 4, p.ynbr)
+                if self.b:
+                    self.go(self.side(dp, "B"), self.r1b, 5, p.xnbr)
+
+    def two(self):
+        p = self.p
+        self.arrived(self.r1a, 4)
+        self.add(p.xdp, "A", self.r1a)
+        self.go(self.side(p.xdp), self.rx, 6, p.xnbr)
+        if self.b:
+            self.arrived(self.r1b, 5)
+            self.add(p.ydp, "B", self.r1b)
+        self.go(self.side(p.ydp), self.ry, 7, p.ynbr)
+
+    def three(self):
+        p = self.p
+        self.arrived(self.rx, 6)
+        self.arrived(self.ry, 7)
+
+        @pl.loop(0, 4)
+        def _(i):
+            key = (rows_at(p.dp * 4 * ROWS + i * ROWS, ROWS, 16), self.cols())
+            own = rows_at(i * ROWS, ROWS, 16)
+            self.grad[key] = self.grad[key] + (self.rx[own, :] + self.ry[own, :])
+
+        for d in (1, 3, 2):
+            z = (p.z + d) % 4
+            src = self.grad.at[rows_at((p.dp * 4 + z) * ROWS, ROWS, 16), self.cols()]
+            self.go(src, self.r3.at[d - 1], 7 + d, p.at(p.dp, z, p.core))
+
+    def four(self):
+        p = self.p
+        for d in (1, 3, 2):
+            self.arrived(self.r3.at[d - 1], 7 + d)
+        rows = rows_at((p.dp * 4 + p.z) * ROWS, ROWS, 16)
+        total = self.grad[rows, self.cols()].astype(f32)
+        for d in range(3):
+            total = total + self.r3[d].astype(f32)
+        upper, lower = total[: ROWS // 2], total[ROWS // 2 :]
+        first = p.core == 0
+        self.give[...] = jnp.where(first, lower, upper)
+        self.out[:, self.cols()] = jnp.where(first, upper, lower)
+        self.go(self.give, self.out.at[:, self.cols()], 11, p.sib)
+
+    def five(self):
+        self.arrived(self.out.at[:, self.cols("AB", 1 - self.p.core)], 11)
+
+    def finish(self):
+        for copy in self.sent:
+            copy.wait_send()
+
+
+def split_half(width, wide_a):
+    tiles = width // 2 // LANES
+    return ((tiles + 1) // 2 if wide_a else max(tiles // 2, 1)) * LANES
+
+
+def scatter_buffers(width, wide_a):
+    half = width // 2
+    a = split_half(width, wide_a)
+    b = half - a
+    return [
+        VM((16 * ROWS, half), bf16),
+        VM((4 * ROWS, a), bf16),
+        VM((4 * ROWS if b else 16, max(b, LANES)), bf16),
+        VM((4 * ROWS, half), bf16),
+        VM((4 * ROWS, half), bf16),
+        VM((3, ROWS, half), bf16),
+        VM((ROWS // 2, half), f32),
+    ]
+
+
+SCATTER_LAGS = {"start": 0, "one": 1, "two": 2, "three": 3, "four": 4, "five": 5}
+FACTOR_LAGS = {"own": -2, "line": 0, "plane": 1, "last": 2, "drain": 3}
+
+
+def scatter_step(sums, jobs):
+    begun = len([s for s in sums.order[: sums.at] if s[0] == "start"])
+    follow = [i for i, s in enumerate(sums.order) if s == ("start", begun + 1)]
+    if begun < len(jobs):
+        sums.step((follow[0] if follow else sums.order.index(("start", begun)) + 1) - sums.at)
+
+
+def backward_kernel(*refs):
+    (
+        cot_ref, x_ref, home_ref, par_ref, r1_ref, r2_ref, z2_ref, fac_ref, csmall_ref,
+        p_hbm, a_hbm, c_hbm, nl_hbm, g_hbm, sl_hbm, z1_hbm, w_hbm, o_hbm, i_hbm, b_hbm,
+    ) = refs[:20]
+    gt_ref, gq_ref, go_ref, gi_ref, gb_ref, gs_ref = refs[20:26]
+    (
+        pk, at, cx, nl, g, sl, z1, qw, ow, fw,
+        h, df, tr, tr2, dwb, dwi, dwo, dwq, dws, small,
+        sib_buf, full, tmp,
+        f_send, f_recv, pair_send, pair_recv, load, rs_send, rs_recv,
+    ) = refs[26:56]
+    bufs = refs[56:]
+    p = Place()
+    rows, width = x_ref.shape
+    segs = rows // SEG_LEN
+    hidden = g.shape[1]
+    pairs = width // LANES
+    tile = 256
+    chunks = hidden // tile
+
+    loads = {}
+    order = [
+        ("g", g_hbm, g), ("b", b_hbm, fw), ("sl", sl_hbm, sl), ("nl", nl_hbm, nl), ("z1", z1_hbm, z1),
+        ("c", c_hbm, cx), ("o", o_hbm, ow), ("p", p_hbm, pk), ("a", a_hbm, at), ("w", w_hbm, qw),
+        ("i", i_hbm, fw),
+    ]
+    for i, (name, src, dst) in enumerate(order):
+        loads[name] = pltpu.make_async_copy(src, dst, load.at[i])
+    for name, _, _ in order[:-1]:
+        loads[name].start()
+    greet(gather_peers(p))
+
+    lead = fac_ref.shape[0]
+    lead2 = 2 * lead
+    key_f = rows_at((p.dp * 4 + p.z) * lead2, lead2, 16)
+    swap = remote(fac_ref, sib_buf, pair_send, pair_recv, p.sib)
+    swap.start()
+
+    class Factor(Gather):
+        def __init__(self, i):
+            mine = lambda z: full.at[key_f, self.cols(p.core)]
+            super().__init__(p, full, i * width, width, mine, i, (f_send, f_recv), lead2, i % 2 == 0)
+
+    factors = Staged([Factor(i) for i in range(4)], staggered(4, FACTOR_LAGS))
+
+    def factor_own():
+        swap.wait_recv()
+        base = (p.dp * 4 + p.z) * lead2
+        for i in range(4):
+            cols = lanes(i * width + p.core * (width // 2), width // 2)
+            full[rows_at(base + p.core * lead, lead, 16), cols] = fac_ref[:, cols]
+            full[rows_at(base + (1 - p.core) * lead, lead, 16), cols] = sib_buf[:, cols]
+
+    def factor_grads():
+        slab = width // 4
+
+        def rows_of(z, at_col, size):
+            return jnp.concatenate(
+                [full[rows_at((i * 4 + z) * lead2, lead2, 16), pl.ds(at_col, size)] for i in range(4)],
+                axis=0,
+            )
+
+        base = 2 * width + 3 * slab
+        own = rows_at(p.fsdp * (ROWS // 2), ROWS // 2, 8)
+        xl = rows_of(p.dp, base + slab, slab)
+        nlf = rows_of(p.dp, base + 2 * slab, slab)
+        dff = rows_of(p.dp, base + 3 * slab, slab)
+        ctx = rows_of(p.dp, base + 4 * slab, slab)
+        for z in range(4):
+            tmp[:, :width] = mm(dff, rows_of(z, 0, width), TN)
+            gb_ref[1, :, z * width : (z + 1) * width] = tmp[own, :width]
+            tmp[:, :width] = mm(nlf, rows_of(z, width, width), TN)
+            gi_ref[1, :, z * width : (z + 1) * width] = tmp[own, :width]
+            tmp[:, : 3 * slab] = mm(xl, rows_of(z, 2 * width, 3 * slab), TN)
+            got = tmp[own, : 3 * slab]
+            for j in range(3):
+                spot = j * width + z * slab
+                gq_ref[1, :, spot : spot + slab] = got[:, j * slab : (j + 1) * slab]
+            tmp[:, :slab] = mm(ctx, rows_of(z, base, slab), TN)
+            go_ref[1, :, z * slab : (z + 1) * slab] = tmp[own, :slab]
+
+    jobs = []
+    for i, (grad, off, size, dst) in enumerate(
+        [(dwb, i * width, width, gb_ref.at[0]) for i in range(hidden // width)]
+        + [(dwi, i * width, width, gi_ref.at[0]) for i in range(hidden // width)]
+        + [(dwo, 0, width, go_ref.at[0]), (dws, 0, dws.shape[1], gs_ref)]
+        + [(dwq, i * width, width, gq_ref.at[0]) for i in range(3)]
+    ):
+        jobs.append(
+            Scatter(p, grad, off, size, dst, i, (rs_send, rs_recv), bufs[7 * i : 7 * i + 7], i % 2 == 0)
+        )
+    sums = Staged(jobs, staggered(len(jobs), SCATTER_LAGS))
+
+    block_rows = 64
+
+    def norm_back(z_ref, r_ref, gain_row, low_ref, sums):
+        def step(i, acc):
+            key = rows_at(i * block_rows, block_rows, 16)
+            dy = h[key, :]
+            z = z_ref[key, :].astype(f32)
+            r = jnp.concatenate([r_ref[key, :]] * (width // LANES), axis=1)
+            e = dy * par_ref[gain_row : gain_row + 1, :]
+            first = jnp.mean(e, axis=-1, keepdims=True)
+            second = jnp.mean(e * z, axis=-1, keepdims=True)
+            d = r * (e - first - z * second)
+            h[key, :] = d
+            low_ref[key, :] = d.astype(bf16)
+            fold = lambda v: jnp.sum(v.reshape(block_rows // 8, 8, width), axis=0)
+            return acc[0] + fold(dy * z), acc[1] + fold(dy)
+
+        zero = jnp.zeros((8, width), f32)
+        gain, bias = lax.fori_loop(0, rows // block_rows, step, (zero, zero))
+        small[sums : sums + 1, :] = jnp.sum(gain, axis=0, keepdims=True)
+        small[sums + 2 : sums + 3, :] = jnp.sum(bias, axis=0, keepdims=True)
+
+    def turn(tr, ref):
+        @pl.loop(0, width // tile)
+        def _(i):
+            tr[rows_at(i * tile, tile, 16), :] = ref[:, lanes(i * tile, tile)].T
+
+    def outer(dst, tr, src, part):
+        @pl.loop(part * (width // tile), (part + 1) * (width // tile))
+        def _(i):
+            cols = lanes(i * tile, tile)
+            dst[:, cols] = mm(tr[...], src[:, cols], NN).astype(bf16)
+
+    def norm_two():
+        @pl.loop(0, rows // block_rows)
+        def _(i):
+            key = rows_at(i * block_rows, block_rows, 16)
+            h[key, :] = cot_ref[key, :].astype(f32)
+
+        for s in range(segs):
+            h[s * SEG_LEN : s * SEG_LEN + 1, :] = home_ref[s // 2, s % 2 : s % 2 + 1, width:]
+        small[...] = jnp.zeros_like(small)
+        small[4:8, :] = csmall_ref[0:4, :]
+        for s in range(2):
+            row = home_ref[0, s : s + 1, width:] + home_ref[1, s : s + 1, width:]
+            small[pl.ds(8 + p.fsdp * 2 + s, 1), :] = row
+        norm_back(z2_ref, r2_ref, 1, df, 1)
+        turn(tr, df)
+
+    def active_back(first, count):
+        @pl.loop(first, first + count)
+        def _(i):
+            cols = lanes(i * tile, tile)
+            d = mm(df[...], fw[:, cols], NN) * sl[:, cols].astype(f32)
+            sl[:, cols] = d.astype(bf16)
+
+    def add_back(src, weight):
+        @pl.loop(0, width // tile)
+        def _(i):
+            h[:, lanes(i * tile, tile)] += mm(src[...], weight[rows_at(i * tile, tile, 16), :], NT)
+
+    def context_back():
+        @pl.loop(0, width // tile)
+        def _(i):
+            d = mm(df[...], ow[rows_at(i * tile, tile, 16), :], NT)
+            cx[:, lanes(i * tile, tile)] = d.astype(bf16)
+
+    def attend_back(s):
+        key = pl.ds(s * SEG_LEN, SEG_LEN)
+        factor = (LANES // 2) ** (-0.5)
+
+        @pl.loop(0, pairs)
+        def _(j):
+            a = at[rows_at((s * pairs + j) * 2 * SEG_LEN, 2 * SEG_LEN, 16), :]
+            q_cols = lanes(j * LANES, LANES)
+            k_cols = lanes(width + j * LANES, LANES)
+            v_cols = lanes(2 * width + j * LANES, LANES)
+            qs = jnp.concatenate(lane_halves(pk[key, q_cols]), axis=0)
+            ks = jnp.concatenate(lane_halves(pk[key, k_cols]), axis=0)
+            ds_in = jnp.concatenate(lane_halves(cx[key, q_cols]), axis=0)
+            da = mm(ds_in, pk[key, v_cols], NT)
+            af = a.astype(f32)
+            ds = (af * (da - jnp.sum(af * da, axis=-1, keepdims=True))).astype(bf16)
+            dv = mm(a, ds_in, TN)
+            both = jnp.concatenate([ds[:SEG_LEN], ds[SEG_LEN:]], axis=1)
+            dq = mm(both, ks, NN) * factor
+            dk = mm(ds, qs, TN) * factor
+            pk[key, q_cols] = dq.astype(bf16)
+            pk[key, k_cols] = dk.astype(bf16)
+            pk[key, v_cols] = dv.astype(bf16)
+
+    def result():
+        @pl.loop(0, width // tile)
+        def _(i):
+            cols = lanes(i * tile, tile)
+            d = h[:, cols] + mm(pk[...], qw[rows_at(i * tile, tile, 16), :], NT)
+            gt_ref[:, cols] = d.astype(bf16)
+
+    def smalls():
+        dws[:, :LANES] = small[...].T.astype(bf16)
+        dws[:, LANES:] = jnp.zeros((dws.shape[0], LANES), bf16)
+
+    per = hidden // width
+    factor_own()
+    factors.step(3)
+    norm_two()
+    factors.step(3)
+    loads["g"].wait()
+    for i in range(per):
+        outer(dwb, tr, g, i)
+        scatter_step(sums, jobs)
+        factors.step(3)
+    loads["b"].wait()
+    loads["sl"].wait()
+    active_back(0, chunks // 2)
+    factors.step(3)
+    active_back(chunks // 2, chunks - chunks // 2)
+    loads["i"].start()
+    loads["nl"].wait()
+    turn(tr, nl)
+    outer(dwi, tr, sl, 0)
+    scatter_step(sums, jobs)
+    loads["i"].wait()
+    add_back(sl, fw)
+    outer(dwi, tr, sl, 1)
+    scatter_step(sums, jobs)
+    loads["z1"].wait()
+    norm_back(z1, r1_ref, 0, df, 0)
+    smalls()
+    for i in range(2, per - 1):
+        outer(dwi, tr, sl, i)
+        scatter_step(sums, jobs)
+    loads["c"].wait()
+    turn(tr2, cx)
+    loads["o"].wait()
+    outer(dwo, tr2, df, 0)
+    context_back()
+    loads["p"].wait()
+    loads["a"].wait()
+    attend_back(0)
+    outer(dwi, tr, sl, per - 1)
+    scatter_step(sums, jobs)
+    attend_back(1)
+    scatter_step(sums, jobs)
+    attend_back(2)
+    scatter_step(sums, jobs)
+    attend_back(3)
+    turn(tr2, x_ref)
+    for i in range(3):
+        outer(dwq, tr2, pk, i)
+        scatter_step(sums, jobs)
+    loads["w"].wait()
+    result()
+    factors.finish()
+    factor_grads()
+    sums.finish()
+    swap.wait_send()
+
+
+def segment_backward(near, far):
+    cot, x = near[0], near[1]
+    rows, width = x.shape
+    packed, att, context, nl, g = far[:5]
+    hidden = g.shape[1]
+    hbm, vm = pl.BlockSpec(memory_space=pl.ANY), pl.BlockSpec(memory_space=VM)
+    arr = jax.ShapeDtypeStruct
+    own = ROWS // 2
+    lead = near[7].shape[0]
+    like = lambda v: VM(v.shape, v.dtype)
+    wrows = 16 * ROWS
+    widths = [width] * (2 * (hidden // width) + 1) + [256] + [width] * 3
+    bufs = []
+    for i, w in enumerate(widths):
+        bufs += scatter_buffers(w, i % 2 == 0)
+    DMA = pltpu.SemaphoreType.DMA
+    return pl.pallas_call(
+        backward_kernel,
+        out_shape=[
+            arr((rows, width), bf16),
+            arr((2, own, 3 * width), f32),
+            arr((2, own, width), f32),
+            arr((2, own, hidden), f32),
+            arr((2, own, hidden), f32),
+            arr((own, 256), f32),
+        ],
+        in_specs=[vm] * len(near) + [hbm] * len(far),
+        out_specs=[vm] * 6,
+        scratch_shapes=[
+            like(packed), like(att), like(context), like(nl), like(g), like(g), like(nl),
+            VM((wrows, 3 * width), bf16), VM((wrows, width), bf16), VM((wrows, hidden), bf16),
+            VM((rows, width), f32), VM((rows, width), bf16), VM((width, rows), bf16), VM((width, rows), bf16),
+            VM((wrows, hidden), bf16), VM((wrows, hidden), bf16), VM((wrows, width), bf16),
+            VM((wrows, 3 * width), bf16), VM((wrows, 256), bf16), VM((LANES, width), f32),
+            VM((lead, 4 * width), bf16), VM((32 * lead, 4 * width), bf16), VM((width // 4, width), f32),
+            DMA((4, 11)), DMA((4, 11)), DMA, DMA, DMA((11,)), DMA((len(widths), 12)), DMA((len(widths), 12)),
+        ]
+        + bufs,
+        compiler_params=pltpu.CompilerParams(
+            collective_id=1, has_side_effects=True, vmem_limit_bytes=63 * MIB
+        ),
+    )(*near, *far)
 
 
 def matmul(left, right, form):
@@ -292,14 +1463,6 @@
         pos_embed, w_qkv, w_out, w_in, w_back, norm_gain, norm_bias
     )
     output, kept = layer_forward(tokens, doc_ids, seg_weights, cross_weights, pos_full)
-    shards = lax.optimization_barrier(
-        (output, tokens, pos_embed, w_qkv, w_out, w_in, w_back, norm_gain, norm_bias)
-    )
-    seg_weights = gather_segment(shards[3], shards[4], shards[5], shards[6], shards[7], shards[8])
-    cross_weights, pos_full = gather_cross(
-        shards[2], shards[3], shards[4], shards[5], shards[6], shards[7], shards[8]
-    )
-    recomputed, kept = layer_forward(shards[1], doc_ids, seg_weights, cross_weights, pos_full)
     grad_tokens, seg_factors, cross_factors, seg_smalls, cross_smalls, grad_pos = layer_backward(
         cotangent, doc_ids, kept, seg_weights, cross_weights
     )
@@ -336,9 +1499,44 @@
     )
 
 
+def fast_body(tokens, doc_ids, pos_embed, w_qkv, w_out, w_in, w_back, norm_gain, norm_bias, cotangent):
+    nrows, local_len, width = tokens.shape
+    rows = nrows * local_len
+    segs = rows // SEG_LEN
+    hidden = w_in.shape[2]
+    items = jnp.concatenate([norm_gain[0], norm_bias[0], norm_gain[1], norm_bias[1], pos_embed], axis=0)
+    small = jnp.pad(items.T, ((0, 0), (0, 256 - items.shape[0])))
+    x = tokens.reshape(rows, width)
+    cot = cotangent.reshape(rows, width)
+    own_row = lax.dynamic_index_in_dim(doc_ids, lax.axis_index("fsdp") % 2, 0, keepdims=False)
+    mask = (own_row[:, None] == own_row[None, :]).astype(f32)
+    (
+        s_qkv, s_in, s_out, s_back,
+        packed, att, context, nl, act, slope, z_one, z_two,
+        output, par, r_one, r_two, home, fac, cross_small,
+    ) = segment_forward(small, w_qkv, w_out, w_in, jnp.swapaxes(w_back, 1, 2), x, cot, mask)
+    grad_tokens, g_qkv, g_out, g_in, g_back, t_small = segment_backward(
+        (cot, x, home, par, r_one, r_two, z_two, fac, cross_small),
+        (packed, att, context, nl, act, slope, z_one, s_qkv, s_out, s_in, s_back),
+    )
+    s = t_small.T
+    return (
+        output.reshape(tokens.shape),
+        grad_tokens.reshape(tokens.shape),
+        s[8 : 8 + doc_ids.shape[1]],
+        g_qkv,
+        g_out,
+        g_in,
+        jnp.swapaxes(g_back, 1, 2),
+        jnp.stack([s[0:2], s[4:6]]),
+        jnp.stack([s[2:4], s[6:8]]),
+    )
+
+
 def solution(mesh):
+    fast = dict(mesh.shape) == {"dp": 4, "fsdp": 8}
     return jax.shard_map(
-        body,
+        fast_body if fast else body,
         mesh=mesh,
         in_specs=(
             P("dp", "fsdp", None),

time: 1830 us -> 251 us (0.14)
  waiting for transfers between devices: 1050 us -> 0 us
  blocking collectives: 430 us -> 0 us
  Pallas kernels: 0 us -> 236 us
  matrix products: 160 us -> 0 us
  other arithmetic: 77.5 us -> 1.28 us
  local copies, waits for them, and re-layouts: 82.3 us -> 12.7 us
    reduce_scatter x2 -> x0, waiting for transfers between devices: 539 us -> none  [the longest x1 271 us: body(): lax.psum_scatter(weight_terms(cross_factors), ('dp', 'fsdp'), scatter_dim...]
    all_gather x12 -> x0, blocking collectives: 430 us -> none  [the longest x2 84.7 us: gather_segment(): lax.all_gather(norm_bias[0], ('dp', 'fsdp'), axis=1, tiled=True)]
    all_gather x16 -> x0, waiting for transfers between devices: 404 us -> none  [the longest x2 128 us: gather_cross(): lax.all_gather(w_in[1], ('dp', 'fsdp'), axis=0, tiled=True)]
    pallas_call x0 -> x2, Pallas kernels: none -> 236 us  [the longest x1 128 us: segment_forward(): pl.pallas_call(forward_kernel, out_shape=big + near, in_specs=[vm] * 8, o...]
    dot_general x47 -> x0, matrix products: 156 us -> none  [matmul(): return jnp.einsum(form, left, right, preferred_element_type=jnp.float32)]
    unnamed x22 -> x0, waiting for transfers between devices: 106 us -> none
    slice x38 -> x6, local copies, waits for them, and re-layouts: 50.4 us -> 2.14 us  [the longest x2 1 us: fast_body(): s[2:4]]
    concatenate x4 -> x0, other arithmetic: 39.3 us -> none  [the longest x2 37.6 us: weight_terms(): return jnp.concatenate([term_qkv, term_out, term_in, term_back], axis=1)]
  transfers between devices with their start and end apart: 20 -> 0, of which waited for: 12 -> 0; matrix products, arithmetic and copies ran while one was open for 13% -> 0% of each run, Pallas kernels for 0% -> 0%
where the time goes in v3:
time: 251 us; the launch traced here: 250 us
  Pallas kernels  236 us (94%)
  local copies, waits for them, and re-layouts  12.7 us (5%)
    pallas_call x1, Pallas kernels, segment_forward(): pl.pallas_call(forward_kernel, out_shape=big + near, in_specs=[vm] * 8, o...  128 us
    pallas_call x1, Pallas kernels, segment_backward(): pl.pallas_call(backward_kernel, out_shape=[arr((rows, width), bf16), arr(...  108 us
    unnamed x20, local copies, waits for them, and re-layouts  8.12 us

profile of v3, /device:TPU:1, one launch (start us, length us, event | category | flops | bytes accessed | tf_op | source)
XLA Modules:
  0.0 250.5 jit_solution(380716104524016535)
XLA Ops:
  0.6 0.0 copy-start
  0.7 0.7 copy-done
  1.3 0.7 slice_bitcast_fusion.1
  2.0 0.7 slice_bitcast_fusion
  2.7 0.1 copy.22
  2.8 0.1 copy.21
  2.9 0.1 copy.20
  3.0 0.1 copy.19
  3.1 0.8 copy.23
  3.8 0.1 concatenate.3
  3.9 0.6 pad.4.refs_4_
  4.6 0.7 compare_convert_fusion.refs_7_
  5.2 127.9 %shard_map.169 = (bf16[768,2304]{1,0:T(8,128)(2,1)}, bf16[768,3072]{1,0:T(8,128)(2,1)}, bf16[768,768]{1,0:T(8,128)(2,1)}, bf16[768,3072]{1,0:T(8,128)(2,1)}, bf1...) custom-call(bf16[2,24,2304]{2,1,0:T(8,128)(2,1)} %refs_0_.1, ...), custom_call_target="tpu_custom_call" | custom-call | tf_op jit(solution)/shard_map/pallas_call | solution.py:733
  133.1 107.9 %shard_map.170 = (bf16[512,768]{1,0:T(8,128)(2,1)}, f32[2,24,2304]{2,1,0:T(8,128)}, f32[2,24,768]{2,1,0:T(8,128)}, f32[2,24,3072]{2,1,0:T(8,128)}, f32[2,24,3072]{2,1,0:T(8,128)}, /*index=5*/f32[24,256]{1,0:T(8,128)}) custom-call(bf16[512,768]{1,0:T(8,128)(2,1)} %bitcast.25, bf16[512,768]{1,0:T(8,128)(2,1)} %bitcast.23, ...), custom_call_target="tpu_custom_call" | custom-call | tf_op jit(solution)/shard_map/pallas_call | solution.py:1160
  241.0 0.0 copy-start.4
  241.0 0.0 copy-start.5
  241.0 0.0 copy-start.3
  241.0 0.0 copy-start.2
  241.0 0.9 slice.36
  241.9 0.7 copy.28
  242.6 0.9 fusion
  243.5 0.1 copy.26
  243.6 0.1 copy.27
  243.7 0.1 copy.25
  243.8 0.1 copy.24
  243.9 0.6 pad_maximum_fusion
  244.5 0.9 copy.35
  245.3 2.1 copy.36
  247.4 0.8 copy.37
  248.2 0.7 copy.38
  248.8 0.8 copy.39
  249.7 0.8 copy.40
  (7 shorter events, 0.0 us)
Async XLA Ops:
  0.6 0.7 copy-start
  133.1 111.4 %copy-start.1 = (bf16[512,768]{1,0:T(8,128)(2,1)S(1)}, bf16[512,768]{1,0:T(8,128)(2,1)}, u32[]{:S(2)}) copy-start(bf16[512,768]{1,0:T(8,128)(2,1)} %get-tuple-element.34) | copy-start | bytes 2359300
  241.0 6.4 %copy-start.4 = (f32[2,24,2304]{2,1,0:T(8,128)S(1)}, f32[2,24,2304]{2,1,0:T(8,128)}, u32[]{:S(2)}) copy-start(f32[2,24,2304]{2,1,0:T(8,128)} %get-tuple-element.90) | copy-start | bytes 1327108
  241.0 7.2 %copy-start.5 = (f32[2,24,768]{2,1,0:T(8,128)S(1)}, f32[2,24,768]{2,1,0:T(8,128)}, u32[]{:S(2)}) copy-start(f32[2,24,768]{2,1,0:T(8,128)} %get-tuple-element.91) | copy-start | bytes 442372
  241.0 7.8 %copy-start.3 = (f32[2,24,3072]{2,1,0:T(8,128)S(1)}, f32[2,24,3072]{2,1,0:T(8,128)}, u32[]{:S(2)}) copy-start(f32[2,24,3072]{2,1,0:T(8,128)} %get-tuple-element.92) | copy-start | bytes 1769476
  241.0 8.6 %copy-start.2 = (f32[2,24,3072]{2,1,0:T(8,128)S(1)}, f32[2,24,3072]{2,1,0:T(8,128)}, u32[]{:S(2)}) copy-start(f32[2,24,3072]{2,1,0:T(8,128)} %get-tuple-element.58) | copy-start | bytes 1769476

commit v4 on v3

--- a/solution.py
+++ b/solution.py
@@ -254,21 +254,161 @@
     return head + [s for s in tail if s not in done and s[1] < n]
 
 
-def forward_kernel(*refs):
+class Scatter:
+    def __init__(self, place, grad, off, width, out, index, sems, bufs, wide_a=True):
+        self.p, self.grad, self.off, self.out, self.m = place, grad, off, out, index
+        self.send, self.recv = sems
+        self.pair, self.r1a, self.r1b, self.rx, self.ry, self.r3, self.give = bufs
+        self.half = width // 2
+        self.a = split_half(width, wide_a)
+        self.b = self.half - self.a
+        self.sent = []
+        self.free, self.waits, self.frees = None, False, False
+        p = place
+        self.far = (1 - p.y) * 2 + 1 - p.x
+        self.groups = (self.far, p.xdp, p.ydp, p.dp)
+
+    def go(self, src, dst, slot, device):
+        copy = remote(src, dst, self.send.at[self.m, slot], self.recv.at[self.m, slot], device)
+        copy.start()
+        self.sent.append(copy)
+
+    def arrived(self, dst, slot):
+        remote(dst, dst, self.send.at[self.m, slot], self.recv.at[self.m, slot], self.p.sib).wait_recv()
+
+    def cols(self, part="AB", core=None):
+        at, size = {"A": (0, self.a), "B": (self.a, self.b), "AB": (0, self.half)}[part]
+        core = self.p.core if core is None else core
+        return lanes(self.off + core * self.half + at, size)
+
+    def group(self, dp):
+        return rows_at(dp * 4 * ROWS, 4 * ROWS, 16)
+
+    def side(self, dp, part="AB"):
+        return self.grad.at[self.group(dp), self.cols(part)]
+
+    def start(self):
+        p = self.p
+        if self.waits:
+            pl.semaphore_wait(self.free, 1)
+        for i, dp in enumerate(self.groups):
+            theirs = self.grad.at[self.group(dp), self.cols("AB", 1 - p.core)]
+            self.go(theirs, self.pair.at[self.group(dp)], i, p.sib)
+
+    def add(self, dp, part, other, other_row=0):
+        @pl.loop(0, 4)
+        def _(i):
+            key = (rows_at(dp * 4 * ROWS + i * ROWS, ROWS, 16), self.cols(part))
+            self.grad[key] = self.grad[key] + other[rows_at(other_row + i * ROWS, ROWS, 16), :]
+
+    def one(self):
+        p = self.p
+        for i, dp in enumerate(self.groups):
+            self.arrived(self.pair.at[self.group(dp)], i)
+            self.add(dp, "AB", self.pair, dp * 4 * ROWS)
+            if i == 0:
+                self.go(self.side(dp, "A"), self.r1a, 4, p.ynbr)
+                if self.b:
+                    self.go(self.side(dp, "B"), self.r1b, 5, p.xnbr)
+        if self.frees:
+            pl.semaphore_signal(self.free, inc=1, device_id=p.sib, device_id_type=MESH)
+
+    def two(self):
+        p = self.p
+        self.arrived(self.r1a, 4)
+        self.add(p.xdp, "A", self.r1a)
+        self.go(self.side(p.xdp), self.rx, 6, p.xnbr)
+        if self.b:
+            self.arrived(self.r1b, 5)
+            self.add(p.ydp, "B", self.r1b)
+        self.go(self.side(p.ydp), self.ry, 7, p.ynbr)
+
+    def three(self):
+        p = self.p
+        self.arrived(self.rx, 6)
+        self.arrived(self.ry, 7)
+
+        @pl.loop(0, 4)
+        def _(i):
+            key = (rows_at(p.dp * 4 * ROWS + i * ROWS, ROWS, 16), self.cols())
+            own = rows_at(i * ROWS, ROWS, 16)
+            self.grad[key] = self.grad[key] + (self.rx[own, :] + self.ry[own, :])
+
+        for d in (1, 3, 2):
+            z = (p.z + d) % 4
+            src = self.grad.at[rows_at((p.dp * 4 + z) * ROWS, ROWS, 16), self.cols()]
+            self.go(src, self.r3.at[d - 1], 7 + d, p.at(p.dp, z, p.core))
+
+    def four(self):
+        p = self.p
+        for d in (1, 3, 2):
+            self.arrived(self.r3.at[d - 1], 7 + d)
+        rows = rows_at((p.dp * 4 + p.z) * ROWS, ROWS, 16)
+        total = self.grad[rows, self.cols()].astype(f32)
+        for d in range(3):
+            total = total + self.r3[d].astype(f32)
+        upper, lower = total[: ROWS // 2], total[ROWS // 2 :]
+        first = p.core == 0
+        self.give[...] = jnp.where(first, lower, upper)
+        self.out[:, self.cols()] = jnp.where(first, upper, lower)
+        self.go(self.give, self.out.at[:, self.cols()], 11, p.sib)
+
+    def five(self):
+        self.arrived(self.out.at[:, self.cols("AB", 1 - self.p.core)], 11)
+
+    def finish(self):
+        for copy in self.sent:
+            copy.wait_send()
+
+
+def split_half(width, wide_a):
+    tiles = width // 2 // LANES
+    return ((tiles + 1) // 2 if wide_a else max(tiles // 2, 1)) * LANES
+
+
+def scatter_buffers(width, wide_a):
+    half = width // 2
+    a = split_half(width, wide_a)
+    b = half - a
+    return [
+        VM((4 * ROWS, a), bf16),
+        VM((4 * ROWS if b else 16, max(b, LANES)), bf16),
+        VM((4 * ROWS, half), bf16),
+        VM((4 * ROWS, half), bf16),
+        VM((3, ROWS, half), bf16),
+        VM((ROWS // 2, half), f32),
+    ]
+
+
+SCATTER_LAGS = {"start": 0, "one": 1, "two": 2, "three": 3, "four": 4, "five": 5}
+PAIR_SLOTS = 4
+
+
+def tail_units(width):
+    return [(0, width), (width, width), (2 * width, width - 256), (3 * width - 256, 256)]
+
+
+def scatter_step(sums, jobs):
+    begun = len([s for s in sums.order[: sums.at] if s[0] == "start"])
+    follow = [i for i, s in enumerate(sums.order) if s == ("start", begun + 1)]
+    if begun < len(jobs):
+        sums.step((follow[0] if follow else sums.order.index(("start", begun)) + 1) - sums.at)
+
+
+def layer_kernel(*refs):
     wq_ref, wo_ref, wi_ref, wb_ref, ws_ref, x_ref, cot_ref, mask_ref = refs[:8]
-    (
-        w_hbm, i_hbm, o_hbm, b_hbm,
-        p_hbm, a_hbm, c_hbm, nl_hbm, g_hbm, sl_hbm, z1_hbm, z2_hbm,
-        y_ref, par_ref, r1_ref, r2_ref, home_ref, fac_ref, small_ref,
-    ) = refs[8:27]
+    y_ref, gt_ref, gq_ref, go_ref, gi_ref, gb_ref, gs_ref = refs[8:15]
     (
         sw, ow, qw, iw, bw, cw, cwo,
-        pk, at, cx, h, nl, g, sl, z1, z2,
+        pk, at, cx, h, nl, g, sl, z1, z2, r1_ref, r2_ref, par_ref,
         own_buf, sib_buf, block,
-        lead_out, gbuf, lead, xbuf, ybuf, dpack,
-        s_send, s_recv, pair_send, pair_recv, wo_send, wo_recv, local, out_sem,
+        lead_out, gbuf, lead, xbuf, ybuf, dpack, home_ref, fac, fac_sib, csmall,
+        df, tr, tr2, dws, small, full, tmp, ring, pair_wide, pair_small,
+        s_send, s_recv, pair_send, pair_recv, wo_send, wo_recv, local,
         g_send, g_recv, x_send, x_recv, h_send, h_recv, lead_sem,
-    ) = refs[27:]
+        f_send, f_recv, swap_send, swap_recv, rs_send, rs_recv, free,
+    ) = refs[15:78]
+    bufs = refs[78:]
     p = Place()
     rows, width = x_ref.shape
     segs = rows // SEG_LEN
@@ -440,13 +580,6 @@
             def _():
                 wo_copy(i).wait_send()
 
-    kept = []
-
-    def keep(src, dst):
-        copy = pltpu.make_async_copy(src, dst, out_sem.at[len(kept)])
-        copy.start()
-        kept.append(copy)
-
     tile = 256
 
     def params():
@@ -529,460 +662,253 @@
         i = 2 * z + j
         return remote(lead_out.at[j], gbuf.at[p.fsdp], g_send.at[i], g_recv.at[p.fsdp], (p.dp, i))
 
-    per = hidden // width
-    head = width // HEADS
-    heads = HEADS // 4
-    n_tiles = width // tile
-    need(0)
-    params()
-    for i in range(3):
-        need(1 + i)
-        project(i * n_tiles, n_tiles)
-    for s in range(segs):
-        attend(s)
-        comm.upto("drain", 4 + s)
-    keep(qw, w_hbm), keep(pk, p_hbm), keep(at, a_hbm), keep(cx, c_hbm)
-    branch()
-    keep(ow, o_hbm), keep(nl, nl_hbm), keep(z1, z1_hbm)
-    for i in range(per):
-        need(8 + i)
-        feed_in(i * n_tiles, n_tiles)
-    wo_start()
-    keep(iw, i_hbm), keep(g, g_hbm), keep(sl, sl_hbm)
-    for i in range(per):
-        need(5 + per + i)
-        feed_back(i)
-    finish_block()
-    keep(bw, b_hbm), keep(z2, z2_hbm)
-    leaders()
-    for d in range(4):
-        z = (p.z + d) % 4
-        for j in range(2):
-            if d:
-                lead_copy(z, j).start()
-            else:
-
-                @pl.when(p.core != j)
-                def _():
-                    lead_copy(z, j).start()
-
-                @pl.when(p.core == j)
-                def _():
-                    mine = pltpu.make_async_copy(lead_out.at[j], gbuf.at[p.fsdp], lead_sem)
-                    mine.start()
-                    mine.wait()
-
-    need(n_seg)
-    wo_middle()
-    for d in range(1, 8):
-        i = lax.rem(p.fsdp + d, 8)
-        remote(gbuf.at[i], gbuf.at[i], g_send.at[i], g_recv.at[i], p.sib).wait_recv()
-    for i in range(8):
-        lead[2 * i : 2 * i + 2, :] = gbuf[i]
-    states = lead[:, :width]
-    cot = lead[:, width:]
-
-    def sum_z(e, partial_sum):
-        xbuf[e, p.z] = partial_sum.astype(bf16)
-        copies = []
-        for d in (1, 3, 2):
-            z = (p.z + d) % 4
-            copy = remote(
-                xbuf.at[e, p.z], xbuf.at[e, p.z], x_send.at[e, d - 1], x_recv.at[e, p.z],
-                p.at(p.dp, z, p.core),
-            )
-            copy.start()
-            copies.append(copy)
-        for d in (1, 3, 2):
-            z = (p.z + d) % 4
-            piece = xbuf.at[e, z]
-            remote(piece, piece, x_send.at[e, d - 1], x_recv.at[e, z], p.sib).wait_recv()
-        for copy in copies:
-            copy.wait_send()
-        return sum(xbuf[e, z].astype(f32) for z in range(4))
-
-    gain0, gain1 = par_ref[4:5, :], par_ref[5:6, :]
-    bias0, bias1 = par_ref[6:7, :], par_ref[7:8, :]
-    in_cols, back_cols = pl.ds(width, width), pl.ds(2 * width, width)
-    qkv_cols = pl.ds(0, 3 * slab)
-    factor = head ** (-0.5)
-    allowed = mask_ref[...] > 0.5
-
-    xl = states.astype(bf16)
-    packed = mm(xl, cw[:, qkv_cols], NN).astype(bf16)
-    q = [packed[:, i * head : (i + 1) * head] for i in range(heads)]
-    k = [packed[:, slab + i * head : slab + (i + 1) * head] for i in range(heads)]
-    v = [packed[:, 2 * slab + i * head : 2 * slab + (i + 1) * head] for i in range(heads)]
-    att, context = [], []
-    for i in range(heads):
-        scores = jnp.where(allowed, mm(q[i], k[i], NT) * factor, NEG)
-        top = jnp.max(scores, axis=-1, keepdims=True)
-        terms = jnp.exp(scores - top)
-        a = terms / jnp.sum(terms, axis=-1, keepdims=True)
-        att.append(a)
-        context.append(mm(a.astype(bf16), v[i], NN))
-    context = jnp.concatenate(context, axis=1).astype(bf16)
-    wo_finish()
-    branch = sum_z(0, mm(context, cwo[...], NN))
-    normed, z_one, r_one = norm_rows(states + branch, gain0, bias0)
-    nl = normed.astype(bf16)
-    need(n_seg + 1)
-    hidden = mm(nl, cw[:, in_cols], NN)
-    phi, slope = gelu_parts(hidden)
-    active = (hidden * phi).astype(bf16)
-    need(n_seg + 2)
-    feed = sum_z(1, mm(active, cw[:, back_cols], NT))
-    result, z_two, r_two = norm_rows(normed + feed, gain1, bias1)
-    d_two = norm_rows_back(cot, z_two, r_two, gain1)
-    df = d_two.astype(bf16)
-    du = (mm(df, cw[:, back_cols], NN) * slope).astype(bf16)
-    d_normed = d_two + sum_z(2, mm(du, cw[:, in_cols], NT))
-    d_one = norm_rows_back(d_normed, z_one, r_one, gain0)
-    db = d_one.astype(bf16)
-    dc = mm(db, cwo[...], NT).astype(bf16)
-    for i in range(heads):
-        a = att[i]
-        dci = dc[:, i * head : (i + 1) * head]
-        da = mm(dci, v[i], NT)
-        dv = mm(a.astype(bf16), dci, TN)
-        ds = (a * (da - jnp.sum(a * da, axis=-1, keepdims=True))).astype(bf16)
-        dq = mm(ds, k[i], NN) * factor
-        dk = mm(ds, q[i], TN) * factor
-        for j, piece in enumerate((dq, dk, dv)):
-            dpack[:, j * slab + i * head : j * slab + (i + 1) * head] = piece
-    dp = dpack[...].astype(bf16)
-    dx = d_one + sum_z(3, mm(dp, cw[:, qkv_cols], NT))
-    for i in range(8):
-        ybuf[i, :, :width] = result[2 * i : 2 * i + 2]
-        ybuf[i, :, width:] = dx[2 * i : 2 * i + 2]
-    home = remote(
-        ybuf.at[2 * p.z + 1 - p.core], home_ref.at[p.core], h_send, h_recv, p.sib
-    )
-    home.start()
-    home_ref[p.core] = ybuf[2 * p.z + p.core]
-
-    def part(full):
-        pieces = [full[:, i * slab : (i + 1) * slab] for i in range(4)]
-        out = pieces[0]
-        for i in range(1, 4):
-            out = jnp.where(p.z == i, pieces[i], out)
-        return out.astype(bf16)
-
-    fac_ref[:, :width] = active
-    fac_ref[:, width : 2 * width] = du
-    fac_ref[:, 2 * width :] = jnp.concatenate(
-        [dp, part(d_one), part(states), part(normed), part(d_two), context], axis=1
-    )
-    once = jnp.where(p.z == 0, 1.0, 0.0)
-    sums = [d_normed * z_one, cot * z_two, d_normed, cot]
-    small_ref[...] = jnp.zeros_like(small_ref)
-    for i, s in enumerate(sums):
-        small_ref[i : i + 1, :] = once * jnp.sum(s, axis=0, keepdims=True)
-    theirs = home_ref.at[1 - p.core]
-    remote(theirs, theirs, h_send, h_recv, p.sib).wait_recv()
-    home.wait_send()
-    for d in range(4):
-        z = (p.z + d) % 4
-        for j in range(2):
-            if d:
-                lead_copy(z, j).wait_send()
-            else:
-
-                @pl.when(p.core != j)
-                def _():
-                    lead_copy(z, j).wait_send()
-    comm.finish()
-    for i in range(n_seg + 2):
-        pair(i).wait_send()
-    for s in range(segs):
-        spot = pl.ds(s * SEG_LEN, 16)
-        old = y_ref[spot, :].astype(f32)
-        new = jnp.broadcast_to(home_ref[s // 2, s % 2 : s % 2 + 1, :width], old.shape)
-        top = lax.broadcasted_iota(jnp.int32, old.shape, 0) == 0
-        y_ref[spot, :] = jnp.where(top, new, old).astype(bf16)
-    for copy in kept:
-        copy.wait()
-
-
-def segment_forward(ws, wq, wo, wi, wb, x, cot, mask):
-    wrows = 16 * ROWS
-    rows, width = x.shape
-    segs = rows // SEG_LEN
-    leads = mask.shape[0]
-    hidden = wi.shape[2]
-    cross_width = 3 * width
-    total = ws.shape[1] + 3 * width + width + 2 * hidden + 4 * cross_width + width
-    parts = 5 + 2 * hidden // width + 2
-    n_units = parts - 2 + 3
-    hbm, vm = pl.BlockSpec(memory_space=pl.ANY), pl.BlockSpec(memory_space=VM)
-    arr = jax.ShapeDtypeStruct
-    DMA = pltpu.SemaphoreType.DMA
-    att_rows = segs * HEADS * SEG_LEN
-    big = [
-        arr((wrows, 3 * width), bf16), arr((wrows, hidden), bf16), arr((wrows, width), bf16),
-        arr((wrows, hidden), bf16),
-        arr((rows, 3 * width), bf16), arr((att_rows, SEG_LEN), bf16), arr((rows, width), bf16),
-        arr((rows, width), bf16), arr((rows, hidden), bf16), arr((rows, hidden), bf16),
-        arr((rows, width), bf16), arr((rows, width), bf16),
-    ]
-    near = [
-        arr((rows, width), bf16), arr((24, width), f32),
-        arr((rows, LANES), f32), arr((rows, LANES), f32),
-        arr((2, 2, 2 * width), f32), arr((leads, 4 * width), bf16), arr((8, width), f32),
-    ]
-    return pl.pallas_call(
-        forward_kernel,
-        out_shape=big + near,
-        in_specs=[vm] * 8,
-        out_specs=[hbm] * len(big) + [vm] * len(near),
-        scratch_shapes=[
-            VM((wrows, ws.shape[1]), bf16), VM((wrows, width), bf16), VM((wrows, 3 * width), bf16),
-            VM((wrows, hidden), bf16), VM((wrows, hidden), bf16),
-            VM((wrows, cross_width), bf16), VM((wrows // 4, width), bf16),
-            VM((rows, 3 * width), bf16), VM((att_rows, SEG_LEN), bf16), VM((rows, width), bf16),
-            VM((rows, width), f32), VM((rows, width), bf16), VM((rows, hidden), bf16),
-            VM((rows, hidden), bf16), VM((rows, width), bf16), VM((rows, width), bf16),
-            VM((32, total), bf16), VM((32, total), bf16), VM((ROWS, 4 * cross_width + width), bf16),
-            VM((2, 2, 2 * width), f32), VM((8, 2, 2 * width), f32), VM((leads, 2 * width), f32),
-            VM((4, 4, leads, width), bf16), VM((8, 2, 2 * width), f32), VM((leads, 3 * width // 4), f32),
-            DMA((n_units, 11)), DMA((n_units, 11)), DMA((parts,)), DMA((parts,)),
-            DMA((5,)), DMA((5,)), DMA, DMA((12,)),
-            DMA((8,)), DMA((8,)), DMA((4, 3)), DMA((4, 4)), DMA, DMA, DMA,
-        ],
-        compiler_params=pltpu.CompilerParams(
-            collective_id=0, has_side_effects=True, vmem_limit_bytes=60 * MIB
-        ),
-    )(wq, wo, wi, wb, ws, x, cot, mask)
-
-
-class Scatter:
-    def __init__(self, place, grad, off, width, out, index, sems, bufs, wide_a=True):
-        self.p, self.grad, self.off, self.out, self.m = place, grad, off, out, index
-        self.send, self.recv = sems
-        self.pair, self.r1a, self.r1b, self.rx, self.ry, self.r3, self.give = bufs
-        self.half = width // 2
-        self.a = split_half(width, wide_a)
-        self.b = self.half - self.a
-        self.sent = []
-        p = place
-        self.far = (1 - p.y) * 2 + 1 - p.x
-        self.groups = (self.far, p.xdp, p.ydp, p.dp)
-
-    def go(self, src, dst, slot, device):
-        copy = remote(src, dst, self.send.at[self.m, slot], self.recv.at[self.m, slot], device)
-        copy.start()
-        self.sent.append(copy)
-
-    def arrived(self, dst, slot):
-        remote(dst, dst, self.send.at[self.m, slot], self.recv.at[self.m, slot], self.p.sib).wait_recv()
-
-    def cols(self, part="AB", core=None):
-        at, size = {"A": (0, self.a), "B": (self.a, self.b), "AB": (0, self.half)}[part]
-        core = self.p.core if core is None else core
-        return lanes(self.off + core * self.half + at, size)
-
-    def group(self, dp):
-        return rows_at(dp * 4 * ROWS, 4 * ROWS, 16)
-
-    def side(self, dp, part="AB"):
-        return self.grad.at[self.group(dp), self.cols(part)]
-
-    def start(self):
-        p = self.p
-        for i, dp in enumerate(self.groups):
-            theirs = self.grad.at[self.group(dp), self.cols("AB", 1 - p.core)]
-            self.go(theirs, self.pair.at[self.group(dp)], i, p.sib)
-
-    def add(self, dp, part, other, other_row=0):
-        @pl.loop(0, 4)
-        def _(i):
-            key = (rows_at(dp * 4 * ROWS + i * ROWS, ROWS, 16), self.cols(part))
-            self.grad[key] = self.grad[key] + other[rows_at(other_row + i * ROWS, ROWS, 16), :]
-
-    def one(self):
-        p = self.p
-        for i, dp in enumerate(self.groups):
-            self.arrived(self.pair.at[self.group(dp)], i)
-            self.add(dp, "AB", self.pair, dp * 4 * ROWS)
-            if i == 0:
-                self.go(self.side(dp, "A"), self.r1a, 4, p.ynbr)
-                if self.b:
-                    self.go(self.side(dp, "B"), self.r1b, 5, p.xnbr)
-
-    def two(self):
-        p = self.p
-        self.arrived(self.r1a, 4)
-        self.add(p.xdp, "A", self.r1a)
-        self.go(self.side(p.xdp), self.rx, 6, p.xnbr)
-        if self.b:
-            self.arrived(self.r1b, 5)
-            self.add(p.ydp, "B", self.r1b)
-        self.go(self.side(p.ydp), self.ry, 7, p.ynbr)
-
-    def three(self):
-        p = self.p
-        self.arrived(self.rx, 6)
-        self.arrived(self.ry, 7)
-
-        @pl.loop(0, 4)
-        def _(i):
-            key = (rows_at(p.dp * 4 * ROWS + i * ROWS, ROWS, 16), self.cols())
-            own = rows_at(i * ROWS, ROWS, 16)
-            self.grad[key] = self.grad[key] + (self.rx[own, :] + self.ry[own, :])
-
-        for d in (1, 3, 2):
-            z = (p.z + d) % 4
-            src = self.grad.at[rows_at((p.dp * 4 + z) * ROWS, ROWS, 16), self.cols()]
-            self.go(src, self.r3.at[d - 1], 7 + d, p.at(p.dp, z, p.core))
-
-    def four(self):
-        p = self.p
-        for d in (1, 3, 2):
-            self.arrived(self.r3.at[d - 1], 7 + d)
-        rows = rows_at((p.dp * 4 + p.z) * ROWS, ROWS, 16)
-        total = self.grad[rows, self.cols()].astype(f32)
-        for d in range(3):
-            total = total + self.r3[d].astype(f32)
-        upper, lower = total[: ROWS // 2], total[ROWS // 2 :]
-        first = p.core == 0
-        self.give[...] = jnp.where(first, lower, upper)
-        self.out[:, self.cols()] = jnp.where(first, upper, lower)
-        self.go(self.give, self.out.at[:, self.cols()], 11, p.sib)
-
-    def five(self):
-        self.arrived(self.out.at[:, self.cols("AB", 1 - self.p.core)], 11)
-
-    def finish(self):
-        for copy in self.sent:
-            copy.wait_send()
-
-
-def split_half(width, wide_a):
-    tiles = width // 2 // LANES
-    return ((tiles + 1) // 2 if wide_a else max(tiles // 2, 1)) * LANES
-
-
-def scatter_buffers(width, wide_a):
-    half = width // 2
-    a = split_half(width, wide_a)
-    b = half - a
-    return [
-        VM((16 * ROWS, half), bf16),
-        VM((4 * ROWS, a), bf16),
-        VM((4 * ROWS if b else 16, max(b, LANES)), bf16),
-        VM((4 * ROWS, half), bf16),
-        VM((4 * ROWS, half), bf16),
-        VM((3, ROWS, half), bf16),
-        VM((ROWS // 2, half), f32),
-    ]
-
-
-SCATTER_LAGS = {"start": 0, "one": 1, "two": 2, "three": 3, "four": 4, "five": 5}
-FACTOR_LAGS = {"own": -2, "line": 0, "plane": 1, "last": 2, "drain": 3}
-
-
-def scatter_step(sums, jobs):
-    begun = len([s for s in sums.order[: sums.at] if s[0] == "start"])
-    follow = [i for i, s in enumerate(sums.order) if s == ("start", begun + 1)]
-    if begun < len(jobs):
-        sums.step((follow[0] if follow else sums.order.index(("start", begun)) + 1) - sums.at)
-
-
-def backward_kernel(*refs):
-    (
-        cot_ref, x_ref, home_ref, par_ref, r1_ref, r2_ref, z2_ref, fac_ref, csmall_ref,
-        p_hbm, a_hbm, c_hbm, nl_hbm, g_hbm, sl_hbm, z1_hbm, w_hbm, o_hbm, i_hbm, b_hbm,
-    ) = refs[:20]
-    gt_ref, gq_ref, go_ref, gi_ref, gb_ref, gs_ref = refs[20:26]
-    (
-        pk, at, cx, nl, g, sl, z1, qw, ow, fw,
-        h, df, tr, tr2, dwb, dwi, dwo, dwq, dws, small,
-        sib_buf, full, tmp,
-        f_send, f_recv, pair_send, pair_recv, load, rs_send, rs_recv,
-    ) = refs[26:56]
-    bufs = refs[56:]
-    p = Place()
-    rows, width = x_ref.shape
-    segs = rows // SEG_LEN
-    hidden = g.shape[1]
-    pairs = width // LANES
-    tile = 256
-    chunks = hidden // tile
-
-    loads = {}
-    order = [
-        ("g", g_hbm, g), ("b", b_hbm, fw), ("sl", sl_hbm, sl), ("nl", nl_hbm, nl), ("z1", z1_hbm, z1),
-        ("c", c_hbm, cx), ("o", o_hbm, ow), ("p", p_hbm, pk), ("a", a_hbm, at), ("w", w_hbm, qw),
-        ("i", i_hbm, fw),
-    ]
-    for i, (name, src, dst) in enumerate(order):
-        loads[name] = pltpu.make_async_copy(src, dst, load.at[i])
-    for name, _, _ in order[:-1]:
-        loads[name].start()
-    greet(gather_peers(p))
-
-    lead = fac_ref.shape[0]
-    lead2 = 2 * lead
+
+    leads = fac.shape[0]
+    lead2 = 2 * leads
     key_f = rows_at((p.dp * 4 + p.z) * lead2, lead2, 16)
-    swap = remote(fac_ref, sib_buf, pair_send, pair_recv, p.sib)
-    swap.start()
+
+    def swap(i):
+        cols = pl.ds(i * width, width)
+        return remote(fac.at[:, cols], fac_sib.at[:, cols], swap_send.at[i], swap_recv.at[i], p.sib)
+
+    def give_factor(i, value):
+        fac[:, i * width : (i + 1) * width] = value
+        swap(i).start()
 
     class Factor(Gather):
         def __init__(self, i):
             mine = lambda z: full.at[key_f, self.cols(p.core)]
             super().__init__(p, full, i * width, width, mine, i, (f_send, f_recv), lead2, i % 2 == 0)
-
-    factors = Staged([Factor(i) for i in range(4)], staggered(4, FACTOR_LAGS))
-
-    def factor_own():
-        swap.wait_recv()
-        base = (p.dp * 4 + p.z) * lead2
-        for i in range(4):
-            cols = lanes(i * width + p.core * (width // 2), width // 2)
-            full[rows_at(base + p.core * lead, lead, 16), cols] = fac_ref[:, cols]
-            full[rows_at(base + (1 - p.core) * lead, lead, 16), cols] = sib_buf[:, cols]
+            self.i = i
+
+        def own(self):
+            swap(self.i).wait_recv()
+            base = (p.dp * 4 + p.z) * lead2
+            cols = lanes(self.i * width + p.core * (width // 2), width // 2)
+            full[rows_at(base + p.core * leads, leads, 16), cols] = fac[:, cols]
+            full[rows_at(base + (1 - p.core) * leads, leads, 16), cols] = fac_sib[:, cols]
+            super().own()
+
+    factors = [Factor(i) for i in range(4)]
 
     def factor_grads():
-        slab = width // 4
-
         def rows_of(z, at_col, size):
             return jnp.concatenate(
                 [full[rows_at((i * 4 + z) * lead2, lead2, 16), pl.ds(at_col, size)] for i in range(4)],
                 axis=0,
             )
 
-        base = 2 * width + 3 * slab
+        base = 2 * width
         own = rows_at(p.fsdp * (ROWS // 2), ROWS // 2, 8)
-        xl = rows_of(p.dp, base + slab, slab)
-        nlf = rows_of(p.dp, base + 2 * slab, slab)
-        dff = rows_of(p.dp, base + 3 * slab, slab)
-        ctx = rows_of(p.dp, base + 4 * slab, slab)
+        xl = rows_of(p.dp, base, slab)
+        nlf = rows_of(p.dp, base + slab, slab)
+        dff = rows_of(p.dp, base + 2 * slab, slab)
+        ctx = rows_of(p.dp, base + 3 * slab, slab)
         for z in range(4):
             tmp[:, :width] = mm(dff, rows_of(z, 0, width), TN)
             gb_ref[1, :, z * width : (z + 1) * width] = tmp[own, :width]
             tmp[:, :width] = mm(nlf, rows_of(z, width, width), TN)
             gi_ref[1, :, z * width : (z + 1) * width] = tmp[own, :width]
-            tmp[:, : 3 * slab] = mm(xl, rows_of(z, 2 * width, 3 * slab), TN)
+            tmp[:, : 3 * slab] = mm(xl, rows_of(z, 3 * width, 3 * slab), TN)
             got = tmp[own, : 3 * slab]
             for j in range(3):
                 spot = j * width + z * slab
                 gq_ref[1, :, spot : spot + slab] = got[:, j * slab : (j + 1) * slab]
-            tmp[:, :slab] = mm(ctx, rows_of(z, base, slab), TN)
+            tmp[:, :slab] = mm(ctx, rows_of(z, 3 * width + 3 * slab, slab), TN)
             go_ref[1, :, z * slab : (z + 1) * slab] = tmp[own, :slab]
 
-    jobs = []
-    for i, (grad, off, size, dst) in enumerate(
-        [(dwb, i * width, width, gb_ref.at[0]) for i in range(hidden // width)]
-        + [(dwi, i * width, width, gi_ref.at[0]) for i in range(hidden // width)]
-        + [(dwo, 0, width, go_ref.at[0]), (dws, 0, dws.shape[1], gs_ref)]
-        + [(dwq, i * width, width, gq_ref.at[0]) for i in range(3)]
-    ):
-        jobs.append(
-            Scatter(p, grad, off, size, dst, i, (rs_send, rs_recv), bufs[7 * i : 7 * i + 7], i % 2 == 0)
+
+    n_tiles = width // tile
+    head = width // HEADS
+    heads = HEADS // 4
+
+    def cross():
+        for d in range(4):
+            z = (p.z + d) % 4
+            for j in range(2):
+                if d:
+                    lead_copy(z, j).start()
+                else:
+
+                    @pl.when(p.core != j)
+                    def _():
+                        lead_copy(z, j).start()
+
+                    @pl.when(p.core == j)
+                    def _():
+                        mine = pltpu.make_async_copy(lead_out.at[j], gbuf.at[p.fsdp], lead_sem)
+                        mine.start()
+                        mine.wait()
+
+        need(n_seg)
+        wo_middle()
+        for d in range(1, 8):
+            i = lax.rem(p.fsdp + d, 8)
+            remote(gbuf.at[i], gbuf.at[i], g_send.at[i], g_recv.at[i], p.sib).wait_recv()
+        for i in range(8):
+            lead[2 * i : 2 * i + 2, :] = gbuf[i]
+        states = lead[:, :width]
+        cot_rows = lead[:, width:]
+
+        def sum_z(e, partial_sum, between):
+            xbuf[e, p.z] = partial_sum.astype(bf16)
+            copies = []
+            for d in (1, 3, 2):
+                z = (p.z + d) % 4
+                copy = remote(
+                    xbuf.at[e, p.z], xbuf.at[e, p.z], x_send.at[e, d - 1], x_recv.at[e, p.z],
+                    p.at(p.dp, z, p.core),
+                )
+                copy.start()
+                copies.append(copy)
+            between()
+            for d in (1, 3, 2):
+                z = (p.z + d) % 4
+                piece = xbuf.at[e, z]
+                remote(piece, piece, x_send.at[e, d - 1], x_recv.at[e, z], p.sib).wait_recv()
+            for copy in copies:
+                copy.wait_send()
+            return sum(xbuf[e, z].astype(f32) for z in range(4))
+
+        gain0, gain1 = par_ref[4:5, :], par_ref[5:6, :]
+        bias0, bias1 = par_ref[6:7, :], par_ref[7:8, :]
+        in_cols, back_cols = pl.ds(width, width), pl.ds(2 * width, width)
+        qkv_cols = pl.ds(0, 3 * slab)
+        factor = head ** (-0.5)
+        allowed = mask_ref[...] > 0.5
+
+        def part(full):
+            pieces = [full[:, i * slab : (i + 1) * slab] for i in range(4)]
+            out = pieces[0]
+            for i in range(1, 4):
+                out = jnp.where(p.z == i, pieces[i], out)
+            return out.astype(bf16)
+
+        xl = states.astype(bf16)
+        packed = mm(xl, cw[:, qkv_cols], NN).astype(bf16)
+        q = [packed[:, i * head : (i + 1) * head] for i in range(heads)]
+        k = [packed[:, slab + i * head : slab + (i + 1) * head] for i in range(heads)]
+        v = [packed[:, 2 * slab + i * head : 2 * slab + (i + 1) * head] for i in range(heads)]
+        att, context = [], []
+        for i in range(heads):
+            scores = jnp.where(allowed, mm(q[i], k[i], NT) * factor, NEG)
+            top = jnp.max(scores, axis=-1, keepdims=True)
+            terms = jnp.exp(scores - top)
+            a = terms / jnp.sum(terms, axis=-1, keepdims=True)
+            att.append(a)
+            context.append(mm(a.astype(bf16), v[i], NN))
+        context = jnp.concatenate(context, axis=1).astype(bf16)
+        wo_finish()
+        branch = sum_z(0, mm(context, cwo[...], NN), lambda: None)
+        normed, z_one, r_one = norm_rows(states + branch, gain0, bias0)
+        nl = normed.astype(bf16)
+        need(n_seg + 1)
+        hidden = mm(nl, cw[:, in_cols], NN)
+        phi, slope = gelu_parts(hidden)
+        active = (hidden * phi).astype(bf16)
+        give_factor(0, active)
+        need(n_seg + 2)
+
+        def during_one():
+            factors[0].own()
+
+        feed = sum_z(1, mm(active, cw[:, back_cols], NT), during_one)
+        result, z_two, r_two = norm_rows(normed + feed, gain1, bias1)
+        d_two = norm_rows_back(cot_rows, z_two, r_two, gain1)
+        df = d_two.astype(bf16)
+        du = (mm(df, cw[:, back_cols], NN) * slope).astype(bf16)
+        give_factor(1, du)
+        give_factor(2, jnp.concatenate([part(states), part(normed), part(d_two), context], axis=1))
+
+        def during_two():
+            factors[0].line()
+            factors[1].own()
+            factors[2].own()
+
+        d_normed = d_two + sum_z(2, mm(du, cw[:, in_cols], NT), during_two)
+        d_one = norm_rows_back(d_normed, z_one, r_one, gain0)
+        db = d_one.astype(bf16)
+        dc = mm(db, cwo[...], NT).astype(bf16)
+        for i in range(heads):
+            a = att[i]
+            dci = dc[:, i * head : (i + 1) * head]
+            da = mm(dci, v[i], NT)
+            dv = mm(a.astype(bf16), dci, TN)
+            ds = (a * (da - jnp.sum(a * da, axis=-1, keepdims=True))).astype(bf16)
+            dq = mm(ds, k[i], NN) * factor
+            dk = mm(ds, q[i], TN) * factor
+            for j, piece in enumerate((dq, dk, dv)):
+                dpack[:, j * slab + i * head : j * slab + (i + 1) * head] = piece
+        dp = dpack[...].astype(bf16)
+        give_factor(3, jnp.concatenate([dp, part(d_one)], axis=1))
+
+        def during_three():
+            factors[0].plane()
+            factors[1].line()
+            factors[3].own()
+            factors[2].line()
+
+        dx = d_one + sum_z(3, mm(dp, cw[:, qkv_cols], NT), during_three)
+        for i in range(8):
+            ybuf[i, :, :width] = result[2 * i : 2 * i + 2]
+            ybuf[i, :, width:] = dx[2 * i : 2 * i + 2]
+        home = remote(
+            ybuf.at[2 * p.z + 1 - p.core], home_ref.at[p.core], h_send, h_recv, p.sib
         )
+        home.start()
+        home_ref[p.core] = ybuf[2 * p.z + p.core]
+
+        once = jnp.where(p.z == 0, 1.0, 0.0)
+        sums_of = [d_normed * z_one, cot_rows * z_two, d_normed, cot_rows]
+        csmall[...] = jnp.zeros_like(csmall)
+        for i, s in enumerate(sums_of):
+            csmall[i : i + 1, :] = once * jnp.sum(s, axis=0, keepdims=True)
+        theirs = home_ref.at[1 - p.core]
+        remote(theirs, theirs, h_send, h_recv, p.sib).wait_recv()
+        home.wait_send()
+
+    def wait_leads():
+        for d in range(4):
+            z = (p.z + d) % 4
+            for j in range(2):
+                if d:
+                    lead_copy(z, j).wait_send()
+                else:
+
+                    @pl.when(p.core != j)
+                    def _():
+                        lead_copy(z, j).wait_send()
+
+
+    def patch():
+        for s in range(segs):
+            spot = pl.ds(s * SEG_LEN, 16)
+            old = y_ref[spot, :].astype(f32)
+            new = jnp.broadcast_to(home_ref[s // 2, s % 2 : s % 2 + 1, :width], old.shape)
+            top = lax.broadcasted_iota(jnp.int32, old.shape, 0) == 0
+            y_ref[spot, :] = jnp.where(top, new, old).astype(bf16)
+    per = hidden // width
+    parts = [(bw, i * width, width, gb_ref.at[0]) for i in range(per)]
+    parts += [(iw, i * width, width, gi_ref.at[0]) for i in range(per)]
+    parts += [(ow, 0, width, go_ref.at[0]), (dws, 0, dws.shape[1], gs_ref)]
+    parts += [(qw, at_col, size, gq_ref.at[0]) for at_col, size in tail_units(width)]
+    jobs, shared = [], []
+    for i, (grad, off, size, dst) in enumerate(parts):
+        job_bufs = list(bufs[6 * i : 6 * i + 6])
+        if size == width:
+            slot = len(shared) % PAIR_SLOTS
+            job = Scatter(p, grad, off, size, dst, i, (rs_send, rs_recv), [ring.at[slot]] + job_bufs, i % 2 == 0)
+            job.free = free.at[slot]
+            if len(shared) >= PAIR_SLOTS:
+                job.waits = True
+                shared[len(shared) - PAIR_SLOTS].frees = True
+            shared.append(job)
+        else:
+            own_pair = pair_wide if size > 256 else pair_small.at[len([j for j in jobs if j.half == LANES])]
+            job = Scatter(p, grad, off, size, dst, i, (rs_send, rs_recv), [own_pair] + job_bufs, i % 2 == 0)
+        jobs.append(job)
     sums = Staged(jobs, staggered(len(jobs), SCATTER_LAGS))
 
-    block_rows = 64
 
     def norm_back(z_ref, r_ref, gain_row, low_ref, sums):
         def step(i, acc):
@@ -1009,8 +935,8 @@
         def _(i):
             tr[rows_at(i * tile, tile, 16), :] = ref[:, lanes(i * tile, tile)].T
 
-    def outer(dst, tr, src, part):
-        @pl.loop(part * (width // tile), (part + 1) * (width // tile))
+    def outer(dst, tr, src, first, size):
+        @pl.loop(first // tile, (first + size) // tile)
         def _(i):
             cols = lanes(i * tile, tile)
             dst[:, cols] = mm(tr[...], src[:, cols], NN).astype(bf16)
@@ -1024,24 +950,27 @@
         for s in range(segs):
             h[s * SEG_LEN : s * SEG_LEN + 1, :] = home_ref[s // 2, s % 2 : s % 2 + 1, width:]
         small[...] = jnp.zeros_like(small)
-        small[4:8, :] = csmall_ref[0:4, :]
+        small[4:8, :] = csmall[0:4, :]
         for s in range(2):
             row = home_ref[0, s : s + 1, width:] + home_ref[1, s : s + 1, width:]
             small[pl.ds(8 + p.fsdp * 2 + s, 1), :] = row
-        norm_back(z2_ref, r2_ref, 1, df, 1)
+        norm_back(z2, r2_ref, 1, df, 1)
         turn(tr, df)
 
-    def active_back(first, count):
-        @pl.loop(first, first + count)
+    def active_back(part):
+        @pl.loop(part * n_tiles, (part + 1) * n_tiles)
         def _(i):
             cols = lanes(i * tile, tile)
-            d = mm(df[...], fw[:, cols], NN) * sl[:, cols].astype(f32)
+            d = mm(df[...], bw[:, cols], NN) * sl[:, cols].astype(f32)
             sl[:, cols] = d.astype(bf16)
 
-    def add_back(src, weight):
-        @pl.loop(0, width // tile)
+    def add_back(src, weight, first, size):
+        inner = pl.ds(first, size)
+
+        @pl.loop(0, n_tiles)
         def _(i):
-            h[:, lanes(i * tile, tile)] += mm(src[...], weight[rows_at(i * tile, tile, 16), :], NT)
+            cols = lanes(i * tile, tile)
+            h[:, cols] += mm(src[:, inner], weight[rows_at(i * tile, tile, 16), inner], NT)
 
     def context_back():
         @pl.loop(0, width // tile)
@@ -1074,92 +1003,121 @@
             pk[key, v_cols] = dv.astype(bf16)
 
     def result():
-        @pl.loop(0, width // tile)
+        @pl.loop(0, rows // block_rows)
         def _(i):
-            cols = lanes(i * tile, tile)
-            d = h[:, cols] + mm(pk[...], qw[rows_at(i * tile, tile, 16), :], NT)
-            gt_ref[:, cols] = d.astype(bf16)
+            key = rows_at(i * block_rows, block_rows, 16)
+            gt_ref[key, :] = h[key, :].astype(bf16)
 
     def smalls():
         dws[:, :LANES] = small[...].T.astype(bf16)
         dws[:, LANES:] = jnp.zeros((dws.shape[0], LANES), bf16)
 
-    per = hidden // width
-    factor_own()
-    factors.step(3)
+    need(0)
+    params()
+    for i in range(3):
+        need(1 + i)
+        project(i * n_tiles, n_tiles)
+    for s in range(segs):
+        attend(s)
+        comm.upto("drain", 4 + s)
+    branch()
+    for i in range(per):
+        need(8 + i)
+        feed_in(i * n_tiles, n_tiles)
+    wo_start()
+    for i in range(per):
+        need(5 + per + i)
+        feed_back(i)
+    finish_block()
+    leaders()
+    cross()
+    comm.finish()
+    for i in range(n_seg + 2):
+        pair(i).wait_send()
+    patch()
+    sum_step = lambda: scatter_step(sums, jobs)
     norm_two()
-    factors.step(3)
-    loads["g"].wait()
+    factors[1].plane()
+    factors[2].plane()
+    factors[0].last()
     for i in range(per):
-        outer(dwb, tr, g, i)
-        scatter_step(sums, jobs)
-        factors.step(3)
-    loads["b"].wait()
-    loads["sl"].wait()
-    active_back(0, chunks // 2)
-    factors.step(3)
-    active_back(chunks // 2, chunks - chunks // 2)
-    loads["i"].start()
-    loads["nl"].wait()
+        active_back(i)
+        outer(bw, tr, g, i * width, width)
+        sum_step()
+        if i == 0:
+            factors[3].line()
+            factors[1].last()
+        if i == 1:
+            factors[2].last()
+            factors[3].plane()
+        if i == 2:
+            factors[3].last()
     turn(tr, nl)
-    outer(dwi, tr, sl, 0)
-    scatter_step(sums, jobs)
-    loads["i"].wait()
-    add_back(sl, fw)
-    outer(dwi, tr, sl, 1)
-    scatter_step(sums, jobs)
-    loads["z1"].wait()
+    add_back(sl, iw, 0, 2 * width)
+    add_back(sl, iw, 2 * width, hidden - 2 * width)
+    outer(iw, tr, sl, 0, width)
+    sum_step()
     norm_back(z1, r1_ref, 0, df, 0)
+    outer(iw, tr, sl, width, width)
+    sum_step()
     smalls()
+    turn(tr2, cx)
+    context_back()
+    attend_back(0)
     for i in range(2, per - 1):
-        outer(dwi, tr, sl, i)
-        scatter_step(sums, jobs)
-    loads["c"].wait()
-    turn(tr2, cx)
-    loads["o"].wait()
-    outer(dwo, tr2, df, 0)
-    context_back()
-    loads["p"].wait()
-    loads["a"].wait()
-    attend_back(0)
-    outer(dwi, tr, sl, per - 1)
-    scatter_step(sums, jobs)
+        outer(iw, tr, sl, i * width, width)
+        sum_step()
     attend_back(1)
-    scatter_step(sums, jobs)
+    outer(iw, tr, sl, (per - 1) * width, width)
+    sum_step()
     attend_back(2)
-    scatter_step(sums, jobs)
+    outer(ow, tr2, df, 0, width)
+    sum_step()
     attend_back(3)
+    sum_step()
     turn(tr2, x_ref)
-    for i in range(3):
-        outer(dwq, tr2, pk, i)
-        scatter_step(sums, jobs)
-    loads["w"].wait()
+    for at_col, size in tail_units(width):
+        add_back(pk, qw, at_col, size)
+        outer(qw, tr2, pk, at_col, size)
+        sum_step()
     result()
-    factors.finish()
+    for unit in factors:
+        unit.drain()
     factor_grads()
     sums.finish()
-    swap.wait_send()
-
-
-def segment_backward(near, far):
-    cot, x = near[0], near[1]
+    for unit in factors:
+        unit.finish()
+    for i in range(4):
+        swap(i).wait_send()
+    wait_leads()
+
+
+def layer(ws, wq, wo, wi, wb, x, cot, mask):
+    wrows = 16 * ROWS
     rows, width = x.shape
-    packed, att, context, nl, g = far[:5]
-    hidden = g.shape[1]
-    hbm, vm = pl.BlockSpec(memory_space=pl.ANY), pl.BlockSpec(memory_space=VM)
+    segs = rows // SEG_LEN
+    leads = mask.shape[0]
+    hidden = wi.shape[2]
+    own = ROWS // 2
+    cross_width = 3 * width
+    total = ws.shape[1] + 3 * width + width + 2 * hidden + 4 * cross_width + width
+    parts = 5 + 2 * hidden // width + 2
+    n_units = parts - 2 + 3
+    vm = pl.BlockSpec(memory_space=VM)
     arr = jax.ShapeDtypeStruct
-    own = ROWS // 2
-    lead = near[7].shape[0]
-    like = lambda v: VM(v.shape, v.dtype)
-    wrows = 16 * ROWS
-    widths = [width] * (2 * (hidden // width) + 1) + [256] + [width] * 3
+    DMA = pltpu.SemaphoreType.DMA
+    att_rows = segs * HEADS * SEG_LEN
+    wide = lambda v, kind=bf16: VM((rows, v), kind)
+    weight = lambda v: VM((wrows, v), bf16)
+    widths = [width] * (2 * (hidden // width) + 1) + [256] + [size for _, size in tail_units(width)]
     bufs = []
     for i, w in enumerate(widths):
         bufs += scatter_buffers(w, i % 2 == 0)
-    DMA = pltpu.SemaphoreType.DMA
+    small_units = len([w for w in widths if w == 256])
     return pl.pallas_call(
-        backward_kernel,
+        layer_kernel,
         out_shape=[
+            arr((rows, width), bf16),
             arr((rows, width), bf16),
             arr((2, own, 3 * width), f32),
             arr((2, own, width), f32),
@@ -1167,22 +1125,34 @@
             arr((2, own, hidden), f32),
             arr((own, 256), f32),
         ],
-        in_specs=[vm] * len(near) + [hbm] * len(far),
-        out_specs=[vm] * 6,
+        in_specs=[vm] * 8,
+        out_specs=[vm] * 7,
         scratch_shapes=[
-            like(packed), like(att), like(context), like(nl), like(g), like(g), like(nl),
-            VM((wrows, 3 * width), bf16), VM((wrows, width), bf16), VM((wrows, hidden), bf16),
-            VM((rows, width), f32), VM((rows, width), bf16), VM((width, rows), bf16), VM((width, rows), bf16),
-            VM((wrows, hidden), bf16), VM((wrows, hidden), bf16), VM((wrows, width), bf16),
-            VM((wrows, 3 * width), bf16), VM((wrows, 256), bf16), VM((LANES, width), f32),
-            VM((lead, 4 * width), bf16), VM((32 * lead, 4 * width), bf16), VM((width // 4, width), f32),
-            DMA((4, 11)), DMA((4, 11)), DMA, DMA, DMA((11,)), DMA((len(widths), 12)), DMA((len(widths), 12)),
+            weight(ws.shape[1]), weight(width), weight(3 * width), weight(hidden), weight(hidden),
+            weight(cross_width), VM((wrows // 4, width), bf16),
+            wide(3 * width), VM((att_rows, SEG_LEN), bf16), wide(width), wide(width, f32), wide(width),
+            wide(hidden), wide(hidden), wide(width), wide(width),
+            wide(LANES, f32), wide(LANES, f32), VM((24, width), f32),
+            VM((32, total), bf16), VM((32, total), bf16), VM((ROWS, 4 * cross_width + width), bf16),
+            VM((2, 2, 2 * width), f32), VM((8, 2, 2 * width), f32), VM((leads, 2 * width), f32),
+            VM((4, 4, leads, width), bf16), VM((8, 2, 2 * width), f32), VM((leads, 3 * width // 4), f32),
+            VM((2, 2, 2 * width), f32), VM((leads, 4 * width), bf16), VM((leads, 4 * width), bf16),
+            VM((8, width), f32),
+            wide(width), VM((width, rows), bf16), VM((width, rows), bf16), weight(256),
+            VM((LANES, width), f32), VM((32 * leads, 4 * width), bf16), VM((width // 4, width), f32),
+            VM((PAIR_SLOTS, wrows, width // 2), bf16), weight((width - 256) // 2),
+            VM((small_units, wrows, LANES), bf16),
+            DMA((n_units, 11)), DMA((n_units, 11)), DMA((parts,)), DMA((parts,)),
+            DMA((5,)), DMA((5,)), DMA,
+            DMA((8,)), DMA((8,)), DMA((4, 3)), DMA((4, 4)), DMA, DMA, DMA,
+            DMA((4, 11)), DMA((4, 11)), DMA((4,)), DMA((4,)),
+            DMA((len(widths), 12)), DMA((len(widths), 12)), pltpu.SemaphoreType.REGULAR((PAIR_SLOTS,)),
         ]
         + bufs,
         compiler_params=pltpu.CompilerParams(
-            collective_id=1, has_side_effects=True, vmem_limit_bytes=63 * MIB
+            collective_id=0, has_side_effects=True, vmem_limit_bytes=63 * MIB
         ),
-    )(*near, *far)
+    )(wq, wo, wi, wb, ws, x, cot, mask)
 
 
 def matmul(left, right, form):
@@ -1510,14 +1480,8 @@
     cot = cotangent.reshape(rows, width)
     own_row = lax.dynamic_index_in_dim(doc_ids, lax.axis_index("fsdp") % 2, 0, keepdims=False)
     mask = (own_row[:, None] == own_row[None, :]).astype(f32)
-    (
-        s_qkv, s_in, s_out, s_back,
-        packed, att, context, nl, act, slope, z_one, z_two,
-        output, par, r_one, r_two, home, fac, cross_small,
-    ) = segment_forward(small, w_qkv, w_out, w_in, jnp.swapaxes(w_back, 1, 2), x, cot, mask)
-    grad_tokens, g_qkv, g_out, g_in, g_back, t_small = segment_backward(
-        (cot, x, home, par, r_one, r_two, z_two, fac, cross_small),
-        (packed, att, context, nl, act, slope, z_one, s_qkv, s_out, s_in, s_back),
+    output, grad_tokens, g_qkv, g_out, g_in, g_back, t_small = layer(
+        small, w_qkv, w_out, w_in, jnp.swapaxes(w_back, 1, 2), x, cot, mask
     )
     s = t_small.T
     return (

time: 251 us -> 239 us (0.952)
  Pallas kernels: 236 us -> 224 us
    pallas_call x2 -> x1, Pallas kernels: 236 us -> 224 us  [layer(): pl.pallas_call(layer_kernel, out_shape=[arr((rows, width), bf16), arr((ro...]
    unnamed x20 -> x28, local copies, waits for them, and re-layouts: 8.12 us -> 10.6 us
where the time goes in v4:
time: 239 us
  Pallas kernels  224 us (94%)
  local copies, waits for them, and re-layouts  12.9 us (5%)
    pallas_call x1, Pallas kernels, layer(): pl.pallas_call(layer_kernel, out_shape=[arr((rows, width), bf16), arr((ro...  224 us
    unnamed x28, local copies, waits for them, and re-layouts  10.6 us

profile of v4, /device:TPU:1, one launch (start us, length us, event | category | flops | bytes accessed | tf_op | source)
XLA Modules:
  0.0 238.9 jit_solution(3340433103335995171)
XLA Ops:
  0.6 0.0 copy-start
  0.7 0.7 copy-done
  1.3 0.7 copy-done.8
  2.0 0.7 copy-done.9
  2.7 0.1 copy.22
  2.8 0.1 copy.21
  2.9 0.1 copy.20
  3.0 0.1 copy.19
  3.1 0.6 copy-done.7
  3.7 0.1 copy.23
  3.8 0.1 concatenate.3
  3.9 0.6 pad.4.refs_4_
  4.5 0.7 compare_convert_fusion.refs_7_
  5.2 224.0 %shard_map.169 = (bf16[512,768]{1,0:T(8,128)(2,1)}, bf16[512,768]{1,0:T(8,128)(2,1)}, f32[2,24,2304]{2,1,0:T(8,128)}, f32[2,24,768]{2,1,0:T(8,128)}, f32[2,24,30...) custom-call(bf16[2,24,2304]{2,1,0:T(8,128)(2,1)} %refs_0_.1, bf16[2,24,768]{2,1,0:T(8,128)(2,1)} %refs_1_.1, ...), custom_call_target="tpu_custom_call" | custom-call | tf_op jit(solution)/shard_map/pallas_call | solution.py:1117
  229.2 0.0 copy-start.5
  229.2 0.8 slice.36
  230.0 0.7 copy.28
  230.7 0.1 fusion
  230.8 0.1 copy.26
  230.8 0.1 copy.27
  230.9 0.1 copy.25
  231.0 0.1 copy.24
  231.1 0.6 pad_maximum_fusion
  231.7 2.1 copy.35
  233.8 0.9 copy.36
  234.7 0.4 copy-done.4
  235.1 0.8 copy.37
  235.9 0.3 copy-done.6
  236.2 0.7 copy.38
  236.8 0.8 copy.39
  237.6 0.5 copy-done.2
  238.1 0.8 copy.40
  (14 shorter events, 0.0 us)
Async XLA Ops:
  0.6 0.7 copy-start
  1.3 0.7 copy-start.8
  2.0 0.7 copy-start.9
  3.0 0.7 copy-start.7
  229.2 1.5 copy-start.5
  231.7 2.1 copy-start.1
  233.8 1.3 copy-start.4
  235.1 1.0 copy-start.6
  235.1 1.7 copy-start.3
  236.8 1.3 copy-start.2

commit v5 on v4

--- a/solution.py
+++ b/solution.py
@@ -396,19 +396,19 @@
 
 
 def layer_kernel(*refs):
-    wq_ref, wo_ref, wi_ref, wb_ref, ws_ref, x_ref, cot_ref, mask_ref = refs[:8]
-    y_ref, gt_ref, gq_ref, go_ref, gi_ref, gb_ref, gs_ref = refs[8:15]
+    wq_ref, wo_ref, wi_ref, wb_ref, gain_ref, bias_ref, pos_ref, docs_ref, x_ref, cot_ref = refs[:10]
+    y_ref, gt_ref, gq_ref, go_ref, gi_ref, gb_ref, gs_ref = refs[10:17]
     (
         sw, ow, qw, iw, bw, cw, cwo,
         pk, at, cx, h, nl, g, sl, z1, z2, r1_ref, r2_ref, par_ref,
-        own_buf, sib_buf, block,
+        own_buf, sib_buf, block, square,
         lead_out, gbuf, lead, xbuf, ybuf, dpack, home_ref, fac, fac_sib, csmall,
         df, tr, tr2, dws, small, full, tmp, ring, pair_wide, pair_small,
         s_send, s_recv, pair_send, pair_recv, wo_send, wo_recv, local,
         g_send, g_recv, x_send, x_recv, h_send, h_recv, lead_sem,
         f_send, f_recv, swap_send, swap_recv, rs_send, rs_recv, free,
-    ) = refs[15:78]
-    bufs = refs[78:]
+    ) = refs[17:81]
+    bufs = refs[81:]
     p = Place()
     rows, width = x_ref.shape
     segs = rows // SEG_LEN
@@ -419,7 +419,7 @@
     half_rows = ROWS // 2
     key_own = rows_at((p.dp * 4 + p.z) * ROWS, ROWS, 16)
 
-    sizes = [ws_ref.shape[1]] + [width] * (3 + 1 + 2 * (hidden // width)) + [4 * cross_width, width]
+    sizes = [sw.shape[1]] + [width] * (3 + 1 + 2 * (hidden // width)) + [4 * cross_width, width]
     starts = [sum(sizes[:i]) for i in range(len(sizes))]
     n_seg = len(sizes) - 2
     part_cross, part_wo = n_seg, n_seg + 1
@@ -439,7 +439,14 @@
         spot = starts[i]
         per = hidden // width
         if i == 0:
-            put(spot, ws_ref[...])
+            own = gain_ref.shape[2]
+            square[...] = jnp.zeros_like(square)
+            for b in range(2):
+                square[4 * b : 4 * b + 2, :own] = gain_ref[b].astype(f32)
+                square[4 * b + 2 : 4 * b + 4, :own] = bias_ref[b].astype(f32)
+            square[8 : 8 + pos_ref.shape[0], :own] = pos_ref[...].astype(f32)
+            turned = square[...].T[:half_rows]
+            put(spot, jnp.concatenate([turned, jnp.zeros_like(turned)], axis=1))
         elif i < 4:
             put(spot, wq_ref[0, :, (i - 1) * width : i * width])
         elif i == 4:
@@ -594,7 +601,7 @@
     def attend(s):
         key = pl.ds(s * SEG_LEN, SEG_LEN)
 
-        @pl.loop(0, pairs)
+        @pl.loop(0, pairs, unroll=True)
         def _(j):
             q2 = pk[key, lanes(j * LANES, LANES)]
             k2 = pk[key, lanes(width + j * LANES, LANES)]
@@ -616,7 +623,7 @@
             cols = lanes(i * tile, tile)
             h[:, cols] = x_ref[:, cols].astype(f32) + mm(cx[...], ow[:, cols], NN)
 
-        @pl.loop(0, rows // block_rows)
+        @pl.loop(0, rows // block_rows, unroll=2)
         def _(i):
             key = rows_at(i * block_rows, block_rows, 16)
             normed, scaled, inverse = norm_rows(h[key, :], par_ref[0:1, :], par_ref[2:3, :])
@@ -643,7 +650,7 @@
             h[:, cols] += mm(g[:, inner], bw[rows_at(i * tile, tile, 16), inner], NT)
 
     def finish_block():
-        @pl.loop(0, rows // block_rows)
+        @pl.loop(0, rows // block_rows, unroll=2)
         def _(i):
             key = rows_at(i * block_rows, block_rows, 16)
             result, scaled, inverse = norm_rows(h[key, :], par_ref[1:2, :], par_ref[3:4, :])
@@ -775,7 +782,12 @@
         in_cols, back_cols = pl.ds(width, width), pl.ds(2 * width, width)
         qkv_cols = pl.ds(0, 3 * slab)
         factor = head ** (-0.5)
-        allowed = mask_ref[...] > 0.5
+        docs = docs_ref[...].astype(f32)
+        number = docs.shape[1]
+        square[:number, :number] = jnp.broadcast_to(
+            jnp.where(p.core == 0, docs[0:1], docs[1:2]), (number, number)
+        )
+        allowed = square[:number, :number] == square[...].T[:number, :number]
 
         def part(full):
             pieces = [full[:, i * slab : (i + 1) * slab] for i in range(4)]
@@ -926,7 +938,7 @@
             return acc[0] + fold(dy * z), acc[1] + fold(dy)
 
         zero = jnp.zeros((8, width), f32)
-        gain, bias = lax.fori_loop(0, rows // block_rows, step, (zero, zero))
+        gain, bias = lax.fori_loop(0, rows // block_rows, step, (zero, zero), unroll=2)
         small[sums : sums + 1, :] = jnp.sum(gain, axis=0, keepdims=True)
         small[sums + 2 : sums + 3, :] = jnp.sum(bias, axis=0, keepdims=True)
 
@@ -942,7 +954,7 @@
             dst[:, cols] = mm(tr[...], src[:, cols], NN).astype(bf16)
 
     def norm_two():
-        @pl.loop(0, rows // block_rows)
+        @pl.loop(0, rows // block_rows, unroll=2)
         def _(i):
             key = rows_at(i * block_rows, block_rows, 16)
             h[key, :] = cot_ref[key, :].astype(f32)
@@ -982,7 +994,7 @@
         key = pl.ds(s * SEG_LEN, SEG_LEN)
         factor = (LANES // 2) ** (-0.5)
 
-        @pl.loop(0, pairs)
+        @pl.loop(0, pairs, unroll=True)
         def _(j):
             a = at[rows_at((s * pairs + j) * 2 * SEG_LEN, 2 * SEG_LEN, 16), :]
             q_cols = lanes(j * LANES, LANES)
@@ -1003,7 +1015,7 @@
             pk[key, v_cols] = dv.astype(bf16)
 
     def result():
-        @pl.loop(0, rows // block_rows)
+        @pl.loop(0, rows // block_rows, unroll=2)
         def _(i):
             key = rows_at(i * block_rows, block_rows, 16)
             gt_ref[key, :] = h[key, :].astype(bf16)
@@ -1022,12 +1034,13 @@
         comm.upto("drain", 4 + s)
     branch()
     for i in range(per):
-        need(8 + i)
+        need(4 + per + i)
         feed_in(i * n_tiles, n_tiles)
+        if i:
+            feed_back(i - 1)
     wo_start()
-    for i in range(per):
-        need(5 + per + i)
-        feed_back(i)
+    need(4 + 2 * per)
+    feed_back(per - 1)
     finish_block()
     leaders()
     cross()
@@ -1092,15 +1105,15 @@
     wait_leads()
 
 
-def layer(ws, wq, wo, wi, wb, x, cot, mask):
+def layer(wq, wo, wi, wb, gain, bias, pos, docs, x, cot):
     wrows = 16 * ROWS
     rows, width = x.shape
     segs = rows // SEG_LEN
-    leads = mask.shape[0]
+    leads = docs.shape[1]
     hidden = wi.shape[2]
     own = ROWS // 2
     cross_width = 3 * width
-    total = ws.shape[1] + 3 * width + width + 2 * hidden + 4 * cross_width + width
+    total = 2 * LANES + 3 * width + width + 2 * hidden + 4 * cross_width + width
     parts = 5 + 2 * hidden // width + 2
     n_units = parts - 2 + 3
     vm = pl.BlockSpec(memory_space=VM)
@@ -1125,15 +1138,16 @@
             arr((2, own, hidden), f32),
             arr((own, 256), f32),
         ],
-        in_specs=[vm] * 8,
+        in_specs=[vm] * 10,
         out_specs=[vm] * 7,
         scratch_shapes=[
-            weight(ws.shape[1]), weight(width), weight(3 * width), weight(hidden), weight(hidden),
+            weight(2 * LANES), weight(width), weight(3 * width), weight(hidden), weight(hidden),
             weight(cross_width), VM((wrows // 4, width), bf16),
             wide(3 * width), VM((att_rows, SEG_LEN), bf16), wide(width), wide(width, f32), wide(width),
             wide(hidden), wide(hidden), wide(width), wide(width),
             wide(LANES, f32), wide(LANES, f32), VM((24, width), f32),
             VM((32, total), bf16), VM((32, total), bf16), VM((ROWS, 4 * cross_width + width), bf16),
+            VM((LANES, LANES), f32),
             VM((2, 2, 2 * width), f32), VM((8, 2, 2 * width), f32), VM((leads, 2 * width), f32),
             VM((4, 4, leads, width), bf16), VM((8, 2, 2 * width), f32), VM((leads, 3 * width // 4), f32),
             VM((2, 2, 2 * width), f32), VM((leads, 4 * width), bf16), VM((leads, 4 * width), bf16),
@@ -1152,7 +1166,7 @@
         compiler_params=pltpu.CompilerParams(
             collective_id=0, has_side_effects=True, vmem_limit_bytes=63 * MIB
         ),
-    )(wq, wo, wi, wb, ws, x, cot, mask)
+    )(wq, wo, wi, wb, gain, bias, pos, docs, x, cot)
 
 
 def matmul(left, right, form):
@@ -1469,31 +1483,57 @@
     )
 
 
+def write_kernel(n, *refs):
+    sources, smalls = refs[:n], refs[n]
+    targets, pos_ref, gain_ref, bias_ref, sems = refs[n + 1 : 2 * n + 1], *refs[2 * n + 1 :]
+    copies = [pltpu.make_async_copy(sources[i], targets[i], sems.at[i]) for i in range(n)]
+    for copy in copies:
+        copy.start()
+    rows = smalls[:, :LANES].T[:, : smalls.shape[0]]
+    pos_ref[...] = rows[8 : 8 + pos_ref.shape[0]]
+    for b in range(2):
+        gain_ref[b] = rows[4 * b : 4 * b + 2]
+        bias_ref[b] = rows[4 * b + 2 : 4 * b + 4]
+    for copy in copies:
+        copy.wait()
+
+
+def write_results(arrays, smalls, positions):
+    n = len(arrays)
+    own = smalls.shape[0]
+    hbm, vm = pl.BlockSpec(memory_space=pl.ANY), pl.BlockSpec(memory_space=VM)
+    like = [jax.ShapeDtypeStruct(v.shape, v.dtype) for v in arrays]
+    shapes = [(positions, own), (2, 2, own), (2, 2, own)]
+    return pl.pallas_call(
+        partial(write_kernel, n),
+        out_shape=like + [jax.ShapeDtypeStruct(v, f32) for v in shapes],
+        in_specs=[vm] * (n + 1),
+        out_specs=[hbm] * n + [vm] * 3,
+        scratch_shapes=[pltpu.SemaphoreType.DMA((n,))],
+    )(*arrays, smalls)
+
+
 def fast_body(tokens, doc_ids, pos_embed, w_qkv, w_out, w_in, w_back, norm_gain, norm_bias, cotangent):
     nrows, local_len, width = tokens.shape
     rows = nrows * local_len
-    segs = rows // SEG_LEN
-    hidden = w_in.shape[2]
-    items = jnp.concatenate([norm_gain[0], norm_bias[0], norm_gain[1], norm_bias[1], pos_embed], axis=0)
-    small = jnp.pad(items.T, ((0, 0), (0, 256 - items.shape[0])))
     x = tokens.reshape(rows, width)
     cot = cotangent.reshape(rows, width)
-    own_row = lax.dynamic_index_in_dim(doc_ids, lax.axis_index("fsdp") % 2, 0, keepdims=False)
-    mask = (own_row[:, None] == own_row[None, :]).astype(f32)
     output, grad_tokens, g_qkv, g_out, g_in, g_back, t_small = layer(
-        small, w_qkv, w_out, w_in, jnp.swapaxes(w_back, 1, 2), x, cot, mask
-    )
-    s = t_small.T
+        w_qkv, w_out, w_in, jnp.swapaxes(w_back, 1, 2), norm_gain, norm_bias, pos_embed, doc_ids, x, cot
+    )
+    output, grad_tokens, g_qkv, g_out, g_in, g_back, grad_pos, grad_gain, grad_bias = write_results(
+        (output, grad_tokens, g_qkv, g_out, g_in, g_back), t_small, doc_ids.shape[1]
+    )
     return (
         output.reshape(tokens.shape),
         grad_tokens.reshape(tokens.shape),
-        s[8 : 8 + doc_ids.shape[1]],
+        grad_pos,
         g_qkv,
         g_out,
         g_in,
         jnp.swapaxes(g_back, 1, 2),
-        jnp.stack([s[0:2], s[4:6]]),
-        jnp.stack([s[2:4], s[6:8]]),
+        grad_gain,
+        grad_bias,
     )
 
 

time: 239 us -> 224 us (0.937)
  local copies, waits for them, and re-layouts: 12.9 us -> 0 us
    unnamed x28 -> x0, local copies, waits for them, and re-layouts: 10.6 us -> none
    pallas_call x1, Pallas kernels: 224 us -> 219 us  [layer(): pl.pallas_call(layer_kernel, out_shape=[arr((rows, width), bf16), arr((ro...]
    pallas_call x0 -> x1, Pallas kernels: none -> 4.28 us  [write_results(): pl.pallas_call(partial(write_kernel, n), out_shape=like + [jax.ShapeDtype...]
where the time goes in v5:
time: 224 us
  Pallas kernels  223 us (100%)
    pallas_call x1, Pallas kernels, layer(): pl.pallas_call(layer_kernel, out_shape=[arr((rows, width), bf16), arr((ro...  219 us

profile of v5, /device:TPU:1, one launch (start us, length us, event | category | flops | bytes accessed | tf_op | source)
XLA Modules:
  0.0 223.8 jit_solution(15694150456883070988)
XLA Ops:
  0.6 218.7 %shard_map.169 = (bf16[512,768]{1,0:T(8,128)(2,1)}, bf16[512,768]{1,0:T(8,128)(2,1)}, f32[2,24,2304]{2,1,0:T(8,128)}, f32[2,24,768]{2,1,0:T(8,128)}, f32[2,24,30...) custom-call(bf16[2,24,2304]{2,1,0:T(8,128)(2,1)} %refs_0_.1, bf16[2,24,768]{2,1,0:T(8,128)(2,1)} %refs_1_.1, ...), custom_call_target="tpu_custom_call" | custom-call | tf_op jit(solution)/shard_map/pallas_call | solution.py:1130
  219.4 4.3 %shard_map.170 = (bf16[512,768]{1,0:T(8,128)(2,1)}, bf16[512,768]{1,0:T(8,128)(2,1)}, f32[2,24,2304]{2,1,0:T(8,128)}, f32[2,24,768]{2,1,0:T(8,128)}, f32[2,24,30...) custom-call(bf16[512,768]{1,0:T(8,128)(2,1)} %get-tuple-element.25.re, ...), custom_call_target="tpu_custom_call" | custom-call | tf_op jit(solution)/shard_map/pallas_call | solution.py:1507

commit v6 on v5

--- a/solution.py
+++ b/solution.py
@@ -380,7 +380,7 @@
     ]
 
 
-SCATTER_LAGS = {"start": 0, "one": 1, "two": 2, "three": 3, "four": 4, "five": 5}
+SCATTER_LAGS = {"start": 0, "one": 1, "two": 2, "three": 4, "four": 7, "five": 9}
 PAIR_SLOTS = 4
 
 
@@ -402,13 +402,13 @@
         sw, ow, qw, iw, bw, cw, cwo,
         pk, at, cx, h, nl, g, sl, z1, z2, r1_ref, r2_ref, par_ref,
         own_buf, sib_buf, block, square,
-        lead_out, gbuf, lead, xbuf, ybuf, dpack, home_ref, fac, fac_sib, csmall,
+        lead_out, gbuf, lead, xbuf, ybuf, dpack, home_y, home_dx, dbuf, dland, fac, fac_sib, csmall,
         df, tr, tr2, dws, small, full, tmp, ring, pair_wide, pair_small,
         s_send, s_recv, pair_send, pair_recv, wo_send, wo_recv, local,
-        g_send, g_recv, x_send, x_recv, h_send, h_recv, lead_sem,
+        g_send, g_recv, x_send, x_recv, h_send, h_recv, lead_sem, d_send, d_recv,
         f_send, f_recv, swap_send, swap_recv, rs_send, rs_recv, free,
-    ) = refs[17:81]
-    bufs = refs[81:]
+    ) = refs[17:86]
+    bufs = refs[86:]
     p = Place()
     rows, width = x_ref.shape
     segs = rows // SEG_LEN
@@ -660,9 +660,11 @@
             r2_ref[key, :] = jnp.broadcast_to(inverse, (block_rows, LANES))
 
     def leaders():
+        first = [h[s * SEG_LEN : s * SEG_LEN + 1, :] for s in range(segs)]
+        result = norm_rows(jnp.concatenate(first, axis=0), par_ref[1:2, :], par_ref[3:4, :])[0]
         for s in range(segs):
             pos = par_ref[pl.ds(8 + p.fsdp * 2 + s % 2, 1), :]
-            lead_out[s // 2, s % 2 : s % 2 + 1, :width] = h[s * SEG_LEN : s * SEG_LEN + 1, :] + pos
+            lead_out[s // 2, s % 2 : s % 2 + 1, :width] = result[s : s + 1] + pos
             lead_out[s // 2, s % 2 : s % 2 + 1, width:] = cot_ref[s * SEG_LEN : s * SEG_LEN + 16, :].astype(f32)[:1]
 
     def lead_copy(z, j):
@@ -747,6 +749,9 @@
                         mine.start()
                         mine.wait()
 
+        comm.upto("plane", n_seg)
+        comm.upto("line", n_seg + 2)
+        finish_block()
         need(n_seg)
         wo_middle()
         for d in range(1, 8):
@@ -811,7 +816,7 @@
             context.append(mm(a.astype(bf16), v[i], NN))
         context = jnp.concatenate(context, axis=1).astype(bf16)
         wo_finish()
-        branch = sum_z(0, mm(context, cwo[...], NN), lambda: None)
+        branch = sum_z(0, mm(context, cwo[...], NN), norm_two)
         normed, z_one, r_one = norm_rows(states + branch, gain0, bias0)
         nl = normed.astype(bf16)
         need(n_seg + 1)
@@ -832,7 +837,13 @@
         give_factor(1, du)
         give_factor(2, jnp.concatenate([part(states), part(normed), part(d_two), context], axis=1))
 
+        for i in range(8):
+            ybuf[i] = result[2 * i : 2 * i + 2]
+        home = remote(ybuf.at[2 * p.z + 1 - p.core], home_y.at[p.core], h_send, h_recv, p.sib)
+
         def during_two():
+            home.start()
+            home_y[p.core] = ybuf[2 * p.z + p.core]
             factors[0].line()
             factors[1].own()
             factors[2].own()
@@ -860,22 +871,31 @@
             factors[3].own()
             factors[2].line()
 
-        dx = d_one + sum_z(3, mm(dp, cw[:, qkv_cols], NT), during_three)
+        partial_dx = mm(dp, cw[:, qkv_cols], NT)
         for i in range(8):
-            ybuf[i, :, :width] = result[2 * i : 2 * i + 2]
-            ybuf[i, :, width:] = dx[2 * i : 2 * i + 2]
-        home = remote(
-            ybuf.at[2 * p.z + 1 - p.core], home_ref.at[p.core], h_send, h_recv, p.sib
-        )
-        home.start()
-        home_ref[p.core] = ybuf[2 * p.z + p.core]
-
+            mine = jnp.where(p.z == i // 2, 1.0, 0.0) * d_one[2 * i : 2 * i + 2]
+            dbuf[i] = partial_dx[2 * i : 2 * i + 2] + mine
+        sent = []
+        for d in range(1, 8):
+            i = lax.rem(p.fsdp + d, 8)
+            copy = remote(dbuf.at[i], dland.at[p.fsdp], d_send.at[d], d_recv.at[p.fsdp], (p.dp, i))
+            copy.start()
+            sent.append(copy)
+        during_three()
+        dland[p.fsdp] = dbuf[p.fsdp]
+        for d in range(1, 8):
+            i = lax.rem(p.fsdp + d, 8)
+            remote(dland.at[i], dland.at[i], d_send.at[d], d_recv.at[i], p.sib).wait_recv()
+        for j in range(2):
+            home_dx[j] = (dland[j] + dland[2 + j]) + (dland[4 + j] + dland[6 + j])
+        for copy in sent:
+            copy.wait_send()
         once = jnp.where(p.z == 0, 1.0, 0.0)
         sums_of = [d_normed * z_one, cot_rows * z_two, d_normed, cot_rows]
         csmall[...] = jnp.zeros_like(csmall)
         for i, s in enumerate(sums_of):
             csmall[i : i + 1, :] = once * jnp.sum(s, axis=0, keepdims=True)
-        theirs = home_ref.at[1 - p.core]
+        theirs = home_y.at[1 - p.core]
         remote(theirs, theirs, h_send, h_recv, p.sib).wait_recv()
         home.wait_send()
 
@@ -896,7 +916,7 @@
         for s in range(segs):
             spot = pl.ds(s * SEG_LEN, 16)
             old = y_ref[spot, :].astype(f32)
-            new = jnp.broadcast_to(home_ref[s // 2, s % 2 : s % 2 + 1, :width], old.shape)
+            new = jnp.broadcast_to(home_y[s // 2, s % 2 : s % 2 + 1, :], old.shape)
             top = lax.broadcasted_iota(jnp.int32, old.shape, 0) == 0
             y_ref[spot, :] = jnp.where(top, new, old).astype(bf16)
     per = hidden // width
@@ -954,19 +974,34 @@
             dst[:, cols] = mm(tr[...], src[:, cols], NN).astype(bf16)
 
     def norm_two():
-        @pl.loop(0, rows // block_rows, unroll=2)
+        @pl.loop(0, rows // block_rows)
         def _(i):
             key = rows_at(i * block_rows, block_rows, 16)
             h[key, :] = cot_ref[key, :].astype(f32)
 
         for s in range(segs):
-            h[s * SEG_LEN : s * SEG_LEN + 1, :] = home_ref[s // 2, s % 2 : s % 2 + 1, width:]
+            h[s * SEG_LEN : s * SEG_LEN + 1, :] = jnp.zeros((1, width), f32)
         small[...] = jnp.zeros_like(small)
+        norm_back(z2, r2_ref, 1, df, 1)
+
+    def norm_leaders():
+        pick = lambda take: jnp.concatenate([take(s * SEG_LEN) for s in range(segs)], axis=0)
+        dy = jnp.concatenate([home_dx[s // 2, s % 2 : s % 2 + 1, :] for s in range(segs)], axis=0)
+        z = pick(lambda row: z2[row : row + 16, :].astype(f32)[:1])
+        r = pick(lambda row: jnp.concatenate([r2_ref[row : row + 1, :]] * (width // LANES), axis=1))
+        d = norm_rows_back(dy, z, r, par_ref[1:2, :])
+        for s in range(segs):
+            h[s * SEG_LEN : s * SEG_LEN + 1, :] = d[s : s + 1]
+            spot = pl.ds(s * SEG_LEN, 16)
+            old = df[spot, :].astype(f32)
+            top = lax.broadcasted_iota(jnp.int32, old.shape, 0) == 0
+            df[spot, :] = jnp.where(top, jnp.broadcast_to(d[s : s + 1], old.shape), old).astype(bf16)
+        small[1:2, :] += jnp.sum(dy * z, axis=0, keepdims=True)
+        small[3:4, :] += jnp.sum(dy, axis=0, keepdims=True)
         small[4:8, :] = csmall[0:4, :]
         for s in range(2):
-            row = home_ref[0, s : s + 1, width:] + home_ref[1, s : s + 1, width:]
+            row = home_dx[0, s : s + 1, :] + home_dx[1, s : s + 1, :]
             small[pl.ds(8 + p.fsdp * 2 + s, 1), :] = row
-        norm_back(z2, r2_ref, 1, df, 1)
         turn(tr, df)
 
     def active_back(part):
@@ -1041,7 +1076,6 @@
     wo_start()
     need(4 + 2 * per)
     feed_back(per - 1)
-    finish_block()
     leaders()
     cross()
     comm.finish()
@@ -1049,7 +1083,7 @@
         pair(i).wait_send()
     patch()
     sum_step = lambda: scatter_step(sums, jobs)
-    norm_two()
+    norm_leaders()
     factors[1].plane()
     factors[2].plane()
     factors[0].last()
@@ -1149,8 +1183,9 @@
             VM((32, total), bf16), VM((32, total), bf16), VM((ROWS, 4 * cross_width + width), bf16),
             VM((LANES, LANES), f32),
             VM((2, 2, 2 * width), f32), VM((8, 2, 2 * width), f32), VM((leads, 2 * width), f32),
-            VM((4, 4, leads, width), bf16), VM((8, 2, 2 * width), f32), VM((leads, 3 * width // 4), f32),
-            VM((2, 2, 2 * width), f32), VM((leads, 4 * width), bf16), VM((leads, 4 * width), bf16),
+            VM((4, 4, leads, width), bf16), VM((8, 2, width), f32), VM((leads, 3 * width // 4), f32),
+            VM((2, 2, width), f32), VM((2, 2, width), f32), VM((8, 2, width), f32), VM((8, 2, width), f32),
+            VM((leads, 4 * width), bf16), VM((leads, 4 * width), bf16),
             VM((8, width), f32),
             wide(width), VM((width, rows), bf16), VM((width, rows), bf16), weight(256),
             VM((LANES, width), f32), VM((32 * leads, 4 * width), bf16), VM((width // 4, width), f32),
@@ -1158,7 +1193,7 @@
             VM((small_units, wrows, LANES), bf16),
             DMA((n_units, 11)), DMA((n_units, 11)), DMA((parts,)), DMA((parts,)),
             DMA((5,)), DMA((5,)), DMA,
-            DMA((8,)), DMA((8,)), DMA((4, 3)), DMA((4, 4)), DMA, DMA, DMA,
+            DMA((8,)), DMA((8,)), DMA((4, 3)), DMA((4, 4)), DMA, DMA, DMA, DMA((8,)), DMA((8,)),
             DMA((4, 11)), DMA((4, 11)), DMA((4,)), DMA((4,)),
             DMA((len(widths), 12)), DMA((len(widths), 12)), pltpu.SemaphoreType.REGULAR((PAIR_SLOTS,)),
         ]

time: 224 us -> 212 us (0.946)
  Pallas kernels: 223 us -> 211 us
    pallas_call x1, Pallas kernels: 219 us -> 206 us  [layer(): pl.pallas_call(layer_kernel, out_shape=[arr((rows, width), bf16), arr((ro...]
where the time goes in v6:
time: 212 us; the launch traced here: 211 us
  Pallas kernels  211 us (100%)
    pallas_call x1, Pallas kernels, layer(): pl.pallas_call(layer_kernel, out_shape=[arr((rows, width), bf16), arr((ro...  206 us
    pallas_call x1, Pallas kernels, write_results(): pl.pallas_call(partial(write_kernel, n), out_shape=like + [jax.ShapeDtype...  4.28 us

profile of v6, /device:TPU:1, one launch (start us, length us, event | category | flops | bytes accessed | tf_op | source)
XLA Modules:
  0.0 211.4 jit_solution(16130869489085371805)
XLA Ops:
  0.6 206.2 %shard_map.169 = (bf16[512,768]{1,0:T(8,128)(2,1)}, bf16[512,768]{1,0:T(8,128)(2,1)}, f32[2,24,2304]{2,1,0:T(8,128)}, f32[2,24,768]{2,1,0:T(8,128)}, f32[2,24,30...) custom-call(bf16[2,24,2304]{2,1,0:T(8,128)(2,1)} %refs_0_.1, bf16[2,24,768]{2,1,0:T(8,128)(2,1)} %refs_1_.1, ...), custom_call_target="tpu_custom_call" | custom-call | tf_op jit(solution)/shard_map/pallas_call | solution.py:1164
  206.9 4.3 %shard_map.170 = (bf16[512,768]{1,0:T(8,128)(2,1)}, bf16[512,768]{1,0:T(8,128)(2,1)}, f32[2,24,2304]{2,1,0:T(8,128)}, f32[2,24,768]{2,1,0:T(8,128)}, f32[2,24,30...) custom-call(bf16[512,768]{1,0:T(8,128)(2,1)} %get-tuple-element.25.re, ...), custom_call_target="tpu_custom_call" | custom-call | tf_op jit(solution)/shard_map/pallas_call | solution.py:1542

commit v7 on v6

--- a/solution.py
+++ b/solution.py
@@ -55,10 +55,11 @@
         return (self.ydp, self.fsdp)
 
 
-def greet(devices):
+def greet(devices, meanwhile):
     barrier = pltpu.get_barrier_semaphore()
     for device in devices:
         pl.semaphore_signal(barrier, inc=1, device_id=device, device_id_type=MESH)
+    meanwhile()
     pl.semaphore_wait(barrier, len(devices))
 
 
@@ -396,20 +397,26 @@
 
 
 def layer_kernel(*refs):
-    wq_ref, wo_ref, wi_ref, wb_ref, gain_ref, bias_ref, pos_ref, docs_ref, x_ref, cot_ref = refs[:10]
+    wq_ref, wo_ref, wi_ref, wb_ref, gain_ref, bias_ref, pos_ref, docs_ref, x_hbm, cot_hbm = refs[:10]
     y_ref, gt_ref, gq_ref, go_ref, gi_ref, gb_ref, gs_ref = refs[10:17]
     (
         sw, ow, qw, iw, bw, cw, cwo,
         pk, at, cx, h, nl, g, sl, z1, z2, r1_ref, r2_ref, par_ref,
-        own_buf, sib_buf, block, square,
+        x_ref, cot_ref, in_sem, own_buf, sib_buf, block, square,
         lead_out, gbuf, lead, xbuf, ybuf, dpack, home_y, home_dx, dbuf, dland, fac, fac_sib, csmall,
         df, tr, tr2, dws, small, full, tmp, ring, pair_wide, pair_small,
         s_send, s_recv, pair_send, pair_recv, wo_send, wo_recv, local,
         g_send, g_recv, x_send, x_recv, h_send, h_recv, lead_sem, d_send, d_recv,
         f_send, f_recv, swap_send, swap_recv, rs_send, rs_recv, free,
-    ) = refs[17:86]
-    bufs = refs[86:]
+    ) = refs[17:89]
+    bufs = refs[89:]
     p = Place()
+    inputs = [
+        pltpu.make_async_copy(x_hbm, x_ref, in_sem.at[0]),
+        pltpu.make_async_copy(cot_hbm, cot_ref, in_sem.at[1]),
+    ]
+    for copy in inputs:
+        copy.start()
     rows, width = x_ref.shape
     segs = rows // SEG_LEN
     hidden = iw.shape[1]
@@ -481,11 +488,9 @@
             stage(i)
             pair(i).start()
 
-    stage(0)
-    greet(everyone(p))
-    pair(0).start()
-    for i in range(1, ahead):
-        begin(i)
+    greet(everyone(p), lambda: [stage(i) for i in range(ahead)])
+    for i in range(ahead):
+        pair(i).start()
 
     sems = (s_send, s_recv)
     dests = [(sw, 0)] + [(qw, i * width) for i in range(3)] + [(ow, 0)]
@@ -846,7 +851,6 @@
             home_y[p.core] = ybuf[2 * p.z + p.core]
             factors[0].line()
             factors[1].own()
-            factors[2].own()
 
         d_normed = d_two + sum_z(2, mm(du, cw[:, in_cols], NT), during_two)
         d_one = norm_rows_back(d_normed, z_one, r_one, gain0)
@@ -867,9 +871,8 @@
 
         def during_three():
             factors[0].plane()
+            factors[2].own()
             factors[1].line()
-            factors[3].own()
-            factors[2].line()
 
         partial_dx = mm(dp, cw[:, qkv_cols], NT)
         for i in range(8):
@@ -1061,6 +1064,8 @@
 
     need(0)
     params()
+    for copy in inputs:
+        copy.wait()
     for i in range(3):
         need(1 + i)
         project(i * n_tiles, n_tiles)
@@ -1083,9 +1088,10 @@
         pair(i).wait_send()
     patch()
     sum_step = lambda: scatter_step(sums, jobs)
+    factors[3].own()
     norm_leaders()
+    factors[2].line()
     factors[1].plane()
-    factors[2].plane()
     factors[0].last()
     for i in range(per):
         active_back(i)
@@ -1093,10 +1099,11 @@
         sum_step()
         if i == 0:
             factors[3].line()
+            factors[2].plane()
             factors[1].last()
         if i == 1:
+            factors[3].plane()
             factors[2].last()
-            factors[3].plane()
         if i == 2:
             factors[3].last()
     turn(tr, nl)
@@ -1172,7 +1179,7 @@
             arr((2, own, hidden), f32),
             arr((own, 256), f32),
         ],
-        in_specs=[vm] * 10,
+        in_specs=[vm] * 8 + [pl.BlockSpec(memory_space=pl.ANY)] * 2,
         out_specs=[vm] * 7,
         scratch_shapes=[
             weight(2 * LANES), weight(width), weight(3 * width), weight(hidden), weight(hidden),
@@ -1180,6 +1187,7 @@
             wide(3 * width), VM((att_rows, SEG_LEN), bf16), wide(width), wide(width, f32), wide(width),
             wide(hidden), wide(hidden), wide(width), wide(width),
             wide(LANES, f32), wide(LANES, f32), VM((24, width), f32),
+            wide(width), wide(width), DMA((2,)),
             VM((32, total), bf16), VM((32, total), bf16), VM((ROWS, 4 * cross_width + width), bf16),
             VM((LANES, LANES), f32),
             VM((2, 2, 2 * width), f32), VM((8, 2, 2 * width), f32), VM((leads, 2 * width), f32),
@@ -1520,9 +1528,14 @@
 
 def write_kernel(n, *refs):
     sources, smalls = refs[:n], refs[n]
-    targets, pos_ref, gain_ref, bias_ref, sems = refs[n + 1 : 2 * n + 1], *refs[2 * n + 1 :]
-    copies = [pltpu.make_async_copy(sources[i], targets[i], sems.at[i]) for i in range(n)]
-    for copy in copies:
+    targets, pos_ref, gain_ref, bias_ref = refs[n + 1 : 2 * n + 1], *refs[2 * n + 1 : 2 * n + 4]
+    bufs, sems = refs[2 * n + 4 : 3 * n + 4], refs[3 * n + 4]
+    loads = [pltpu.make_async_copy(sources[i], bufs[i], sems.at[0, i]) for i in range(n)]
+    copies = [pltpu.make_async_copy(bufs[i], targets[i], sems.at[1, i]) for i in range(n)]
+    for load in loads:
+        load.start()
+    for load, copy in zip(loads, copies):
+        load.wait()
         copy.start()
     rows = smalls[:, :LANES].T[:, : smalls.shape[0]]
     pos_ref[...] = rows[8 : 8 + pos_ref.shape[0]]
@@ -1542,9 +1555,9 @@
     return pl.pallas_call(
         partial(write_kernel, n),
         out_shape=like + [jax.ShapeDtypeStruct(v, f32) for v in shapes],
-        in_specs=[vm] * (n + 1),
+        in_specs=[hbm] * n + [vm],
         out_specs=[hbm] * n + [vm] * 3,
-        scratch_shapes=[pltpu.SemaphoreType.DMA((n,))],
+        scratch_shapes=[VM(v.shape, v.dtype) for v in arrays] + [pltpu.SemaphoreType.DMA((2, n))],
     )(*arrays, smalls)
 
 

time: 212 us -> 211 us (level)
  no operation moved by 1% of the time
where the time goes in v7:
time: 211 us; the launch traced here: 210 us
  Pallas kernels  209 us (99%)
    pallas_call x1, Pallas kernels, layer(): pl.pallas_call(layer_kernel, out_shape=[arr((rows, width), bf16), arr((ro...  205 us
    pallas_call x1, Pallas kernels, write_results(): pl.pallas_call(partial(write_kernel, n), out_shape=like + [jax.ShapeDtype...  4.3 us

profile of v7, /device:TPU:1, one launch (start us, length us, event | category | flops | bytes accessed | tf_op | source)
XLA Modules:
  0.0 210.3 jit_solution(12965179690179403111)
XLA Ops:
  0.6 205.2 %shard_map.169 = (bf16[512,768]{1,0:T(8,128)(2,1)}, bf16[512,768]{1,0:T(8,128)(2,1)}, f32[2,24,2304]{2,1,0:T(8,128)}, f32[2,24,768]{2,1,0:T(8,128)}, f32[2,24,30...) custom-call(bf16[2,24,2304]{2,1,0:T(8,128)(2,1)} %refs_0_.1, bf16[2,24,768]{2,1,0:T(8,128)(2,1)} %refs_1_.1, ...), custom_call_target="tpu_custom_call" | custom-call | tf_op jit(solution)/shard_map/pallas_call | solution.py:1171
  205.8 4.3 %shard_map.170 = (bf16[512,768]{1,0:T(8,128)(2,1)}, bf16[512,768]{1,0:T(8,128)(2,1)}, f32[2,24,2304]{2,1,0:T(8,128)}, f32[2,24,768]{2,1,0:T(8,128)}, f32[2,24,30...) custom-call(bf16[512,768]{1,0:T(8,128)(2,1)} %get-tuple-element.25.re, ...), custom_call_target="tpu_custom_call" | custom-call | tf_op jit(solution)/shard_map/pallas_call | solution.py:1555

commit v8 on v7

--- a/solution.py
+++ b/solution.py
@@ -1043,7 +1043,8 @@
             ds_in = jnp.concatenate(lane_halves(cx[key, q_cols]), axis=0)
             da = mm(ds_in, pk[key, v_cols], NT)
             af = a.astype(f32)
-            ds = (af * (da - jnp.sum(af * da, axis=-1, keepdims=True))).astype(bf16)
+            inner = jnp.sum(af * da, axis=-1, keepdims=True) / jnp.sum(af, axis=-1, keepdims=True)
+            ds = (af * (da - inner)).astype(bf16)
             dv = mm(a, ds_in, TN)
             both = jnp.concatenate([ds[:SEG_LEN], ds[SEG_LEN:]], axis=1)
             dq = mm(both, ks, NN) * factor

time: 211 us -> 211 us (level)
  no operation moved by 1% of the time
where the time goes in v8:
time: 211 us; the launch traced here: 210 us
  Pallas kernels  210 us (100%)
    pallas_call x1, Pallas kernels, layer(): pl.pallas_call(layer_kernel, out_shape=[arr((rows, width), bf16), arr((ro...  205 us
    pallas_call x1, Pallas kernels, write_results(): pl.pallas_call(partial(write_kernel, n), out_shape=like + [jax.ShapeDtype...  4.3 us

profile of v8, /device:TPU:1, one launch (start us, length us, event | category | flops | bytes accessed | tf_op | source)
XLA Modules:
  0.0 210.4 jit_solution(12816816286958299119)
XLA Ops:
  0.6 205.2 %shard_map.169 = (bf16[512,768]{1,0:T(8,128)(2,1)}, bf16[512,768]{1,0:T(8,128)(2,1)}, f32[2,24,2304]{2,1,0:T(8,128)}, f32[2,24,768]{2,1,0:T(8,128)}, f32[2,24,30...) custom-call(bf16[2,24,2304]{2,1,0:T(8,128)(2,1)} %refs_0_.1, bf16[2,24,768]{2,1,0:T(8,128)(2,1)} %refs_1_.1, ...), custom_call_target="tpu_custom_call" | custom-call | tf_op jit(solution)/shard_map/pallas_call | solution.py:1172
  205.9 4.3 %shard_map.170 = (bf16[512,768]{1,0:T(8,128)(2,1)}, bf16[512,768]{1,0:T(8,128)(2,1)}, f32[2,24,2304]{2,1,0:T(8,128)}, f32[2,24,768]{2,1,0:T(8,128)}, f32[2,24,30...) custom-call(bf16[512,768]{1,0:T(8,128)(2,1)} %get-tuple-element.25.re, ...), custom_call_target="tpu_custom_call" | custom-call | tf_op jit(solution)/shard_map/pallas_call | solution.py:1556
